TPU v7x, 32 devices: a whole 2x2x4 slice. The times are simulated.
32 devices in a mesh: dp: 2 (over core), wide: 16 (over z, y, x).
Axes of the slice: x: 2, y: 2, z: 4, core: 2. Of those that a mesh axis runs over, the one named last changes fastest.
Arguments:
- layer_in: bfloat16 [256, 4096], P('wide', 'dp'), may hold values from -6 to 6
- route_ids: int32 [256, 8], P('wide'), may hold values from 0 to 15, all different within a row; in each aligned block of 16 rows (0 to 15, 16 to 31, ...) at most 16 rows name the same one
- route_scores: float32 [256, 8], P('wide'), may hold values from 0.05 to 1
- expert_gate: bfloat16 [16, 1536, 4096], P('wide', None, 'dp'), may hold values from -0.09375 to 0.09375
- expert_up: bfloat16 [16, 1536, 4096], P('wide', None, 'dp'), may hold values from -0.09375 to 0.09375
- expert_down: bfloat16 [16, 1536, 4096], P('wide', None, 'dp'), may hold values from -0.15625 to 0.15625
- student_gate: bfloat16 [12288, 4096], P('wide', 'dp'), may hold values from -0.09375 to 0.09375
- student_up: bfloat16 [12288, 4096], P('wide', 'dp'), may hold values from -0.09375 to 0.09375
- student_down: bfloat16 [12288, 4096], P('wide', 'dp'), may hold values from -0.0546875 to 0.0546875
Outputs:
- teacher_out: bfloat16 [256, 4096], P('wide', 'dp')
- grad_gate: bfloat16 [12288, 4096], P('wide', 'dp')
- grad_up: bfloat16 [12288, 4096], P('wide', 'dp')
- grad_down: bfloat16 [12288, 4096], P('wide', 'dp')
Inputs may be any that keep to these rules, and one draw needn't show every extreme that they name: `route_ids`: each row names 8 different experts. Within the 16 rows of one device no expert is named more than 16 times, a bound that some block reaches there.
All inputs are finite; a program needn't handle non-finite values.
Results may differ from a plain program's by a relative error of at most 0.0058.
Values may be sent and summed in bfloat16 or wider, within the bound.
No kernel may reach another device: no remote copies, remote signals or barrier semaphores. Data moves between devices by JAX's collectives and lax.ppermute only.
A program may use at most 128 MiB of HBM per device.

v0:
```python
import math

import jax
import jax.numpy as jnp
from jax import lax
from jax.sharding import PartitionSpec as P


def silu_terms(values):
    sig_value = jax.nn.sigmoid(values)
    return (values * sig_value, sig_value)


def pair_total(first_term, second_term):
    return lax.psum((first_term, second_term), "dp")


def against(left_mat, right_mat):
    return lax.dot_general(
        left_mat, right_mat, (((1,), (1,)), ((), ())), preferred_element_type=jnp.float32
    )


def across(left_mat, right_mat):
    return lax.dot_general(
        left_mat, right_mat, (((0,), (0,)), ((), ())), preferred_element_type=jnp.float32
    )


def precise_against(left_mat, right_mat):
    return lax.dot_general(
        left_mat,
        right_mat,
        (((1,), (1,)), ((), ())),
        precision=lax.Precision.HIGHEST,
        preferred_element_type=jnp.float32,
    )


def precise_across(left_mat, right_mat):
    return lax.dot_general(
        left_mat,
        right_mat,
        (((0,), (0,)), ((), ())),
        precision=lax.Precision.HIGHEST,
        preferred_element_type=jnp.float32,
    )


def shards(
    layer_in,
    route_ids,
    route_scores,
    expert_gate,
    expert_up,
    expert_down,
    student_gate,
    student_up,
    student_down,
):
    owners = lax.axis_size("wide")
    tok_rows, columns = layer_in.shape
    top_k = route_ids.shape[1]
    capacity = min(tok_rows, max(2, 2 * tok_rows * top_k // owners))
    slot_count = owners * capacity
    gate_mat = expert_gate[0]
    up_mat = expert_up[0]
    down_mat = expert_down[0]
    flat_ids = route_ids.reshape(-1)
    chosen = (flat_ids[:, None] == jnp.arange(owners, dtype=jnp.int32)[None, :]).astype(jnp.int32)
    earlier = jnp.cumsum(chosen, axis=0) - chosen
    slot_rank = jnp.sum(earlier * chosen, axis=1)
    slot_of = flat_ids * capacity + slot_rank
    placed = (slot_of[None, :] == jnp.arange(slot_count, dtype=jnp.int32)[:, None]).astype(
        jnp.float32
    )
    placed = placed.reshape(slot_count, tok_rows, top_k)
    picker = jnp.sum(placed, axis=2).astype(jnp.bfloat16)
    outgoing = jnp.dot(picker, layer_in, preferred_element_type=jnp.float32).astype(jnp.bfloat16)
    outgoing = outgoing.reshape(owners, capacity, columns)
    route_weights = route_scores / jnp.sum(route_scores, axis=1, keepdims=True)
    mix_table = jnp.sum(placed * route_weights[None, :, :], axis=2)
    arrived = lax.all_to_all(outgoing, "wide", split_axis=0, concat_axis=0, tiled=True)
    sources, slot_len, col_len = arrived.shape
    flat_rows = arrived.reshape(sources * slot_len, col_len)
    gate_part = against(flat_rows, gate_mat)
    up_part = against(flat_rows, up_mat)
    gate_share = lax.psum_scatter(gate_part, "dp", scatter_dimension=1, tiled=True)
    up_share = lax.psum_scatter(up_part, "dp", scatter_dimension=1, tiled=True)
    swished, _ = silu_terms(gate_share)
    expert_hidden = lax.all_gather(
        (swished * up_share).astype(jnp.bfloat16), "dp", axis=1, tiled=True
    )
    expert_value = jnp.dot(expert_hidden, down_mat, preferred_element_type=jnp.float32).astype(
        jnp.bfloat16
    )
    returned = lax.all_to_all(
        expert_value.reshape(sources, slot_len, col_len),
        "wide",
        split_axis=0,
        concat_axis=0,
        tiled=True,
    )
    returned = returned.reshape(slot_count, columns).astype(jnp.float32)
    mixed_rows = lax.dot_general(
        mix_table,
        returned,
        (((0,), (0,)), ((), ())),
        precision=lax.Precision.HIGHEST,
        preferred_element_type=jnp.float32,
    )
    gathered = lax.all_gather(layer_in, "wide", axis=0, tiled=True)
    gate_pre, up_pre = pair_total(against(gathered, student_gate), against(gathered, student_up))
    swished, sig_value = silu_terms(gate_pre)
    student_hidden = (swished * up_pre).astype(jnp.bfloat16)
    part_rows = student_hidden
    student_out = lax.psum_scatter(
        jnp.dot(part_rows, student_down, preferred_element_type=jnp.float32),
        "wide",
        scatter_dimension=0,
        tiled=True,
    )
    saved_state = (gathered, gate_pre, up_pre, swished, sig_value, student_hidden, student_out)
    teacher_out = mixed_rows.astype(jnp.bfloat16)
    gathered, gate_pre, up_pre, swished, sig_value, student_hidden, student_out = saved_state
    loss_scale = 1.0 / math.sqrt(tok_rows * owners)
    delta_rows = (student_out - mixed_rows) * loss_scale
    delta_all = lax.all_gather(delta_rows, "wide", axis=0, tiled=True)
    grad_down = precise_across(student_hidden.astype(jnp.float32), delta_all).astype(jnp.bfloat16)
    hidden_grad = lax.psum(precise_against(delta_all, student_down.astype(jnp.float32)), "dp")
    gate_grad_pre = (
        hidden_grad * up_pre * sig_value * (1.0 + gate_pre * (1.0 - sig_value))
    ).astype(jnp.bfloat16)
    up_grad_pre = (hidden_grad * swished).astype(jnp.bfloat16)
    grad_gate = across(gate_grad_pre, gathered).astype(jnp.bfloat16)
    grad_up = across(up_grad_pre, gathered).astype(jnp.bfloat16)
    return (teacher_out, grad_gate, grad_up, grad_down)


def solution(mesh):
    in_specs = (
        P("wide", "dp"),
        P("wide", None),
        P("wide", None),
        P("wide", None, "dp"),
        P("wide", None, "dp"),
        P("wide", None, "dp"),
        P("wide", "dp"),
        P("wide", "dp"),
        P("wide", "dp"),
    )
    out_specs = (P("wide", "dp"), P("wide", "dp"), P("wide", "dp"), P("wide", "dp"))
    return jax.shard_map(shards, mesh=mesh, in_specs=in_specs, out_specs=out_specs, check_vma=False)
```

profile of v0, /device:TPU:1, one launch (start us, length us, event | category | flops | bytes accessed | tf_op | source)
XLA Modules:
  0.0 319.6 jit_solution(2431403838243526596)
XLA Ops:
  7.2 0.0 copy-start
  7.2 0.0 all-gather.3.cloned.1.call-start
  7.2 0.7 all-gather.3.cloned.1.call-update
  7.9 1.0 copy.19
  8.9 0.1 eq.29
  9.0 0.1 fusion.12
  9.1 0.2 reduce_window_sum.11
  9.2 0.2 select_reduce_fusion.1
  9.4 0.1 reduce_sum.39
  9.5 0.7 reduce_sum.40
  10.2 0.7 broadcast_divide_fusion
  10.9 0.1 copy.21
  11.0 0.2 convert_reduce_fusion
  11.1 2.3 convolution_convert_fusion.3
  13.4 7.5 %all-to-all-start = ((bf16[16,16,2048]{2,1,0:T(8,128)(2,1)}), bf16[16,16,2048]{2,1,0:T(8,128)(2,1)}, u32[]{:S(2)}, u32[]{:S(2)}) async-start(bf16[16,16,2048]{2,1,0:T(8,128)(2,1)} %bitcast.34), calls=%async_computation | async-start | bytes 2097152 | tf_op jit(solution)/shard_map/all_to_all | solution.py:83
  20.9 0.0 all-reduce.6.cloned.1.call-start
  20.9 54.7 %all-gather.3.cloned.1.call-done = bf16[256,2048]{1,0:T(8,128)(2,1)} async-done(((bf16[16,2048]{1,0:T(8,128)(2,1)}), bf16[256,2048]{1,0:T(8,128)(2,1)}) %all-gather.3.cloned.1.call-update) | async-done | bytes 1048592 | tf_op jit(solution)/shard_map/all_gather | solution.py:112
  75.7 0.0 copy-start.2
  75.7 0.0 copy-start.3
  75.7 4.3 %fusion.16 = f32[256,768]{1,0:T(8,128)} fusion(bf16[256,2048]{1,0:T(8,128)(2,1)} %all-gather.3.cloned.1.call-done, bf16[768,2048]{1,0:T(8,128)(2,1)} %param.15), kind=kOutput, calls=%fused_computation.30 | convolution fusion | flops 805306368 | bytes 4980736 | tf_op jit(solution)/shard_map/dot_general | solution.py:19
  79.9 0.0 copy-done.2
  79.9 0.0 copy-done.3
  79.9 1.9 fusion.17
  81.9 0.0 all-reduce.6.cloned.1.call-update
  81.9 0.0 reduce-scatter.6.cloned.1.call-start
  81.9 0.0 all-to-all-done
  81.9 6.1 %fusion.2 = f32[256,1536]{1,0:T(8,128)} fusion(bf16[256,2048]{1,0:T(8,128)(2,1)} %bitcast.1, bf16[1,1536,2048]{2,1,0:T(8,128)(2,1)} %param.13), kind=kOutput, calls=%fused_computation.2 | convolution fusion | flops 1610612736 | bytes 8912896 | tf_op jit(solution)/shard_map/dot_general | solution.py:19
  88.0 0.0 reduce-scatter.6.cloned.1.call-update
  88.1 0.0 reduce-scatter.4.cloned.1.call-start
  88.1 6.3 %fusion.4 = f32[256,1536]{1,0:T(8,128)} fusion(bf16[256,2048]{1,0:T(8,128)(2,1)} %bitcast.1, bf16[1,1536,2048]{2,1,0:T(8,128)(2,1)} %param.12), kind=kOutput, calls=%fused_computation.4 | convolution fusion | flops 1610612736 | bytes 8912896 | tf_op jit(solution)/shard_map/dot_general | solution.py:19
  94.5 0.0 reduce-scatter.4.cloned.1.call-update
  94.5 0.0 reduce-scatter.8.cloned.1.call-start
  94.5 8.5 %all-reduce.6.cloned.1.call-done = (f32[256,768]{1,0:T(8,128)}, f32[256,768]{1,0:T(8,128)}) async-done(((f32[256,768]{1,0:T(8,128)}, f32[256,768]{1,0:T(8,128)}), (f32[256,768]{1,0:T(8,128)}, f32[256,768]{1,0:T(8,128)})) %all-reduce.6.cloned.1.call-update) | async-done | bytes 1572880 | tf_op jit(solution)/shard_map/psum | solution.py:15
  103.0 1.6 multiply_convert_fusion.2
  104.6 0.0 copy-done
  104.6 2.3 fusion.18
  106.9 0.0 reduce-scatter.8.cloned.1.call-update
  106.9 0.0 all-gather.5.cloned.1.call-start
  107.0 9.2 %reduce-scatter.6.cloned.1.call-done = f32[256,768]{1,0:T(8,128)} async-done(((f32[256,1536]{1,0:T(8,128)}), f32[256,768]{1,0:T(8,128)}) %reduce-scatter.6.cloned.1.call-update) | async-done | bytes 786448 | tf_op jit(solution)/shard_map/reduce_scatter | solution.py:89
  116.2 13.0 %reduce-scatter.4.cloned.1.call-done = f32[256,768]{1,0:T(8,128)} async-done(((f32[256,1536]{1,0:T(8,128)}), f32[256,768]{1,0:T(8,128)}) %reduce-scatter.4.cloned.1.call-update) | async-done | bytes 786448 | tf_op jit(solution)/shard_map/reduce_scatter | solution.py:88
  129.2 1.6 multiply_convert_fusion.3
  130.8 2.4 all_gather.9
  133.1 4.6 %fusion.6 = bf16[256,2048]{1,0:T(8,128)(2,1)S(1)} fusion(bf16[256,1536]{1,0:T(8,128)(2,1)S(1)} %all_gather.9, bf16[1,1536,2048]{2,1,0:T(8,128)(2,1)} %param.14), kind=kOutput, calls=%fused_computation.9 | convolution fusion | flops 1611137024 | bytes 8126464 | tf_op jit(solution)/shard_map/dot_general | solution.py:94
  137.7 38.0 %all_to_all.10 = bf16[16,16,2048]{2,1,0:T(8,128)(2,1)} all-to-all(bf16[16,16,2048]{2,1,0:T(8,128)(2,1)S(1)} %bitcast.36), channel_id=1, replica_groups=mesh['dp'=2,'wide'=16] {'wide'}, dimensions={0} | all-to-all | bytes 2097152 | tf_op jit(solution)/shard_map/all_to_all | solution.py:97
  175.8 32.2 %reduce-scatter.8.cloned.1.call-done = f32[16,2048]{1,0:T(8,128)} async-done(((f32[256,2048]{1,0:T(8,128)}), f32[16,2048]{1,0:T(8,128)}) %reduce-scatter.8.cloned.1.call-update) | async-done | bytes 131088 | tf_op jit(solution)/shard_map/reduce_scatter | solution.py:117
  208.0 2.4 subtract_multiply_fusion
  210.4 0.0 all-gather.5.cloned.1.call-update
  210.5 0.2 all-reduce.4.cloned.1.call-start
  210.7 70.1 %all-gather.5.cloned.1.call-done = f32[256,2048]{1,0:T(8,128)} async-done(((f32[16,2048]{1,0:T(8,128)}), f32[256,2048]{1,0:T(8,128)}) %all-gather.5.cloned.1.call-update) | async-done | bytes 2097168 | tf_op jit(solution)/shard_map/all_gather | solution.py:128
  280.8 5.3 %fusion.19 = f32[256,768]{1,0:T(8,128)} fusion(f32[256,2048]{1,0:T(8,128)} %all-gather.5.cloned.1.call-done, bf16[768,2048]{1,0:T(8,128)(2,1)S(1)} %copy-done), kind=kOutput, calls=%fused_computation.33 | convolution fusion | flops 4831838208 | bytes 6029312 | tf_op jit(solution)/shard_map/dot_general | solution.py:31
  286.1 0.0 all-reduce.4.cloned.1.call-update
  286.1 5.8 %convolution_convert_fusion = bf16[768,2048]{1,0:T(8,128)(2,1)} fusion(bf16[256,768]{1,0:T(8,128)(2,1)S(1)} %multiply_convert_fusion.2, f32[256,2048]{1,0:T(8,128)} %all-gather.5.cloned.1.call-done), kind=kOutput, calls=%fused_computation.6 | convolution fusion | flops 4833411072 | bytes 5636096 | tf_op jit(solution)/shard_map/dot_general | solution.py:41
  291.9 13.0 %all-reduce.4.cloned.1.call-done = f32[256,768]{1,0:T(8,128)} async-done(((f32[256,768]{1,0:T(8,128)}), f32[256,768]{1,0:T(8,128)}) %all-reduce.4.cloned.1.call-update) | async-done | bytes 786448 | tf_op jit(solution)/shard_map/psum | solution.py:130
  305.0 0.0 copy-start.1
  305.0 0.0 copy-start.4
  305.0 0.0 copy-start.5
  305.0 5.0 %convolution_convert_fusion.2 = bf16[768,2048]{1,0:T(8,128)(2,1)} fusion(bf16[256,2048]{1,0:T(8,128)(2,1)} %all-gather.3.cloned.1.call-done, f32[256,768]{1,0:T(8,128)} %get-tuple-element.6, f32[256,768]{1,0:T(8,128)} %all-reduce.4.cloned.1.call-done, f32[256,768]{1,0:T(8,128)} %get-tuple-element.7), kind=kOutput, calls=%fused_computation.8 | convolution fusion | flops 808845312 | bytes 6553600 | tf_op jit(solution)/shard_map/dot_general | solution.py:25
  310.0 0.0 copy-done.1
  310.0 0.0 copy-done.4
  310.0 0.0 copy-done.5
  310.0 2.7 convolution_convert_fusion.1
  (1 shorter events, 0.0 us)
Async XLA Ops:
  7.2 97.4 %copy-start = (bf16[768,2048]{1,0:T(8,128)(2,1)S(1)}, bf16[768,2048]{1,0:T(8,128)(2,1)}, u32[]{:S(2)}) copy-start(bf16[768,2048]{1,0:T(8,128)(2,1)} %param.17) | copy-start | bytes 9437188
  7.2 68.5 %all-gather.3.cloned.1.call-start = ((), (), s32[]{:S(2)}) async-start(), calls=%async_computation.7 | async-start | bytes 1114112 | tf_op jit(solution)/shard_map/all_gather | solution.py:112
  13.4 68.5 %all-to-all-start = ((bf16[16,16,2048]{2,1,0:T(8,128)(2,1)}), bf16[16,16,2048]{2,1,0:T(8,128)(2,1)}, u32[]{:S(2)}, u32[]{:S(2)}) async-start(bf16[16,16,2048]{2,1,0:T(8,128)(2,1)} %bitcast.34), calls=%async_computation | async-start | bytes 2097152 | tf_op jit(solution)/shard_map/all_to_all | solution.py:83
  20.9 82.1 %all-reduce.6.cloned.1.call-start = ((), (), s32[]{:S(2)}) async-start(), calls=%async_computation.11 | async-start | bytes 3145728 | tf_op jit(solution)/shard_map/psum | solution.py:15
  75.7 4.3 %copy-start.2 = (bf16[768,2048]{1,0:T(8,128)(2,1)S(1)}, bf16[768,2048]{1,0:T(8,128)(2,1)}, u32[]{:S(2)}) copy-start(bf16[768,2048]{1,0:T(8,128)(2,1)} %param.16) | copy-start | bytes 9437188
  75.7 4.3 %copy-start.3 = (bf16[256,2048]{1,0:T(8,128)(2,1)S(1)}, bf16[256,2048]{1,0:T(8,128)(2,1)}, u32[]{:S(2)}) copy-start(bf16[256,2048]{1,0:T(8,128)(2,1)} %all-gather.3.cloned.1.call-done) | copy-start | bytes 3145732
  81.9 34.3 %reduce-scatter.6.cloned.1.call-start = ((), (), s32[]{:S(2)}) async-start(), calls=%async_computation.6 | async-start | bytes 2359296 | tf_op jit(solution)/shard_map/reduce_scatter | solution.py:89
  88.1 41.1 %reduce-scatter.4.cloned.1.call-start = ((), (), s32[]{:S(2)}) async-start(), calls=%async_computation.5 | async-start | bytes 2359296 | tf_op jit(solution)/shard_map/reduce_scatter | solution.py:88
  94.5 113.5 %reduce-scatter.8.cloned.1.call-start = ((), (), s32[]{:S(2)}) async-start(), calls=%async_computation.8 | async-start | bytes 2228224 | tf_op jit(solution)/shard_map/reduce_scatter | solution.py:117
  106.9 173.9 %all-gather.5.cloned.1.call-start = ((), (), s32[]{:S(2)}) async-start(), calls=%async_computation.9 | async-start | bytes 2228224 | tf_op jit(solution)/shard_map/all_gather | solution.py:128
  210.5 94.5 %all-reduce.4.cloned.1.call-start = ((), (), s32[]{:S(2)}) async-start(), calls=%async_computation.10 | async-start | bytes 1572864 | tf_op jit(solution)/shard_map/psum | solution.py:130
  305.0 5.0 %copy-start.1 = (f32[256,768]{1,0:T(8,128)S(1)}, f32[256,768]{1,0:T(8,128)}, u32[]{:S(2)}) copy-start(f32[256,768]{1,0:T(8,128)} %get-tuple-element.6) | copy-start | bytes 2359300
  305.0 5.0 %copy-start.4 = (bf16[256,2048]{1,0:T(8,128)(2,1)S(1)}, bf16[256,2048]{1,0:T(8,128)(2,1)}, u32[]{:S(2)}) copy-start(bf16[256,2048]{1,0:T(8,128)(2,1)} %all-gather.3.cloned.1.call-done) | copy-start | bytes 3145732
  305.0 5.0 %copy-start.5 = (f32[256,768]{1,0:T(8,128)S(1)}, f32[256,768]{1,0:T(8,128)}, u32[]{:S(2)}) copy-start(f32[256,768]{1,0:T(8,128)} %all-reduce.4.cloned.1.call-done) | copy-start | bytes 2359300
Sparse Core Ops, SparseCore 0:
  10.8 64.8 all-gather.2
  82.0 20.9 all-reduce.5
  105.9 10.2 reduce-scatter.5
  118.9 10.2 reduce-scatter.3
  132.0 75.9 reduce-scatter.7
  211.6 69.1 all-gather.4
  286.2 18.7 all-reduce.3
where the time goes:
time: 320 us
  waiting for transfers between devices  202 us (63%)
  matrix products  49 us (15%)
  blocking collectives  40.4 us (13%)
  between operations  14.2 us (4%)
  starting transfers between devices  7.93 us (2%)
  other arithmetic  5.2 us (2%)
    all_gather x1, waiting for transfers between devices, shards(): delta_all = lax.all_gather(delta_rows, 'wide', axis=0, tiled=True)  70.1 us
    all_gather x1, waiting for transfers between devices, shards(): gathered = lax.all_gather(layer_in, 'wide', axis=0, tiled=True)  54.7 us
    all_to_all x1, blocking collectives, shards(): lax.all_to_all(expert_value.reshape(sources, slot_len, col_len), 'wide',...  38 us
    reduce_scatter x1, waiting for transfers between devices, shards(): lax.psum_scatter(jnp.dot(part_rows, student_down, preferred_element_type=...  32.2 us
    dot_general x4, matrix products, against(): lax.dot_general(left_mat, right_mat, (((1,), (1,)), ((), ())), preferred_...  18.6 us
    psum x1, waiting for transfers between devices, shards(): lax.psum(precise_against(delta_all, student_down.astype(jnp.float32)), 'dp')  13 us
    reduce_scatter x1, waiting for transfers between devices, shards(): lax.psum_scatter(gate_part, 'dp', scatter_dimension=1, tiled=True)  13 us
    reduce_scatter x1, waiting for transfers between devices, shards(): up_share = lax.psum_scatter(up_part, 'dp', scatter_dimension=1, tiled=True)  9.22 us
  transfers between devices with their start and end apart: 8, of which 7 were waited for; matrix products, arithmetic and copies ran while one was open for 13% of the time, Pallas kernels for 0%

commit v1 on v0

v1 whole, which is shorter than its diff:
```python
import functools
import math

import jax
import jax.numpy as jnp
from jax import lax
from jax.experimental import pallas as pl
from jax.experimental.pallas import tpu as pltpu
from jax.sharding import PartitionSpec as P

BF16 = jnp.bfloat16
F32 = jnp.float32
VMEM_LIMIT = 48 * 1024 * 1024
LANES = 128


def against(left_mat, right_mat):
    return lax.dot_general(left_mat, right_mat, (((1,), (1,)), ((), ())), preferred_element_type=F32)


def across(left_mat, right_mat):
    return lax.dot_general(left_mat, right_mat, (((0,), (0,)), ((), ())), preferred_element_type=F32)


def plain(left_mat, right_mat):
    return lax.dot_general(left_mat, right_mat, (((1,), (0,)), ((), ())), preferred_element_type=F32)


def block_of(size, most=256):
    fits = [b for b in range(LANES, most + 1, LANES) if size % b == 0]
    return fits[-1] if fits else size


def params():
    return pltpu.CompilerParams(vmem_limit_bytes=VMEM_LIMIT, dimension_semantics=("arbitrary",))


def cost(flops, nbytes):
    return pl.CostEstimate(flops=int(flops), bytes_accessed=int(nbytes), transcendentals=0)


class Ring:
    def __init__(self, size):
        inner = max(d for d in range(1, size + 1) if size % d == 0 and d * d <= size)
        self.size, self.inner, self.outer = size, inner, size // inner
        self.binary = size & (size - 1) == 0

    def add(self, index, near, far):
        if self.binary:
            return index ^ (near + self.inner * far)
        low, high = index % self.inner, index // self.inner
        return (low + near) % self.inner + self.inner * ((high + far) % self.outer)

    def fetch(self, value, near, far):
        return lax.ppermute(value, "wide", [(self.add(i, near, far), i) for i in range(self.size)])

    def send(self, value, near, far):
        return lax.ppermute(value, "wide", [(i, self.add(i, near, far)) for i in range(self.size)])

    def gather(self, value):
        column = [value] + [self.fetch(value, 0, k) for k in range(1, self.outer)]
        column = jnp.concatenate(column, axis=0)
        pieces = [column] + [self.fetch(column, k, 0) for k in range(1, self.inner)]
        return jnp.concatenate(pieces, axis=0)

    def reduce(self, pieces):
        arrived = [pieces[0]] + [self.send(pieces[k], k, 0) for k in range(1, self.inner)]
        column = sum(a.astype(F32) for a in arrived).astype(BF16)
        column = column.reshape(self.outer, column.shape[0] // self.outer, column.shape[1])
        arrived = [column[0]] + [self.send(column[k], 0, k) for k in range(1, self.outer)]
        return sum(a.astype(F32) for a in arrived)


def from_pair(value):
    size = lax.axis_size("dp")
    return [lax.ppermute(value, "dp", [(i, (i + s) % size) for i in range(size)]) for s in range(1, size)]


def payload_kernel(owners, layer_ref, ids_ref, scores_ref, out_ref):
    rows, columns = layer_ref.shape
    out_ref[:, :columns] = layer_ref[...]
    scores = scores_ref[...]
    weights = scores / jnp.sum(scores, axis=0, keepdims=True)
    ids = ids_ref[...]
    shape = (out_ref.shape[1] - columns, rows)
    place = lax.broadcasted_iota(jnp.int32, shape, 0)
    expert = jnp.where(place >= owners, place - owners, place)
    table = jnp.zeros(shape, F32)
    for k in range(ids.shape[0]):
        table = table + jnp.where(ids[k : k + 1, :] == expert, weights[k : k + 1, :], 0.0)
    high = table.astype(BF16).astype(F32)
    table = jnp.where(place < owners, high, table - high).astype(BF16)
    square = (rows, rows)
    same = lax.broadcasted_iota(jnp.int32, square, 0) == lax.broadcasted_iota(jnp.int32, square, 1)
    out_ref[:, columns:] = against(jnp.where(same, 1.0, 0.0).astype(BF16), table).astype(BF16)


def make_payload(layer_in, route_ids, route_scores, owners):
    rows, columns = layer_in.shape
    extra = -(-2 * owners // LANES) * LANES
    return pl.pallas_call(
        functools.partial(payload_kernel, owners),
        out_shape=jax.ShapeDtypeStruct((rows, columns + extra), BF16),
        name="payload",
    )(layer_in, route_ids.T, route_scores.T)


def pre_kernel(x_ref, gate_ref, up_ref, out_ref):
    block = gate_ref.shape[0]
    out_ref[:, :block] = against(x_ref[...], gate_ref[...]).astype(out_ref.dtype)
    out_ref[:, block:] = against(x_ref[...], up_ref[...]).astype(out_ref.dtype)


def pre_parts(x, gate, up, dtype, name):
    hidden, columns = gate.shape
    rows, block = x.shape[0], block_of(hidden)
    return pl.pallas_call(
        pre_kernel,
        grid=(hidden // block,),
        in_specs=[
            pl.BlockSpec((rows, columns), lambda i: (0, 0)),
            pl.BlockSpec((block, columns), lambda i: (i, 0)),
            pl.BlockSpec((block, columns), lambda i: (i, 0)),
        ],
        out_specs=pl.BlockSpec((rows, 2 * block), lambda i: (0, i)),
        out_shape=jax.ShapeDtypeStruct((rows, 2 * hidden), dtype),
        compiler_params=params(),
        cost_estimate=cost(4 * rows * hidden * columns, 4 * hidden * columns + 4 * rows * hidden),
        name=name,
    )(x, gate, up)


def added(refs):
    total = refs[0][...].astype(F32)
    for ref in refs[1:]:
        total = total + ref[...].astype(F32)
    half = total.shape[1] // 2
    return total[:, :half], total[:, half:]


def teacher_kernel(parts, inner, owners, *refs):
    me_ref, pre_refs, down_ref, table_ref = refs[0], refs[1 : 1 + parts], refs[1 + parts], refs[2 + parts]
    out_refs, total = refs[3 + parts : 3 + parts + inner], refs[-1]
    step = pl.program_id(0)
    gate, up = added(pre_refs)
    hidden = (gate * jax.nn.sigmoid(gate) * up).astype(BF16)
    term = plain(hidden, down_ref[...])

    @pl.when(step == 0)
    def _():
        total[...] = term

    @pl.when(step > 0)
    def _():
        total[...] += term

    @pl.when(step == pl.num_programs(0) - 1)
    def _():
        me = me_ref[0]
        table = table_ref[...].astype(F32)
        lane = lax.broadcasted_iota(jnp.int32, table.shape, 1)
        mine = (lane == me) | (lane == me + owners)
        weight = jnp.sum(jnp.where(mine, table, 0.0), axis=1, keepdims=True)
        length = out_refs[0].shape[0]
        for k, out_ref in enumerate(out_refs):
            piece = slice(k * length, (k + 1) * length)
            out_ref[...] = (total[piece, :] * weight[piece, :]).astype(BF16)


def teacher_parts(me, pres, down, payload, inner, owners):
    hidden, columns = down.shape
    rows, block = payload.shape[0], block_of(hidden)
    extra = payload.shape[1] - columns
    return pl.pallas_call(
        functools.partial(teacher_kernel, len(pres), inner, owners),
        grid=(hidden // block,),
        in_specs=[pl.BlockSpec(memory_space=pltpu.SMEM)]
        + [pl.BlockSpec((rows, 2 * block), lambda i: (0, i)) for _ in pres]
        + [
            pl.BlockSpec((block, columns), lambda i: (i, 0)),
            pl.BlockSpec((rows, extra), lambda i: (0, columns // extra)),
        ],
        out_specs=[pl.BlockSpec((rows // inner, columns), lambda i: (0, 0)) for _ in range(inner)],
        out_shape=[jax.ShapeDtypeStruct((rows // inner, columns), BF16) for _ in range(inner)],
        scratch_shapes=[pltpu.VMEM((rows, columns), F32)],
        compiler_params=params(),
        cost_estimate=cost(2 * rows * hidden * columns, 2 * hidden * columns + 10 * rows * hidden),
        name="teacher_down",
    )(me, *pres, down, payload)


def student_kernel(parts, inner, *refs):
    pre_refs, down_ref, teacher_refs = refs[:parts], refs[parts], refs[parts + 1 : parts + 1 + inner]
    hidden_ref, out_refs, total = refs[parts + 1 + inner], refs[parts + 2 + inner : -1], refs[-1]
    step = pl.program_id(0)
    gate, up = added(pre_refs)
    hidden = (gate * jax.nn.sigmoid(gate) * up).astype(BF16)
    hidden_ref[...] = hidden
    term = plain(hidden, down_ref[...])

    @pl.when(step == 0)
    def _():
        total[...] = term

    @pl.when(step > 0)
    def _():
        total[...] += term

    @pl.when(step == pl.num_programs(0) - 1)
    def _():
        length = out_refs[0].shape[0]
        for k, out_ref in enumerate(out_refs):
            out_ref[...] = (total[k * length : (k + 1) * length, :] - teacher_refs[k][...].astype(F32)).astype(BF16)


def student_parts(pres, down, teacher):
    hidden, columns = down.shape
    rows, block, inner = pres[0].shape[0], block_of(hidden), len(teacher)
    whole = pl.BlockSpec((rows // inner, columns), lambda i: (0, 0))
    outs = pl.pallas_call(
        functools.partial(student_kernel, len(pres), inner),
        grid=(hidden // block,),
        in_specs=[pl.BlockSpec((rows, 2 * block), lambda i: (0, i)) for _ in pres]
        + [pl.BlockSpec((block, columns), lambda i: (i, 0))]
        + [whole] * inner,
        out_specs=[pl.BlockSpec((rows, block), lambda i: (0, i))] + [whole] * inner,
        out_shape=[jax.ShapeDtypeStruct((rows, hidden), BF16)]
        + [jax.ShapeDtypeStruct((rows // inner, columns), BF16) for _ in range(inner)],
        scratch_shapes=[pltpu.VMEM((rows, columns), F32)],
        compiler_params=params(),
        cost_estimate=cost(2 * rows * hidden * columns, 2 * hidden * columns + 10 * rows * hidden),
        name="student_down",
    )(*pres, down, *teacher)
    return outs[0], outs[1:]


def hidden_grad_kernel(delta_ref, down_ref, out_ref):
    out_ref[...] = against(delta_ref[...], down_ref[...]).astype(BF16)


def hidden_grad_parts(delta, down):
    hidden, columns = down.shape
    rows, block = delta.shape[0], block_of(hidden)
    return pl.pallas_call(
        hidden_grad_kernel,
        grid=(hidden // block,),
        in_specs=[
            pl.BlockSpec((rows, columns), lambda i: (0, 0)),
            pl.BlockSpec((block, columns), lambda i: (i, 0)),
        ],
        out_specs=pl.BlockSpec((rows, block), lambda i: (0, i)),
        out_shape=jax.ShapeDtypeStruct((rows, hidden), BF16),
        compiler_params=params(),
        cost_estimate=cost(2 * rows * hidden * columns, 2 * hidden * columns + 2 * rows * columns),
        name="hidden_grad",
    )(delta, down)


def grad_down_kernel(hidden_ref, delta_ref, out_ref):
    out_ref[...] = across(hidden_ref[...], delta_ref[...]).astype(BF16)


def grad_down_of(hidden_rows, delta):
    rows, hidden = hidden_rows.shape
    columns, block = delta.shape[1], block_of(hidden)
    return pl.pallas_call(
        grad_down_kernel,
        grid=(hidden // block,),
        in_specs=[
            pl.BlockSpec((rows, block), lambda i: (0, i)),
            pl.BlockSpec((rows, columns), lambda i: (0, 0)),
        ],
        out_specs=pl.BlockSpec((block, columns), lambda i: (i, 0)),
        out_shape=jax.ShapeDtypeStruct((hidden, columns), BF16),
        compiler_params=params(),
        cost_estimate=cost(2 * rows * hidden * columns, 2 * hidden * columns + 2 * rows * columns),
        name="grad_down",
    )(hidden_rows, delta)


def grad_pre_kernel(parts, *refs):
    pre_refs, back_refs, x_ref = refs[:parts], refs[parts : 2 * parts], refs[2 * parts]
    gate_ref, up_ref = refs[-2:]
    gate, up = added(pre_refs)
    back = back_refs[0][...].astype(F32)
    for ref in back_refs[1:]:
        back = back + ref[...].astype(F32)
    sig = jax.nn.sigmoid(gate)
    gate_grad = (back * up * sig * (1.0 + gate * (1.0 - sig))).astype(BF16)
    up_grad = (back * gate * sig).astype(BF16)
    gate_ref[...] = across(gate_grad, x_ref[...]).astype(BF16)
    up_ref[...] = across(up_grad, x_ref[...]).astype(BF16)


def grad_pre_of(pres, backs, payload, columns):
    rows, hidden = backs[0].shape
    block = block_of(hidden)
    return pl.pallas_call(
        functools.partial(grad_pre_kernel, len(pres)),
        grid=(hidden // block,),
        in_specs=[pl.BlockSpec((rows, 2 * block), lambda i: (0, i)) for _ in pres]
        + [pl.BlockSpec((rows, block), lambda i: (0, i)) for _ in backs]
        + [pl.BlockSpec((rows, columns), lambda i: (0, 0))],
        out_specs=[pl.BlockSpec((block, columns), lambda i: (i, 0))] * 2,
        out_shape=[jax.ShapeDtypeStruct((hidden, columns), BF16)] * 2,
        compiler_params=params(),
        cost_estimate=cost(4 * rows * hidden * columns, 4 * hidden * columns + 2 * rows * columns),
        name="grad_gate_up",
    )(*pres, *backs, payload)


def shards(
    layer_in,
    route_ids,
    route_scores,
    expert_gate,
    expert_up,
    expert_down,
    student_gate,
    student_up,
    student_down,
):
    owners = lax.axis_size("wide")
    ring = Ring(owners)
    tok_rows, columns = layer_in.shape
    me = lax.axis_index("wide").astype(jnp.int32).reshape(1)

    payload = ring.gather(make_payload(layer_in, route_ids, route_scores, owners))

    expert_pre = pre_parts(payload, expert_gate[0], expert_up[0], BF16, "teacher_pre")
    expert_pres = [expert_pre] + from_pair(expert_pre)
    student_pre = pre_parts(payload, student_gate, student_up, F32, "student_pre")
    student_pres = [student_pre] + from_pair(student_pre)
    teacher = teacher_parts(me, expert_pres, expert_down[0], payload, ring.inner, owners)
    student_hidden, difference = student_parts(student_pres, student_down, teacher)

    loss_scale = 1.0 / math.sqrt(tok_rows * owners)
    delta = (ring.reduce(difference) * loss_scale).astype(BF16)
    teacher_out = ring.reduce(teacher).astype(BF16)
    delta_all = ring.gather(delta)

    back = hidden_grad_parts(delta_all, student_down)
    backs = [back] + from_pair(back)
    grad_down = grad_down_of(student_hidden, delta_all)
    grad_gate, grad_up = grad_pre_of(student_pres, backs, payload, columns)
    return (teacher_out, grad_gate, grad_up, grad_down)


def solution(mesh):
    in_specs = (
        P("wide", "dp"),
        P("wide", None),
        P("wide", None),
        P("wide", None, "dp"),
        P("wide", None, "dp"),
        P("wide", None, "dp"),
        P("wide", "dp"),
        P("wide", "dp"),
        P("wide", "dp"),
    )
    out_specs = (P("wide", "dp"), P("wide", "dp"), P("wide", "dp"), P("wide", "dp"))
    return jax.shard_map(shards, mesh=mesh, in_specs=in_specs, out_specs=out_specs, check_vma=False)
```

time: 320 us -> 118 us (0.37)
  waiting for transfers between devices: 202 us -> 49.4 us
  matrix products: 49 us -> 0 us
  blocking collectives: 40.4 us -> 0 us
  Pallas kernels: 0 us -> 36 us
  starting transfers between devices: 7.93 us -> 28.4 us
  between operations: 14.2 us -> 0.85 us
  other arithmetic: 5.2 us -> 1.9 us
    all_gather x2 -> x0, waiting for transfers between devices: 125 us -> none  [the longest x1 70.1 us: shards(): delta_all = lax.all_gather(delta_rows, 'wide', axis=0, tiled=True)]
    reduce_scatter x3 -> x0, waiting for transfers between devices: 54.4 us -> none  [the longest x1 32.2 us: shards(): lax.psum_scatter(jnp.dot(part_rows, student_down, preferred_element_type=...]
    ppermute x0 -> x27, waiting for transfers between devices: none -> 49.4 us  [the longest x12 30.8 us: fetch(): lax.ppermute(value, 'wide', [(self.add(i, near, far), i) for i in range(s...]
    dot_general x12 -> x0, matrix products: 49 us -> none  [the longest x4 18.6 us: against(): lax.dot_general(left_mat, right_mat, (((1,), (1,)), ((), ())), preferred_...]
    all_to_all x1 -> x0, blocking collectives: 38 us -> none  [shards(): lax.all_to_all(expert_value.reshape(sources, slot_len, col_len), 'wide',...]
    pallas_call x0 -> x8, Pallas kernels: none -> 36 us  [the longest x2 13 us: pre_parts(): pl.pallas_call(pre_kernel, grid=(hidden // block,), in_specs=[pl.BlockSpe...]
    ppermute x0 -> x27, starting transfers between devices: none -> 28.4 us  [the longest x12 13 us: fetch(): lax.ppermute(value, 'wide', [(self.add(i, near, far), i) for i in range(s...]
    psum x2 -> x0, waiting for transfers between devices: 21.5 us -> none  [the longest x1 13 us: shards(): lax.psum(precise_against(delta_all, student_down.astype(jnp.float32)), 'dp')]
  transfers between devices with their start and end apart: 8 -> 27, of which waited for: 7 -> 13; matrix products, arithmetic and copies ran while one was open for 13% -> 2% of each run, Pallas kernels for 0% -> 13%
where the time goes in v1:
time: 118 us
  waiting for transfers between devices  49.4 us (42%)
  Pallas kernels  36 us (31%)
  starting transfers between devices  28.4 us (24%)
  other arithmetic  1.9 us (2%)
    ppermute x12, waiting for transfers between devices, fetch(): lax.ppermute(value, 'wide', [(self.add(i, near, far), i) for i in range(s...  30.8 us
    ppermute x12, waiting for transfers between devices, send(): lax.ppermute(value, 'wide', [(i, self.add(i, near, far)) for i in range(s...  18.6 us
    pallas_call x2, Pallas kernels, pre_parts(): pl.pallas_call(pre_kernel, grid=(hidden // block,), in_specs=[pl.BlockSpe...  13 us
    ppermute x12, starting transfers between devices, fetch(): lax.ppermute(value, 'wide', [(self.add(i, near, far), i) for i in range(s...  13 us
    ppermute x12, starting transfers between devices, send(): lax.ppermute(value, 'wide', [(i, self.add(i, near, far)) for i in range(s...  8.95 us
    pallas_call x1, Pallas kernels, teacher_parts(): pl.pallas_call(functools.partial(teacher_kernel, len(pres), inner, owners...  7.3 us
    ppermute x3, starting transfers between devices, from_pair(): lax.ppermute(value, 'dp', [(i, (i + s) % size) for i in range(size)])  6.46 us
    pallas_call x1, Pallas kernels, grad_pre_of(): pl.pallas_call(functools.partial(grad_pre_kernel, len(pres)), grid=(hidde...  5.26 us
  transfers between devices with their start and end apart: 27, of which 13 were waited for; matrix products, arithmetic and copies ran while one was open for 2% of the time, Pallas kernels for 13%

profile of v1, /device:TPU:1, one launch (start us, length us, event | category | flops | bytes accessed | tf_op | source)
XLA Modules:
  0.0 117.7 jit_solution(17133039423995964049)
XLA Ops:
  0.6 1.7 %payload.1 = bf16[16,2176]{1,0:T(8,128)(2,1)} custom-call(bf16[16,2048]{1,0:T(8,128)(2,1)} %layer_ref.1, s32[8,16]{1,0:T(8,128)} %bitcast.9, f32[8,16]{1,0:T(8,128)} %bitcast.10), custom_call_target="tpu_custom_call" | custom-call | tf_op jit(solution)/shard_map/payload/pallas_call | solution.py:101
  2.3 4.2 %collective-permute-start.2 = (bf16[16,2176]{1,0:T(8,128)(2,1)}, bf16[16,2176]{1,0:T(8,128)(2,1)S(1)}, u32[]{:S(2)}, u32[]{:S(2)}) collective-permute-start(bf16[16,2176]{1,0:T(8,128)(2,1)} %payload.1), channel_id=1, source_target_pairs={{12,0},{13,1},{14,2},{15,3},{8,4},{9,5},{10,6},{11,7},{4,8},{5,9},... | collective-permute-start | bytes 208904 | tf_op jit(solution)/shard_map/ppermute | solution.py:55
  6.5 0.0 collective-permute-start.1
  6.5 0.3 collective-permute-start
  6.8 0.9 constant_dynamic-update-slice_fusion.6
  7.7 0.7 collective-permute-done.2
  8.4 4.1 %collective-permute-done.1 = bf16[16,2176]{1,0:T(8,128)(2,1)S(1)} collective-permute-done((bf16[16,2176]{1,0:T(8,128)(2,1)}, bf16[16,2176]{1,0:T(8,128)(2,1)S(1)}, u32[]{:S(2)}, u32[]{:S(2)}) %collective-permute-start.1) | collective-permute-done | bytes 69664 | tf_op jit(solution)/shard_map/ppermute | solution.py:55
  12.5 0.0 collective-permute-done
  12.6 0.9 pad_maximum_fusion
  13.5 2.5 %collective-permute-start.5 = (bf16[64,2176]{1,0:T(8,128)(2,1)S(1)}, bf16[64,2176]{1,0:T(8,128)(2,1)S(1)}, u32[]{:S(2)}, u32[]{:S(2)}) collective-permute-start(bf16[64,2176]{1,0:T(8,128)(2,1)S(1)} %pad_maximum_fusion), channel_id=1, source_target_pairs={{3,0},{2,1},{1,2},{0,3},{7,4},{6,5},{5,6},{4,7},{11,8},{10,9},{9,1... | collective-permute-start | bytes 835592 | tf_op jit(solution)/shard_map/ppermute | solution.py:55
  16.0 0.2 collective-permute-start.4
  16.2 0.1 collective-permute-start.3
  16.4 11.9 %collective-permute-done.3 = bf16[64,2176]{1,0:T(8,128)(2,1)S(1)} collective-permute-done((bf16[64,2176]{1,0:T(8,128)(2,1)S(1)}, bf16[64,2176]{1,0:T(8,128)(2,1)S(1)}, u32[]{:S(2)}, u32[]{:S(2)}) %collective-permute-start.3) | collective-permute-done | bytes 278560 | tf_op jit(solution)/shard_map/ppermute | solution.py:55
  28.3 0.8 collective-permute-done.4
  29.1 0.0 collective-permute-done.5
  29.1 0.0 copy-start.1
  29.1 9.0 %teacher_pre.1.refs_1_ = bf16[256,3072]{1,0:T(8,128)(2,1)} custom-call(bf16[256,2176]{1,0:T(8,128)(2,1)S(1)} %constant_dynamic-update-slice_fusion.x_ref.refs_4_, bf16[1536,2048]{1,0:T(8,128)(2,1)} %bitcast.6, bf16[1536,2048]{1,0:T(8,128)(2,1)} %bitcast.7), custom_call_target="tpu_custom_call" | custom-call | flops 3221225472 | bytes 14155776 | tf_op jit(solution)/shard_map/teacher_pre/pallas_call | solution.py:117
  38.2 0.8 collective-permute-start.6
  39.0 4.0 %student_pre.1.refs_0_ = f32[256,1536]{1,0:T(8,128)S(1)} custom-call(bf16[256,2176]{1,0:T(8,128)(2,1)S(1)} %constant_dynamic-update-slice_fusion.x_ref.refs_4_, bf16[768,2048]{1,0:T(8,128)(2,1)S(1)} %copy-done.1, bf16[768,2048]{1,0:T(8,128)(2,1)} %up_ref.1), custom_call_target="tpu_custom_call" | custom-call | flops 1610612736 | bytes 7077888 | tf_op jit(solution)/shard_map/student_pre/pallas_call | solution.py:117
  43.0 0.1 collective-permute-start.13
  43.1 0.0 collective-permute-done.6.refs_2_
  43.1 7.3 %teacher_down.1 = (bf16[64,2048]{1,0:T(8,128)(2,1)S(1)}, bf16[64,2048]{1,0:T(8,128)(2,1)S(1)}, bf16[64,2048]{1,0:T(8,128)(2,1)S(1)}, bf16[64,2048]{1,0:T(8,128)(2,1)S(1)}) custom-call(s32[1]{0:T(128)} %bitcast.refs_0_, bf16[256,3072]{1,0:T(8,128)(2,1)} %teacher_pre.1.refs_1_, bf16[256,3072]{1,0:T(8,128)(2,1)} %collective-permute-done.6.refs_2_, ...), custom_call_target="tpu_custom_call" | custom-call | flops 1610612736 | bytes 10223616 | tf_op jit(solution)/shard_map/teacher_down/pallas_call | solution.py:174
  50.4 0.0 collective-permute-done.13.refs_1_
  50.5 4.3 %student_down.1 = (bf16[256,768]{1,0:T(8,128)(2,1)S(1)}, bf16[64,2048]{1,0:T(8,128)(2,1)S(1)}, bf16[64,2048]{1,0:T(8,128)(2,1)S(1)}, bf16[64,2048]{1,0:T(8,128)(2,1)S(1)}, bf16[64,2048]{1,0:T(8,128)(2,1)S(1)}) custom-call(f32[256,1536]{1,0:T(8,128)S(1)} %student_pre.1.refs_0_, f32[256,1536]{1,0:T(8,128)} %collective-permute-done.13.refs_1_, ...), custom_call_target="tpu_custom_call" | custom-call | flops 805306368 | bytes 5111808 | tf_op jit(solution)/shard_map/student_down/pallas_call | solution.py:220
  54.8 1.3 %collective-permute-start.14 = (bf16[64,2048]{1,0:T(8,128)(2,1)S(1)}, bf16[64,2048]{1,0:T(8,128)(2,1)S(1)}, u32[]{:S(2)}, u32[]{:S(2)}) collective-permute-start(bf16[64,2048]{1,0:T(8,128)(2,1)S(1)} %get-tuple-element.20), channel_id=1, source_target_pairs={{0,1},{1,0},{2,3},{3,2},{4,5},{5,4},{6,7},{7,6},{8,9},{9,8},{10,11... | collective-permute-start | bytes 786440 | tf_op jit(solution)/shard_map/ppermute | solution.py:58
  56.1 0.3 collective-permute-start.15
  56.3 1.2 collective-permute-start.16
  57.5 1.2 %collective-permute-start.7 = (bf16[64,2048]{1,0:T(8,128)(2,1)S(1)}, bf16[64,2048]{1,0:T(8,128)(2,1)S(1)}, u32[]{:S(2)}, u32[]{:S(2)}) collective-permute-start(bf16[64,2048]{1,0:T(8,128)(2,1)S(1)} %get-tuple-element.16.refs_4_), channel_id=1, source_target_pairs={{0,1},{1,0},{2,3},{3,2},{4,5},{5,4},{6,7},{7,6},{8,9},{9,8},{10,11... | collective-permute-start | bytes 786440 | tf_op jit(solution)/shard_map/ppermute | solution.py:58
  58.7 0.3 collective-permute-start.8
  59.0 3.3 %collective-permute-done.14 = bf16[64,2048]{1,0:T(8,128)(2,1)S(1)} collective-permute-done((bf16[64,2048]{1,0:T(8,128)(2,1)S(1)}, bf16[64,2048]{1,0:T(8,128)(2,1)S(1)}, u32[]{:S(2)}, u32[]{:S(2)}) %collective-permute-start.14) | collective-permute-done | bytes 262176 | tf_op jit(solution)/shard_map/ppermute | solution.py:58
  62.3 1.2 %collective-permute-start.9 = (bf16[64,2048]{1,0:T(8,128)(2,1)S(1)}, bf16[64,2048]{1,0:T(8,128)(2,1)S(1)}, u32[]{:S(2)}, u32[]{:S(2)}) collective-permute-start(bf16[64,2048]{1,0:T(8,128)(2,1)S(1)} %get-tuple-element.18.refs_6_), channel_id=1, source_target_pairs={{0,3},{1,2},{2,1},{3,0},{4,7},{5,6},{6,5},{7,4},{8,11},{9,10},{10,... | collective-permute-start | bytes 786440 | tf_op jit(solution)/shard_map/ppermute | solution.py:58
  63.5 0.0 collective-permute-done.15
  63.5 5.3 %collective-permute-done.16 = bf16[64,2048]{1,0:T(8,128)(2,1)S(1)} collective-permute-done((bf16[64,2048]{1,0:T(8,128)(2,1)S(1)}, bf16[64,2048]{1,0:T(8,128)(2,1)S(1)}, u32[]{:S(2)}, u32[]{:S(2)}) %collective-permute-start.16) | collective-permute-done | bytes 262176 | tf_op jit(solution)/shard_map/ppermute | solution.py:58
  68.7 0.1 add_convert_fusion
  68.9 0.1 collective-permute-start.17
  69.0 1.0 collective-permute-start.19
  70.0 3.5 %collective-permute-done.7 = bf16[64,2048]{1,0:T(8,128)(2,1)S(1)} collective-permute-done((bf16[64,2048]{1,0:T(8,128)(2,1)S(1)}, bf16[64,2048]{1,0:T(8,128)(2,1)S(1)}, u32[]{:S(2)}, u32[]{:S(2)}) %collective-permute-start.7) | collective-permute-done | bytes 262176 | tf_op jit(solution)/shard_map/ppermute | solution.py:58
  73.6 0.0 collective-permute-start.18
  73.6 0.9 collective-permute-done.8
  74.4 5.6 %collective-permute-done.9 = bf16[64,2048]{1,0:T(8,128)(2,1)S(1)} collective-permute-done((bf16[64,2048]{1,0:T(8,128)(2,1)S(1)}, bf16[64,2048]{1,0:T(8,128)(2,1)S(1)}, u32[]{:S(2)}, u32[]{:S(2)}) %collective-permute-start.9) | collective-permute-done | bytes 262176 | tf_op jit(solution)/shard_map/ppermute | solution.py:58
  80.0 0.1 add_convert_fusion.1
  80.2 0.0 collective-permute-done.17
  80.2 0.0 collective-permute-done.19
  80.2 0.0 collective-permute-done.18
  80.2 1.0 collective-permute-start.22
  81.3 0.0 collective-permute-start.21
  81.3 2.6 %collective-permute-start.20 = (bf16[16,2048]{1,0:T(8,128)(2,1)S(1)}, bf16[16,2048]{1,0:T(8,128)(2,1)S(1)}, u32[]{:S(2)}, u32[]{:S(2)}) collective-permute-start(bf16[16,2048]{1,0:T(8,128)(2,1)S(1)} %get-tuple-element.27), channel_id=1, source_target_pairs={{4,0},{5,1},{6,2},{7,3},{0,4},{1,5},{2,6},{3,7},{12,8},{13,9},{14,... | collective-permute-start | bytes 196616 | tf_op jit(solution)/shard_map/ppermute | solution.py:55
  83.9 0.1 collective-permute-start.10
  84.0 1.2 collective-permute-start.12
  85.1 0.3 collective-permute-done.22
  85.4 1.2 %collective-permute-start.11 = (bf16[16,2048]{1,0:T(8,128)(2,1)S(1)}, bf16[16,2048]{1,0:T(8,128)(2,1)S(1)}, u32[]{:S(2)}, u32[]{:S(2)}) collective-permute-start(bf16[16,2048]{1,0:T(8,128)(2,1)S(1)} %get-tuple-element.33), channel_id=1, source_target_pairs={{0,8},{1,9},{2,10},{3,11},{4,12},{5,13},{6,14},{7,15},{8,0},{9,1},... | collective-permute-start | bytes 196616 | tf_op jit(solution)/shard_map/ppermute | solution.py:58
  86.6 1.2 %collective-permute-done.21 = bf16[16,2048]{1,0:T(8,128)(2,1)S(1)} collective-permute-done((bf16[16,2048]{1,0:T(8,128)(2,1)S(1)}, bf16[16,2048]{1,0:T(8,128)(2,1)S(1)}, u32[]{:S(2)}, u32[]{:S(2)}) %collective-permute-start.21) | collective-permute-done | bytes 65568 | tf_op jit(solution)/shard_map/ppermute | solution.py:55
  87.8 0.0 collective-permute-done.20
  87.9 0.6 collective-permute-start.24
  88.4 0.8 collective-permute-start.23
  89.3 4.4 %collective-permute-done.23 = bf16[64,2048]{1,0:T(8,128)(2,1)S(1)} collective-permute-done((bf16[64,2048]{1,0:T(8,128)(2,1)S(1)}, bf16[64,2048]{1,0:T(8,128)(2,1)S(1)}, u32[]{:S(2)}, u32[]{:S(2)}) %collective-permute-start.23) | collective-permute-done | bytes 262176 | tf_op jit(solution)/shard_map/ppermute | solution.py:55
  93.6 0.7 collective-permute-start.25
  94.4 7.4 %collective-permute-done.25 = bf16[64,2048]{1,0:T(8,128)(2,1)S(1)} collective-permute-done((bf16[64,2048]{1,0:T(8,128)(2,1)S(1)}, bf16[64,2048]{1,0:T(8,128)(2,1)S(1)}, u32[]{:S(2)}, u32[]{:S(2)}) %collective-permute-start.25) | collective-permute-done | bytes 262176 | tf_op jit(solution)/shard_map/ppermute | solution.py:55
  101.9 1.5 %hidden_grad.1.refs_2_ = bf16[256,768]{1,0:T(8,128)(2,1)S(1)} custom-call(bf16[256,2048]{1,0:T(8,128)(2,1)S(1)} %constant_dynamic-update-slice_fusion.7.delta_ref, bf16[768,2048]{1,0:T(8,128)(2,1)S(1)} %copy-done), custom_call_target="tpu_custom_call" | custom-call | flops 805306368 | bytes 4194304 | tf_op jit(solution)/shard_map/hidden_grad/pallas_call | solution.py:244
  103.4 5.5 %collective-permute-start.26 = (bf16[256,768]{1,0:T(8,128)(2,1)S(1)}, bf16[256,768]{1,0:T(8,128)(2,1)S(1)}, u32[]{:S(2)}, u32[]{:S(2)}) collective-permute-start(bf16[256,768]{1,0:T(8,128)(2,1)S(1)} %hidden_grad.1.refs_2_), channel_id=1, source_target_pairs={{0,16},{16,0},{1,17},{17,1},{2,18},{18,2},{3,19},{19,3},{4,20},{20... | collective-permute-start | bytes 1179656 | tf_op jit(solution)/shard_map/ppermute | solution.py:76
  108.9 0.0 collective-permute-done.10
  108.9 0.7 add_convert_fusion.2
  109.6 2.9 %grad_down.1 = bf16[768,2048]{1,0:T(8,128)(2,1)} custom-call(bf16[256,768]{1,0:T(8,128)(2,1)S(1)} %get-tuple-element.25.hidden_ref, bf16[256,2048]{1,0:T(8,128)(2,1)S(1)} %constant_dynamic-update-slice_fusion.7.delta_ref), custom_call_target="tpu_custom_call" | custom-call | flops 805306368 | bytes 4194304 | tf_op jit(solution)/shard_map/grad_down/pallas_call | solution.py:266
  112.5 5.3 %grad_gate_up.1 = (bf16[768,2048]{1,0:T(8,128)(2,1)}, bf16[768,2048]{1,0:T(8,128)(2,1)}) custom-call(f32[256,1536]{1,0:T(8,128)S(1)} %student_pre.1.refs_0_, f32[256,1536]{1,0:T(8,128)} %collective-permute-done.13.refs_1_, bf16[256,768]{1,0:T(8,128)(2,1)S(1)} %hidden_grad.1.refs_2_, bf16[256,768]{1,0:T(8,128)(2,1)S(1)} %collective-permute-done.26.refs_3_, ...), custom_call_target="tpu_custom_call" | custom-call | flops 1610612736 | bytes 7340032 | tf_op jit(solution)/shard_map/grad_gate_up/pallas_call | solution.py:298
  (23 shorter events, 0.3 us)
Async XLA Ops:
  2.3 6.1 %collective-permute-start.2 = (bf16[16,2176]{1,0:T(8,128)(2,1)}, bf16[16,2176]{1,0:T(8,128)(2,1)S(1)}, u32[]{:S(2)}, u32[]{:S(2)}) collective-permute-start(bf16[16,2176]{1,0:T(8,128)(2,1)} %payload.1), channel_id=1, source_target_pairs={{12,0},{13,1},{14,2},{15,3},{8,4},{9,5},{10,6},{11,7},{4,8},{5,9},... | collective-permute-start | bytes 208904 | tf_op jit(solution)/shard_map/ppermute | solution.py:55
  6.5 6.1 %collective-permute-start.1 = (bf16[16,2176]{1,0:T(8,128)(2,1)}, bf16[16,2176]{1,0:T(8,128)(2,1)S(1)}, u32[]{:S(2)}, u32[]{:S(2)}) collective-permute-start(bf16[16,2176]{1,0:T(8,128)(2,1)} %payload.1), channel_id=1, source_target_pairs={{8,0},{9,1},{10,2},{11,3},{12,4},{13,5},{14,6},{15,7},{0,8},{1,9},... | collective-permute-start | bytes 208904 | tf_op jit(solution)/shard_map/ppermute | solution.py:55
  6.5 6.1 %collective-permute-start = (bf16[16,2176]{1,0:T(8,128)(2,1)}, bf16[16,2176]{1,0:T(8,128)(2,1)S(1)}, u32[]{:S(2)}, u32[]{:S(2)}) collective-permute-start(bf16[16,2176]{1,0:T(8,128)(2,1)} %payload.1), channel_id=1, source_target_pairs={{4,0},{5,1},{6,2},{7,3},{0,4},{1,5},{2,6},{3,7},{12,8},{13,9},{14,... | collective-permute-start | bytes 208904 | tf_op jit(solution)/shard_map/ppermute | solution.py:55
  13.5 15.6 %collective-permute-start.5 = (bf16[64,2176]{1,0:T(8,128)(2,1)S(1)}, bf16[64,2176]{1,0:T(8,128)(2,1)S(1)}, u32[]{:S(2)}, u32[]{:S(2)}) collective-permute-start(bf16[64,2176]{1,0:T(8,128)(2,1)S(1)} %pad_maximum_fusion), channel_id=1, source_target_pairs={{3,0},{2,1},{1,2},{0,3},{7,4},{6,5},{5,6},{4,7},{11,8},{10,9},{9,1... | collective-permute-start | bytes 835592 | tf_op jit(solution)/shard_map/ppermute | solution.py:55
  16.0 13.1 %collective-permute-start.4 = (bf16[64,2176]{1,0:T(8,128)(2,1)S(1)}, bf16[64,2176]{1,0:T(8,128)(2,1)S(1)}, u32[]{:S(2)}, u32[]{:S(2)}) collective-permute-start(bf16[64,2176]{1,0:T(8,128)(2,1)S(1)} %pad_maximum_fusion), channel_id=1, source_target_pairs={{2,0},{3,1},{0,2},{1,3},{6,4},{7,5},{4,6},{5,7},{10,8},{11,9},{8,1... | collective-permute-start | bytes 835592 | tf_op jit(solution)/shard_map/ppermute | solution.py:55
  16.2 12.1 %collective-permute-start.3 = (bf16[64,2176]{1,0:T(8,128)(2,1)S(1)}, bf16[64,2176]{1,0:T(8,128)(2,1)S(1)}, u32[]{:S(2)}, u32[]{:S(2)}) collective-permute-start(bf16[64,2176]{1,0:T(8,128)(2,1)S(1)} %pad_maximum_fusion), channel_id=1, source_target_pairs={{1,0},{0,1},{3,2},{2,3},{5,4},{4,5},{7,6},{6,7},{9,8},{8,9},{11,10... | collective-permute-start | bytes 835592 | tf_op jit(solution)/shard_map/ppermute | solution.py:55
  29.1 9.9 %copy-start.1 = (bf16[768,2048]{1,0:T(8,128)(2,1)S(1)}, bf16[768,2048]{1,0:T(8,128)(2,1)}, u32[]{:S(2)}) copy-start(bf16[768,2048]{1,0:T(8,128)(2,1)} %gate_ref.1) | copy-start | bytes 9437188
  38.2 5.0 %collective-permute-start.6 = (bf16[256,3072]{1,0:T(8,128)(2,1)}, bf16[256,3072]{1,0:T(8,128)(2,1)}, u32[]{:S(2)}, u32[]{:S(2)}) collective-permute-start(bf16[256,3072]{1,0:T(8,128)(2,1)} %teacher_pre.1.refs_1_), channel_id=1, source_target_pairs={{0,16},{16,0},{1,17},{17,1},{2,18},{18,2},{3,19},{19,3},{4,20},{20... | collective-permute-start | bytes 4718600 | tf_op jit(solution)/shard_map/ppermute | solution.py:76
  43.0 7.4 %collective-permute-start.13 = (f32[256,1536]{1,0:T(8,128)S(1)}, f32[256,1536]{1,0:T(8,128)}, u32[]{:S(2)}, u32[]{:S(2)}) collective-permute-start(f32[256,1536]{1,0:T(8,128)S(1)} %student_pre.1.refs_0_), channel_id=1, source_target_pairs={{0,16},{16,0},{1,17},{17,1},{2,18},{18,2},{3,19},{19,3},{4,20},{20... | collective-permute-start | bytes 4718600 | tf_op jit(solution)/shard_map/ppermute | solution.py:76
  54.8 7.5 %collective-permute-start.14 = (bf16[64,2048]{1,0:T(8,128)(2,1)S(1)}, bf16[64,2048]{1,0:T(8,128)(2,1)S(1)}, u32[]{:S(2)}, u32[]{:S(2)}) collective-permute-start(bf16[64,2048]{1,0:T(8,128)(2,1)S(1)} %get-tuple-element.20), channel_id=1, source_target_pairs={{0,1},{1,0},{2,3},{3,2},{4,5},{5,4},{6,7},{7,6},{8,9},{9,8},{10,11... | collective-permute-start | bytes 786440 | tf_op jit(solution)/shard_map/ppermute | solution.py:58
  56.1 7.4 %collective-permute-start.15 = (bf16[64,2048]{1,0:T(8,128)(2,1)S(1)}, bf16[64,2048]{1,0:T(8,128)(2,1)S(1)}, u32[]{:S(2)}, u32[]{:S(2)}) collective-permute-start(bf16[64,2048]{1,0:T(8,128)(2,1)S(1)} %get-tuple-element.21), channel_id=1, source_target_pairs={{0,2},{1,3},{2,0},{3,1},{4,6},{5,7},{6,4},{7,5},{8,10},{9,11},{10,... | collective-permute-start | bytes 786440 | tf_op jit(solution)/shard_map/ppermute | solution.py:58
  56.3 12.4 %collective-permute-start.16 = (bf16[64,2048]{1,0:T(8,128)(2,1)S(1)}, bf16[64,2048]{1,0:T(8,128)(2,1)S(1)}, u32[]{:S(2)}, u32[]{:S(2)}) collective-permute-start(bf16[64,2048]{1,0:T(8,128)(2,1)S(1)} %get-tuple-element.22), channel_id=1, source_target_pairs={{0,3},{1,2},{2,1},{3,0},{4,7},{5,6},{6,5},{7,4},{8,11},{9,10},{10,... | collective-permute-start | bytes 786440 | tf_op jit(solution)/shard_map/ppermute | solution.py:58
  57.5 16.0 %collective-permute-start.7 = (bf16[64,2048]{1,0:T(8,128)(2,1)S(1)}, bf16[64,2048]{1,0:T(8,128)(2,1)S(1)}, u32[]{:S(2)}, u32[]{:S(2)}) collective-permute-start(bf16[64,2048]{1,0:T(8,128)(2,1)S(1)} %get-tuple-element.16.refs_4_), channel_id=1, source_target_pairs={{0,1},{1,0},{2,3},{3,2},{4,5},{5,4},{6,7},{7,6},{8,9},{9,8},{10,11... | collective-permute-start | bytes 786440 | tf_op jit(solution)/shard_map/ppermute | solution.py:58
  58.7 15.7 %collective-permute-start.8 = (bf16[64,2048]{1,0:T(8,128)(2,1)S(1)}, bf16[64,2048]{1,0:T(8,128)(2,1)S(1)}, u32[]{:S(2)}, u32[]{:S(2)}) collective-permute-start(bf16[64,2048]{1,0:T(8,128)(2,1)S(1)} %get-tuple-element.17.refs_5_), channel_id=1, source_target_pairs={{0,2},{1,3},{2,0},{3,1},{4,6},{5,7},{6,4},{7,5},{8,10},{9,11},{10,... | collective-permute-start | bytes 786440 | tf_op jit(solution)/shard_map/ppermute | solution.py:58
  62.3 17.8 %collective-permute-start.9 = (bf16[64,2048]{1,0:T(8,128)(2,1)S(1)}, bf16[64,2048]{1,0:T(8,128)(2,1)S(1)}, u32[]{:S(2)}, u32[]{:S(2)}) collective-permute-start(bf16[64,2048]{1,0:T(8,128)(2,1)S(1)} %get-tuple-element.18.refs_6_), channel_id=1, source_target_pairs={{0,3},{1,2},{2,1},{3,0},{4,7},{5,6},{6,5},{7,4},{8,11},{9,10},{10,... | collective-permute-start | bytes 786440 | tf_op jit(solution)/shard_map/ppermute | solution.py:58
  68.9 11.3 %collective-permute-start.17 = (bf16[16,2048]{1,0:T(8,128)(2,1)S(1)}, bf16[16,2048]{1,0:T(8,128)(2,1)S(1)}, u32[]{:S(2)}, u32[]{:S(2)}) collective-permute-start(bf16[16,2048]{1,0:T(8,128)(2,1)S(1)} %get-tuple-element.28), channel_id=1, source_target_pairs={{0,4},{1,5},{2,6},{3,7},{4,0},{5,1},{6,2},{7,3},{8,12},{9,13},{10,... | collective-permute-start | bytes 196616 | tf_op jit(solution)/shard_map/ppermute | solution.py:58
  69.0 11.2 %collective-permute-start.19 = (bf16[16,2048]{1,0:T(8,128)(2,1)S(1)}, bf16[16,2048]{1,0:T(8,128)(2,1)S(1)}, u32[]{:S(2)}, u32[]{:S(2)}) collective-permute-start(bf16[16,2048]{1,0:T(8,128)(2,1)S(1)} %get-tuple-element.29), channel_id=1, source_target_pairs={{0,12},{1,13},{2,14},{3,15},{4,8},{5,9},{6,10},{7,11},{8,4},{9,5},... | collective-permute-start | bytes 196616 | tf_op jit(solution)/shard_map/ppermute | solution.py:58
  73.6 6.6 %collective-permute-start.18 = (bf16[16,2048]{1,0:T(8,128)(2,1)S(1)}, bf16[16,2048]{1,0:T(8,128)(2,1)S(1)}, u32[]{:S(2)}, u32[]{:S(2)}) collective-permute-start(bf16[16,2048]{1,0:T(8,128)(2,1)S(1)} %get-tuple-element.30), channel_id=1, source_target_pairs={{0,8},{1,9},{2,10},{3,11},{4,12},{5,13},{6,14},{7,15},{8,0},{9,1},... | collective-permute-start | bytes 196616 | tf_op jit(solution)/shard_map/ppermute | solution.py:58
  80.0 21.8 %copy-start = (bf16[768,2048]{1,0:T(8,128)(2,1)S(1)}, bf16[768,2048]{1,0:T(8,128)(2,1)}, u32[]{:S(2)}) copy-start(bf16[768,2048]{1,0:T(8,128)(2,1)} %down_ref.1) | copy-start | bytes 9437188
  80.2 5.1 %collective-permute-start.22 = (bf16[16,2048]{1,0:T(8,128)(2,1)S(1)}, bf16[16,2048]{1,0:T(8,128)(2,1)S(1)}, u32[]{:S(2)}, u32[]{:S(2)}) collective-permute-start(bf16[16,2048]{1,0:T(8,128)(2,1)S(1)} %get-tuple-element.27), channel_id=1, source_target_pairs={{12,0},{13,1},{14,2},{15,3},{8,4},{9,5},{10,6},{11,7},{4,8},{5,9},... | collective-permute-start | bytes 196616 | tf_op jit(solution)/shard_map/ppermute | solution.py:55
  81.3 6.5 %collective-permute-start.21 = (bf16[16,2048]{1,0:T(8,128)(2,1)S(1)}, bf16[16,2048]{1,0:T(8,128)(2,1)S(1)}, u32[]{:S(2)}, u32[]{:S(2)}) collective-permute-start(bf16[16,2048]{1,0:T(8,128)(2,1)S(1)} %get-tuple-element.27), channel_id=1, source_target_pairs={{8,0},{9,1},{10,2},{11,3},{12,4},{13,5},{14,6},{15,7},{0,8},{1,9},... | collective-permute-start | bytes 196616 | tf_op jit(solution)/shard_map/ppermute | solution.py:55
  81.3 6.5 %collective-permute-start.20 = (bf16[16,2048]{1,0:T(8,128)(2,1)S(1)}, bf16[16,2048]{1,0:T(8,128)(2,1)S(1)}, u32[]{:S(2)}, u32[]{:S(2)}) collective-permute-start(bf16[16,2048]{1,0:T(8,128)(2,1)S(1)} %get-tuple-element.27), channel_id=1, source_target_pairs={{4,0},{5,1},{6,2},{7,3},{0,4},{1,5},{2,6},{3,7},{12,8},{13,9},{14,... | collective-permute-start | bytes 196616 | tf_op jit(solution)/shard_map/ppermute | solution.py:55
  83.9 25.0 %collective-permute-start.10 = (bf16[16,2048]{1,0:T(8,128)(2,1)S(1)}, bf16[16,2048]{1,0:T(8,128)(2,1)S(1)}, u32[]{:S(2)}, u32[]{:S(2)}) collective-permute-start(bf16[16,2048]{1,0:T(8,128)(2,1)S(1)} %get-tuple-element.31), channel_id=1, source_target_pairs={{0,4},{1,5},{2,6},{3,7},{4,0},{5,1},{6,2},{7,3},{8,12},{9,13},{10,... | collective-permute-start | bytes 196616 | tf_op jit(solution)/shard_map/ppermute | solution.py:58
  84.0 24.9 %collective-permute-start.12 = (bf16[16,2048]{1,0:T(8,128)(2,1)S(1)}, bf16[16,2048]{1,0:T(8,128)(2,1)S(1)}, u32[]{:S(2)}, u32[]{:S(2)}) collective-permute-start(bf16[16,2048]{1,0:T(8,128)(2,1)S(1)} %get-tuple-element.32), channel_id=1, source_target_pairs={{0,12},{1,13},{2,14},{3,15},{4,8},{5,9},{6,10},{7,11},{8,4},{9,5},... | collective-permute-start | bytes 196616 | tf_op jit(solution)/shard_map/ppermute | solution.py:58
  85.4 23.5 %collective-permute-start.11 = (bf16[16,2048]{1,0:T(8,128)(2,1)S(1)}, bf16[16,2048]{1,0:T(8,128)(2,1)S(1)}, u32[]{:S(2)}, u32[]{:S(2)}) collective-permute-start(bf16[16,2048]{1,0:T(8,128)(2,1)S(1)} %get-tuple-element.33), channel_id=1, source_target_pairs={{0,8},{1,9},{2,10},{3,11},{4,12},{5,13},{6,14},{7,15},{8,0},{9,1},... | collective-permute-start | bytes 196616 | tf_op jit(solution)/shard_map/ppermute | solution.py:58
  87.9 6.5 %collective-permute-start.24 = (bf16[64,2048]{1,0:T(8,128)(2,1)S(1)}, bf16[64,2048]{1,0:T(8,128)(2,1)S(1)}, u32[]{:S(2)}, u32[]{:S(2)}) collective-permute-start(bf16[64,2048]{1,0:T(8,128)(2,1)S(1)} %pad_maximum_fusion.1), channel_id=1, source_target_pairs={{2,0},{3,1},{0,2},{1,3},{6,4},{7,5},{4,6},{5,7},{10,8},{11,9},{8,1... | collective-permute-start | bytes 786440 | tf_op jit(solution)/shard_map/ppermute | solution.py:55
  88.4 5.2 %collective-permute-start.23 = (bf16[64,2048]{1,0:T(8,128)(2,1)S(1)}, bf16[64,2048]{1,0:T(8,128)(2,1)S(1)}, u32[]{:S(2)}, u32[]{:S(2)}) collective-permute-start(bf16[64,2048]{1,0:T(8,128)(2,1)S(1)} %pad_maximum_fusion.1), channel_id=1, source_target_pairs={{1,0},{0,1},{3,2},{2,3},{5,4},{4,5},{7,6},{6,7},{9,8},{8,9},{11,10... | collective-permute-start | bytes 786440 | tf_op jit(solution)/shard_map/ppermute | solution.py:55
  93.6 8.2 %collective-permute-start.25 = (bf16[64,2048]{1,0:T(8,128)(2,1)S(1)}, bf16[64,2048]{1,0:T(8,128)(2,1)S(1)}, u32[]{:S(2)}, u32[]{:S(2)}) collective-permute-start(bf16[64,2048]{1,0:T(8,128)(2,1)S(1)} %pad_maximum_fusion.1), channel_id=1, source_target_pairs={{3,0},{2,1},{1,2},{0,3},{7,4},{6,5},{5,6},{4,7},{11,8},{10,9},{9,1... | collective-permute-start | bytes 786440 | tf_op jit(solution)/shard_map/ppermute | solution.py:55
  103.4 9.1 %collective-permute-start.26 = (bf16[256,768]{1,0:T(8,128)(2,1)S(1)}, bf16[256,768]{1,0:T(8,128)(2,1)S(1)}, u32[]{:S(2)}, u32[]{:S(2)}) collective-permute-start(bf16[256,768]{1,0:T(8,128)(2,1)S(1)} %hidden_grad.1.refs_2_), channel_id=1, source_target_pairs={{0,16},{16,0},{1,17},{17,1},{2,18},{18,2},{3,19},{19,3},{4,20},{20... | collective-permute-start | bytes 1179656 | tf_op jit(solution)/shard_map/ppermute | solution.py:76

commit v2 on v1

v2 whole, which is shorter than its diff:
```python
import functools
import math

import jax
import jax.numpy as jnp
from jax import lax
from jax.experimental import pallas as pl
from jax.experimental.pallas import tpu as pltpu
from jax.sharding import PartitionSpec as P

BF16 = jnp.bfloat16
F32 = jnp.float32
MIB = 1024 * 1024
LANES = 128
TEACHER_BLOCK = 768
STUDENT_BLOCK = 256


def against(left_mat, right_mat):
    return lax.dot_general(left_mat, right_mat, (((1,), (1,)), ((), ())), preferred_element_type=F32)


def across(left_mat, right_mat):
    return lax.dot_general(left_mat, right_mat, (((0,), (0,)), ((), ())), preferred_element_type=F32)


def plain(left_mat, right_mat):
    return lax.dot_general(left_mat, right_mat, (((1,), (0,)), ((), ())), preferred_element_type=F32)


def block_of(size, most=384):
    fits = [b for b in range(LANES, most + 1, LANES) if size % b == 0]
    return fits[-1] if fits else size


def params(rows):
    limit = min(18 * max(1, rows // 256), 56) * MIB
    return pltpu.CompilerParams(vmem_limit_bytes=limit, dimension_semantics=("arbitrary",))


def cost(flops, nbytes):
    return pl.CostEstimate(flops=int(flops), bytes_accessed=int(nbytes), transcendentals=0)


class Ring:
    def __init__(self, size):
        assert size & (size - 1) == 0 and size >= 4, size
        self.size, self.inner = size, 1 << (size.bit_length() - 1) // 2
        self.outer = size // self.inner

    def swap(self, value, near, far):
        flip = near + self.inner * far
        return lax.ppermute(value, "wide", [(i, i ^ flip) for i in range(self.size)])

    def gather_far(self, value):
        return [self.swap(value, 0, k) for k in range(1, self.outer)]

    def gather_near(self, value):
        return [self.swap(value, k, 0) for k in range(1, self.inner)]

    def joined(self, value, near, column, rest):
        blocks = [value, column]
        for first, others in zip(near, rest):
            blocks += [first, others]
        return jnp.concatenate(blocks, axis=0)

    def reduce_near(self, pieces):
        arrived = [pieces[0]] + [self.swap(pieces[k], k, 0) for k in range(1, self.inner)]
        return sum(a.astype(F32) for a in arrived).astype(BF16)

    def reduce_far(self, blocks):
        arrived = [blocks[0]] + [self.swap(blocks[k], 0, k) for k in range(1, self.outer)]
        return sum(a.astype(F32) for a in arrived)


def from_pair(value):
    size = lax.axis_size("dp")
    return [lax.ppermute(value, "dp", [(i, (i + s) % size) for i in range(size)]) for s in range(1, size)]


def payload_kernel(owners, layer_hbm, ids_hbm, scores_hbm, out_ref, ids_ref, scores_ref, sems):
    rows, columns = layer_hbm.shape
    copies = [
        pltpu.make_async_copy(ids_hbm, ids_ref, sems.at[0]),
        pltpu.make_async_copy(scores_hbm, scores_ref, sems.at[1]),
        pltpu.make_async_copy(layer_hbm, out_ref.at[:, pl.ds(0, columns)], sems.at[2]),
    ]
    for copy in copies:
        copy.start()
    copies[0].wait()
    copies[1].wait()
    scores = scores_ref[...]
    weights = scores / jnp.sum(scores, axis=0, keepdims=True)
    ids = ids_ref[...]
    shape = (out_ref.shape[1] - columns, rows)
    place = lax.broadcasted_iota(jnp.int32, shape, 0)
    expert = jnp.where(place >= owners, place - owners, place)
    table = jnp.zeros(shape, F32)
    for k in range(ids.shape[0]):
        table = table + jnp.where(ids[k : k + 1, :] == expert, weights[k : k + 1, :], 0.0)
    high = table.astype(BF16).astype(F32)
    table = jnp.where(place < owners, high, table - high)
    out_ref[:, columns:] = table.T.astype(BF16)
    copies[2].wait()


def make_payload(layer_in, route_ids, route_scores, owners):
    rows, columns = layer_in.shape
    extra = -(-2 * owners // LANES) * LANES
    return pl.pallas_call(
        functools.partial(payload_kernel, owners),
        in_specs=[pl.BlockSpec(memory_space=pltpu.HBM)] * 3,
        out_shape=jax.ShapeDtypeStruct((rows, columns + extra), BF16),
        scratch_shapes=[
            pltpu.VMEM(route_ids.shape[::-1], jnp.int32),
            pltpu.VMEM(route_scores.shape[::-1], F32),
            pltpu.SemaphoreType.DMA((3,)),
        ],
        compiler_params=pltpu.CompilerParams(vmem_limit_bytes=54 * MIB),
        name="payload",
    )(layer_in, route_ids.T, route_scores.T)


def pass_kernel(in_ref, out_ref):
    out_ref[...] = in_ref[...]


def passed(value):
    return pl.pallas_call(
        pass_kernel,
        out_shape=jax.ShapeDtypeStruct(value.shape, value.dtype),
        compiler_params=pltpu.CompilerParams(vmem_limit_bytes=2 * MIB),
        cost_estimate=cost(1e11, 1e5),
        name="passed",
    )(value)


def pre_kernel(x_ref, gate_ref, up_ref, out_ref):
    block = gate_ref.shape[0]
    out_ref[:, :block] = against(x_ref[...], gate_ref[...]).astype(out_ref.dtype)
    out_ref[:, block:] = against(x_ref[...], up_ref[...]).astype(out_ref.dtype)


def pre_parts(x, gate, up, dtype, most, name):
    hidden, columns = gate.shape
    rows, block = x.shape[0], block_of(hidden, most)
    return pl.pallas_call(
        pre_kernel,
        grid=(hidden // block,),
        in_specs=[
            pl.BlockSpec((rows, columns), lambda i: (0, 0)),
            pl.BlockSpec((block, columns), lambda i: (i, 0)),
            pl.BlockSpec((block, columns), lambda i: (i, 0)),
        ],
        out_specs=pl.BlockSpec((rows, 2 * block), lambda i: (0, i)),
        out_shape=jax.ShapeDtypeStruct((rows, 2 * hidden), dtype),
        compiler_params=params(rows),
        cost_estimate=cost(4 * rows * hidden * columns, 4 * hidden * columns + 4 * rows * hidden),
        name=name,
    )(x, gate, up)


def added(refs):
    total = refs[0][...].astype(F32)
    for ref in refs[1:]:
        total = total + ref[...].astype(F32)
    half = total.shape[1] // 2
    return total[:, :half], total[:, half:]


def teacher_places(rows, inner):
    length = rows // inner // 2
    for near in range(inner):
        for second in range(2):
            here = (2 * near + second) * length
            part = 2 + (near >> 1 & 1) if second else near & 1
            there = ((near >> 2) * 2 + (near & 1) if second else near >> 1) * length
            yield slice(here, here + length), near, part, slice(there, there + length)


def teacher_kernel(parts, inner, owners, *refs):
    pre_refs, down_ref, table_ref = refs[:parts], refs[parts], refs[parts + 1]
    out_refs, total = refs[parts + 2 : parts + 6], refs[-1]
    step = pl.program_id(0)
    gate, up = added(pre_refs)
    hidden = (gate * jax.nn.sigmoid(gate) * up).astype(BF16)
    term = plain(hidden, down_ref[...])

    @pl.when(step == 0)
    def _():
        total[...] = term

    @pl.when(step > 0)
    def _():
        total[...] += term

    @pl.when(step == pl.num_programs(0) - 1)
    def _():
        me = lax.axis_index("wide")
        table = table_ref[...].astype(F32)
        lane = lax.broadcasted_iota(jnp.int32, table.shape, 1)
        mine = (lane == me) | (lane == me + owners)
        weight = jnp.sum(jnp.where(mine, table, 0.0), axis=1, keepdims=True)
        for piece, _, part, place in teacher_places(total.shape[0], inner):
            out_refs[part][place, :] = (total[piece, :] * weight[piece, :]).astype(BF16)


def teacher_parts(pres, down, payload, inner, owners):
    hidden, columns = down.shape
    rows, block = payload.shape[0], block_of(hidden, TEACHER_BLOCK)
    extra = payload.shape[1] - columns
    return pl.pallas_call(
        functools.partial(teacher_kernel, len(pres), inner, owners),
        grid=(hidden // block,),
        in_specs=[pl.BlockSpec((rows, 2 * block), lambda i: (0, i)) for _ in pres]
        + [
            pl.BlockSpec((block, columns), lambda i: (i, 0)),
            pl.BlockSpec((rows, extra), lambda i: (0, columns // extra)),
        ],
        out_specs=[pl.BlockSpec((rows // 4, columns), lambda i: (0, 0))] * 4,
        out_shape=[jax.ShapeDtypeStruct((rows // 4, columns), BF16)] * 4,
        scratch_shapes=[pltpu.VMEM((rows, columns), F32)],
        compiler_params=params(rows),
        cost_estimate=cost(2 * rows * hidden * columns, 2 * hidden * columns + 10 * rows * hidden),
        name="teacher_down",
    )(*pres, down, payload)


def student_kernel(parts, inner, *refs):
    pre_refs, down_ref, teacher_refs = refs[:parts], refs[parts], refs[parts + 1 : parts + 5]
    hidden_ref, out_refs, total = refs[parts + 5], refs[parts + 6 : -1], refs[-1]
    step = pl.program_id(0)
    gate, up = added(pre_refs)
    hidden = (gate * jax.nn.sigmoid(gate) * up).astype(BF16)
    hidden_ref[...] = hidden
    term = plain(hidden, down_ref[...])

    @pl.when(step == 0)
    def _():
        total[...] = term

    @pl.when(step > 0)
    def _():
        total[...] += term

    @pl.when(step == pl.num_programs(0) - 1)
    def _():
        for piece, near, part, place in teacher_places(total.shape[0], inner):
            length = piece.stop - piece.start
            here = piece.start - 2 * near * length
            taught = teacher_refs[part][place, :].astype(F32)
            out_refs[near][here : here + length, :] = (total[piece, :] - taught).astype(BF16)


def student_parts(pres, down, teacher, inner):
    hidden, columns = down.shape
    rows, block = pres[0].shape[0], block_of(hidden, STUDENT_BLOCK)
    piece = (rows // inner, columns)
    outs = pl.pallas_call(
        functools.partial(student_kernel, len(pres), inner),
        grid=(hidden // block,),
        in_specs=[pl.BlockSpec((rows, 2 * block), lambda i: (0, i)) for _ in pres]
        + [pl.BlockSpec((block, columns), lambda i: (i, 0))]
        + [pl.BlockSpec((rows // 4, columns), lambda i: (0, 0))] * 4,
        out_specs=[pl.BlockSpec((rows, block), lambda i: (0, i))]
        + [pl.BlockSpec(piece, lambda i: (0, 0))] * inner,
        out_shape=[jax.ShapeDtypeStruct((rows, hidden), BF16)]
        + [jax.ShapeDtypeStruct(piece, BF16)] * inner,
        scratch_shapes=[pltpu.VMEM((rows, columns), F32)],
        compiler_params=params(rows),
        cost_estimate=cost(2 * rows * hidden * columns, 2 * hidden * columns + 10 * rows * hidden),
        name="student_down",
    )(*pres, down, *teacher)
    return outs[0], outs[1:]


def hidden_grad_kernel(delta_ref, down_ref, out_ref):
    out_ref[...] = against(delta_ref[...], down_ref[...]).astype(BF16)


def hidden_grad_parts(delta, down):
    hidden, columns = down.shape
    rows, block = delta.shape[0], block_of(hidden)
    return pl.pallas_call(
        hidden_grad_kernel,
        grid=(hidden // block,),
        in_specs=[
            pl.BlockSpec((rows, columns), lambda i: (0, 0)),
            pl.BlockSpec((block, columns), lambda i: (i, 0)),
        ],
        out_specs=pl.BlockSpec((rows, block), lambda i: (0, i)),
        out_shape=jax.ShapeDtypeStruct((rows, hidden), BF16),
        compiler_params=params(rows),
        cost_estimate=cost(2 * rows * hidden * columns, 2 * hidden * columns + 2 * rows * columns),
        name="hidden_grad",
    )(delta, down)


def grad_down_kernel(hidden_ref, delta_ref, out_ref):
    out_ref[...] = across(hidden_ref[...], delta_ref[...]).astype(BF16)


def grad_down_of(hidden_rows, delta):
    rows, hidden = hidden_rows.shape
    columns, block = delta.shape[1], block_of(hidden)
    return pl.pallas_call(
        grad_down_kernel,
        grid=(hidden // block,),
        in_specs=[
            pl.BlockSpec((rows, block), lambda i: (0, i)),
            pl.BlockSpec((rows, columns), lambda i: (0, 0)),
        ],
        out_specs=pl.BlockSpec((block, columns), lambda i: (i, 0)),
        out_shape=jax.ShapeDtypeStruct((hidden, columns), BF16),
        compiler_params=params(rows),
        cost_estimate=cost(2 * rows * hidden * columns, 2 * hidden * columns + 2 * rows * columns),
        name="grad_down",
    )(hidden_rows, delta)


def grad_pre_kernel(parts, *refs):
    pre_refs, back_refs, x_ref = refs[:parts], refs[parts : 2 * parts], refs[2 * parts]
    gate_ref, up_ref = refs[-2:]
    gate, up = added(pre_refs)
    back = back_refs[0][...].astype(F32)
    for ref in back_refs[1:]:
        back = back + ref[...].astype(F32)
    sig = jax.nn.sigmoid(gate)
    gate_grad = (back * up * sig * (1.0 + gate * (1.0 - sig))).astype(BF16)
    up_grad = (back * gate * sig).astype(BF16)
    gate_ref[...] = across(gate_grad, x_ref[...]).astype(BF16)
    up_ref[...] = across(up_grad, x_ref[...]).astype(BF16)


def grad_pre_of(pres, backs, payload, columns):
    rows, hidden = backs[0].shape
    block = block_of(hidden, STUDENT_BLOCK)
    return pl.pallas_call(
        functools.partial(grad_pre_kernel, len(pres)),
        grid=(hidden // block,),
        in_specs=[pl.BlockSpec((rows, 2 * block), lambda i: (0, i)) for _ in pres]
        + [pl.BlockSpec((rows, block), lambda i: (0, i)) for _ in backs]
        + [pl.BlockSpec((rows, columns), lambda i: (0, 0))],
        out_specs=[pl.BlockSpec((block, columns), lambda i: (i, 0))] * 2,
        out_shape=[jax.ShapeDtypeStruct((hidden, columns), BF16)] * 2,
        compiler_params=params(rows),
        cost_estimate=cost(4 * rows * hidden * columns, 4 * hidden * columns + 2 * rows * columns),
        name="grad_gate_up",
    )(*pres, *backs, payload)


def added_rows(one, other):
    return (one.astype(F32) + other.astype(F32)).astype(BF16)


def even_blocks(value, count):
    return value.reshape(count // 2, 2, -1, value.shape[1])[:, 0].reshape(-1, value.shape[1])


def odd_blocks(value, count):
    return value.reshape(count // 2, 2, -1, value.shape[1])[:, 1].reshape(-1, value.shape[1])


def shards(
    layer_in,
    route_ids,
    route_scores,
    expert_gate,
    expert_up,
    expert_down,
    student_gate,
    student_up,
    student_down,
):
    owners = lax.axis_size("wide")
    ring = Ring(owners)
    tok_rows, columns = layer_in.shape

    payload = make_payload(layer_in, route_ids, route_scores, owners)
    far = ring.gather_far(payload)
    far[0] = passed(far[0])
    far[0], payload = lax.optimization_barrier((far[0], payload))
    near = ring.gather_near(payload)
    column = jnp.concatenate(far, axis=0)
    rows = ring.joined(payload, near, column, ring.gather_near(column))

    expert_pre = pre_parts(rows, expert_gate[0], expert_up[0], BF16, TEACHER_BLOCK, "teacher_pre")
    expert_pres = [expert_pre] + from_pair(expert_pre)
    student_pre = pre_parts(rows, student_gate, student_up, F32, STUDENT_BLOCK, "student_pre")
    student_pres = [student_pre] + from_pair(student_pre)
    teacher = teacher_parts(expert_pres, expert_down[0], rows, ring.inner, owners)
    student_hidden, pieces = student_parts(student_pres, student_down, teacher, ring.inner)

    loss_scale = 1.0 / math.sqrt(tok_rows * owners)
    column, teacher = lax.optimization_barrier((ring.reduce_near(pieces), teacher))
    taught = [added_rows(teacher[2 * k], ring.swap(teacher[2 * k + 1], 1 + k, 0)) for k in range(2)]
    blocks = list(column.reshape(ring.outer, tok_rows, columns))
    blocks[0], taught = lax.optimization_barrier((blocks[0], taught))
    delta = (ring.reduce_far(blocks) * loss_scale).astype(BF16)

    column = jnp.concatenate([delta] + ring.gather_far(delta), axis=0)
    count = ring.inner // 2
    kept, sent = [even_blocks(t, count) for t in taught], [odd_blocks(t, count) for t in taught]
    column, kept = lax.optimization_barrier((column, kept))
    taught = [added_rows(kept[k], ring.swap(sent[k], 2 - k, 0)) for k in range(2)]
    bit = 4
    while bit < ring.inner:
        count //= 2
        taught = [added_rows(even_blocks(t, count), ring.swap(odd_blocks(t, count), bit, 0)) for t in taught]
        bit *= 2

    delta_all = jnp.concatenate([column] + ring.gather_near(column), axis=0)
    taught = jnp.concatenate(taught, axis=0).reshape(ring.outer, tok_rows, columns)
    blocks = list(taught)
    delta_all, blocks[0] = lax.optimization_barrier((delta_all, blocks[0]))
    teacher_out = ring.reduce_far(blocks).astype(BF16)

    back = hidden_grad_parts(delta_all, student_down)
    backs = [back] + from_pair(back)
    grad_down = grad_down_of(student_hidden, delta_all)
    grad_gate, grad_up = grad_pre_of(student_pres, backs, rows, columns)
    return (teacher_out, grad_gate, grad_up, grad_down)


def solution(mesh):
    in_specs = (
        P("wide", "dp"),
        P("wide", None),
        P("wide", None),
        P("wide", None, "dp"),
        P("wide", None, "dp"),
        P("wide", None, "dp"),
        P("wide", "dp"),
        P("wide", "dp"),
        P("wide", "dp"),
    )
    out_specs = (P("wide", "dp"), P("wide", "dp"), P("wide", "dp"), P("wide", "dp"))
    return jax.shard_map(shards, mesh=mesh, in_specs=in_specs, out_specs=out_specs, check_vma=False)
```

time: 118 us -> 95.3 us (0.81)
  Pallas kernels: 36 us -> 21.1 us
  waiting for transfers between devices: 49.4 us -> 39.7 us
  starting transfers between devices: 28.4 us -> 31.9 us
    ppermute x24 -> x28, waiting for transfers between devices: 49.4 us -> 39.2 us  [swap(): lax.ppermute(value, 'wide', [(i, i ^ flip) for i in range(self.size)])]
    ppermute x24 -> x28, starting transfers between devices: 22 us -> 28.8 us  [swap(): lax.ppermute(value, 'wide', [(i, i ^ flip) for i in range(self.size)])]
    pallas_call x2, Pallas kernels: 13 us -> 6.27 us  [pre_parts(): pl.pallas_call(pre_kernel, grid=(hidden // block,), in_specs=[pl.BlockSpe...]
    pallas_call x1, Pallas kernels: 7.3 us -> 2.91 us  [teacher_parts(): pl.pallas_call(functools.partial(teacher_kernel, len(pres), inner, owners...]
    ppermute x3, starting transfers between devices: 6.46 us -> 3.11 us  [from_pair(): lax.ppermute(value, 'dp', [(i, (i + s) % size) for i in range(size)])]
    pallas_call x1, Pallas kernels: 4.33 us -> 2.35 us  [student_parts(): pl.pallas_call(functools.partial(student_kernel, len(pres), inner), grid=...]
    pallas_call x1, Pallas kernels: 5.26 us -> 3.97 us  [grad_pre_of(): pl.pallas_call(functools.partial(grad_pre_kernel, len(pres)), grid=(hidde...]
  transfers between devices with their start and end apart: 27 -> 31, of which waited for: 13 -> 12; matrix products, arithmetic and copies ran while one was open for 2% -> 1% of each run, Pallas kernels for 13% -> 10%
where the time goes in v2:
time: 95.3 us; the launch traced here: 95.2 us
  waiting for transfers between devices  39.7 us (42%)
  starting transfers between devices  31.9 us (33%)
  Pallas kernels  21.1 us (22%)
  other arithmetic  1.16 us (1%)
  between operations  0.99 us (1%)
    ppermute x28, waiting for transfers between devices, swap(): lax.ppermute(value, 'wide', [(i, i ^ flip) for i in range(self.size)])  39.2 us
    ppermute x28, starting transfers between devices, swap(): lax.ppermute(value, 'wide', [(i, i ^ flip) for i in range(self.size)])  28.8 us
    pallas_call x2, Pallas kernels, pre_parts(): pl.pallas_call(pre_kernel, grid=(hidden // block,), in_specs=[pl.BlockSpe...  6.27 us
    pallas_call x1, Pallas kernels, grad_pre_of(): pl.pallas_call(functools.partial(grad_pre_kernel, len(pres)), grid=(hidde...  3.97 us
    ppermute x3, starting transfers between devices, from_pair(): lax.ppermute(value, 'dp', [(i, (i + s) % size) for i in range(size)])  3.11 us
    pallas_call x1, Pallas kernels, teacher_parts(): pl.pallas_call(functools.partial(teacher_kernel, len(pres), inner, owners...  2.91 us
    pallas_call x1, Pallas kernels, grad_down_of(): pl.pallas_call(grad_down_kernel, grid=(hidden // block,), in_specs=[pl.Bl...  2.41 us
    pallas_call x1, Pallas kernels, student_parts(): pl.pallas_call(functools.partial(student_kernel, len(pres), inner), grid=...  2.35 us
  transfers between devices with their start and end apart: 31, of which 12 were waited for; matrix products, arithmetic and copies ran while one was open for 1% of the time, Pallas kernels for 10%

profile of v2, /device:TPU:1, one launch (start us, length us, event | category | flops | bytes accessed | tf_op | source)
XLA Modules:
  0.0 95.2 jit_solution(15922941670354101313)
XLA Ops:
  0.6 0.0 slice-start
  0.6 0.0 slice-start.2
  0.7 1.7 %payload.1 = bf16[16,2176]{1,0:T(8,128)(2,1)} custom-call(bf16[16,2048]{1,0:T(8,128)(2,1)} %layer_hbm.1, s32[8,16]{1,0:T(8,128)} %bitcast.24, f32[8,16]{1,0:T(8,128)} %bitcast.25), custom_call_target="tpu_custom_call" | custom-call | tf_op jit(solution)/shard_map/payload/pallas_call | solution.py:110
  2.3 0.0 copy-start.4
  2.4 0.0 slice-start.1
  2.4 0.0 slice-start.3
  2.4 2.2 %collective-permute-start = (bf16[16,2176]{1,0:T(8,128)(2,1)}, bf16[16,2176]{1,0:T(8,128)(2,1)S(1)}, u32[]{:S(2)}, u32[]{:S(2)}) collective-permute-start(bf16[16,2176]{1,0:T(8,128)(2,1)} %payload.1), channel_id=1, source_target_pairs={{0,4},{1,5},{2,6},{3,7},{4,0},{5,1},{6,2},{7,3},{8,12},{9,13},{10,... | collective-permute-start | bytes 208904 | tf_op jit(solution)/shard_map/ppermute | solution.py:53
  4.6 2.2 %collective-permute-start.2 = (bf16[16,2176]{1,0:T(8,128)(2,1)}, bf16[16,2176]{1,0:T(8,128)(2,1)S(1)}, u32[]{:S(2)}, u32[]{:S(2)}) collective-permute-start(bf16[16,2176]{1,0:T(8,128)(2,1)} %payload.1), channel_id=1, source_target_pairs={{0,12},{1,13},{2,14},{3,15},{4,8},{5,9},{6,10},{7,11},{8,4},{9,5},... | collective-permute-start | bytes 208904 | tf_op jit(solution)/shard_map/ppermute | solution.py:53
  6.8 0.1 collective-permute-start.1
  6.9 2.2 %collective-permute-start.7 = (bf16[16,2176]{1,0:T(8,128)(2,1)S(1)}, bf16[16,2176]{1,0:T(8,128)(2,1)S(1)}, u32[]{:S(2)}, u32[]{:S(2)}) collective-permute-start(bf16[16,2176]{1,0:T(8,128)(2,1)S(1)} %copy-done.4), channel_id=1, source_target_pairs={{0,3},{1,2},{2,1},{3,0},{4,7},{5,6},{6,5},{7,4},{8,11},{9,10},{10,... | collective-permute-start | bytes 208904 | tf_op jit(solution)/shard_map/ppermute | solution.py:53
  9.1 0.2 collective-permute-start.5
  9.4 0.3 collective-permute-start.3
  9.6 4.7 %collective-permute-done.1 = bf16[16,2176]{1,0:T(8,128)(2,1)S(1)} collective-permute-done((bf16[16,2176]{1,0:T(8,128)(2,1)}, bf16[16,2176]{1,0:T(8,128)(2,1)S(1)}, u32[]{:S(2)}, u32[]{:S(2)}) %collective-permute-start.1) | collective-permute-done | bytes 69664 | tf_op jit(solution)/shard_map/ppermute | solution.py:53
  14.4 0.0 collective-permute-done.2
  14.4 2.2 %collective-permute-start.8 = (bf16[48,2176]{1,0:T(8,128)(2,1)S(1)}, bf16[48,2176]{1,0:T(8,128)(2,1)S(1)}, u32[]{:S(2)}, u32[]{:S(2)}) collective-permute-start(bf16[48,2176]{1,0:T(8,128)(2,1)S(1)} %get-tuple-element.68), channel_id=1, source_target_pairs={{0,3},{1,2},{2,1},{3,0},{4,7},{5,6},{6,5},{7,4},{8,11},{9,10},{10,... | collective-permute-start | bytes 626696 | tf_op jit(solution)/shard_map/ppermute | solution.py:53
  16.7 0.2 collective-permute-start.6
  16.9 0.0 collective-permute-done.3
  16.9 0.3 collective-permute-start.4
  17.2 8.9 %collective-permute-done.4 = bf16[48,2176]{1,0:T(8,128)(2,1)S(1)} collective-permute-done((bf16[48,2176]{1,0:T(8,128)(2,1)S(1)}, bf16[48,2176]{1,0:T(8,128)(2,1)S(1)}, u32[]{:S(2)}, u32[]{:S(2)}) %collective-permute-start.4) | collective-permute-done | bytes 208928 | tf_op jit(solution)/shard_map/ppermute | solution.py:53
  26.2 0.8 collective-permute-done.6
  27.1 0.0 copy-start.2
  27.1 0.0 copy-start.3
  27.1 3.8 %teacher_pre.1.refs_0_ = bf16[256,3072]{1,0:T(8,128)(2,1)S(1)} custom-call(bf16[256,2176]{1,0:T(8,128)(2,1)S(1)} %constant_dynamic-update-slice_fusion.3.x_ref.refs_3_.refs_4_, bf16[1536,2048]{1,0:T(8,128)(2,1)S(1)} %bitcast.18, bf16[1536,2048]{1,0:T(8,128)(2,1)S(1)} %bitcast.21), custom_call_target="tpu_custom_call" | custom-call | flops 3221225472 | bytes 14155776 | tf_op jit(solution)/shard_map/teacher_pre/pallas_call | solution.py:147
  31.0 0.7 collective-permute-start.10
  31.7 2.4 %student_pre.1.refs_0_ = f32[256,1536]{1,0:T(8,128)S(1)} custom-call(bf16[256,2176]{1,0:T(8,128)(2,1)S(1)} %constant_dynamic-update-slice_fusion.3.x_ref.refs_3_.refs_4_, bf16[768,2048]{1,0:T(8,128)(2,1)S(1)} %copy-done.2, bf16[768,2048]{1,0:T(8,128)(2,1)S(1)} %copy-done.3), custom_call_target="tpu_custom_call" | custom-call | flops 1610612736 | bytes 7077888 | tf_op jit(solution)/shard_map/student_pre/pallas_call | solution.py:147
  34.2 0.1 collective-permute-start.9
  34.3 0.5 collective-permute-done.10.refs_1_
  34.8 2.9 %teacher_down.1 = (bf16[64,2048]{1,0:T(8,128)(2,1)S(1)}, bf16[64,2048]{1,0:T(8,128)(2,1)S(1)}, bf16[64,2048]{1,0:T(8,128)(2,1)S(1)}, bf16[64,2048]{1,0:T(8,128)(2,1)S(1)}) custom-call(bf16[256,3072]{1,0:T(8,128)(2,1)S(1)} %teacher_pre.1.refs_0_, bf16[256,3072]{1,0:T(8,128)(2,1)S(1)} %collective-permute-done.10.refs_1_, bf16[1536,2048]{1,0:T(8,128)(2,1)S(1)} %bitcast.15, ...), custom_call_target="tpu_custom_call" | custom-call | flops 1610612736 | bytes 10223616 | tf_op jit(solution)/shard_map/teacher_down/pallas_call | solution.py:212
  37.7 2.4 %student_down.1 = (bf16[256,768]{1,0:T(8,128)(2,1)S(1)}, bf16[64,2048]{1,0:T(8,128)(2,1)S(1)}, bf16[64,2048]{1,0:T(8,128)(2,1)S(1)}, bf16[64,2048]{1,0:T(8,128)(2,1)S(1)}, bf16[64,2048]{1,0:T(8,128)(2,1)S(1)}) custom-call(f32[256,1536]{1,0:T(8,128)S(1)} %student_pre.1.refs_0_, f32[256,1536]{1,0:T(8,128)S(1)} %collective-permute-done.9.refs_1_, ...), custom_call_target="tpu_custom_call" | custom-call | flops 805306368 | bytes 5111808 | tf_op jit(solution)/shard_map/student_down/pallas_call | solution.py:259
  40.1 1.3 %collective-permute-start.11 = (bf16[64,2048]{1,0:T(8,128)(2,1)S(1)}, bf16[64,2048]{1,0:T(8,128)(2,1)S(1)}, u32[]{:S(2)}, u32[]{:S(2)}) collective-permute-start(bf16[64,2048]{1,0:T(8,128)(2,1)S(1)} %get-tuple-element.37), channel_id=1, source_target_pairs={{0,1},{1,0},{2,3},{3,2},{4,5},{5,4},{6,7},{7,6},{8,9},{9,8},{10,11... | collective-permute-start | bytes 786440 | tf_op jit(solution)/shard_map/ppermute | solution.py:53
  41.3 0.4 collective-permute-start.12
  41.7 1.1 %collective-permute-start.13 = (bf16[64,2048]{1,0:T(8,128)(2,1)S(1)}, bf16[64,2048]{1,0:T(8,128)(2,1)S(1)}, u32[]{:S(2)}, u32[]{:S(2)}) collective-permute-start(bf16[64,2048]{1,0:T(8,128)(2,1)S(1)} %get-tuple-element.39), channel_id=1, source_target_pairs={{0,3},{1,2},{2,1},{3,0},{4,7},{5,6},{6,5},{7,4},{8,11},{9,10},{10,... | collective-permute-start | bytes 786440 | tf_op jit(solution)/shard_map/ppermute | solution.py:53
  42.8 4.9 %collective-permute-done.11 = bf16[64,2048]{1,0:T(8,128)(2,1)S(1)} collective-permute-done((bf16[64,2048]{1,0:T(8,128)(2,1)S(1)}, bf16[64,2048]{1,0:T(8,128)(2,1)S(1)}, u32[]{:S(2)}, u32[]{:S(2)}) %collective-permute-start.11) | collective-permute-done | bytes 262176 | tf_op jit(solution)/shard_map/ppermute | solution.py:53
  47.6 1.0 %collective-permute-done.12 = bf16[64,2048]{1,0:T(8,128)(2,1)S(1)} collective-permute-done((bf16[64,2048]{1,0:T(8,128)(2,1)S(1)}, bf16[64,2048]{1,0:T(8,128)(2,1)S(1)}, u32[]{:S(2)}, u32[]{:S(2)}) %collective-permute-start.12) | collective-permute-done | bytes 262176 | tf_op jit(solution)/shard_map/ppermute | solution.py:53
  48.6 5.5 %collective-permute-done.13 = bf16[64,2048]{1,0:T(8,128)(2,1)S(1)} collective-permute-done((bf16[64,2048]{1,0:T(8,128)(2,1)S(1)}, bf16[64,2048]{1,0:T(8,128)(2,1)S(1)}, u32[]{:S(2)}, u32[]{:S(2)}) %collective-permute-start.13) | collective-permute-done | bytes 262176 | tf_op jit(solution)/shard_map/ppermute | solution.py:53
  54.1 0.1 add_convert_fusion.2
  54.2 0.6 collective-permute-start.14
  54.8 0.1 collective-permute-start.16
  54.9 1.3 %collective-permute-start.18 = (bf16[16,2048]{1,0:T(8,128)(2,1)S(1)}, bf16[16,2048]{1,0:T(8,128)(2,1)S(1)}, u32[]{:S(2)}, u32[]{:S(2)}) collective-permute-start(bf16[16,2048]{1,0:T(8,128)(2,1)S(1)} %get-tuple-element.61), channel_id=1, source_target_pairs={{0,12},{1,13},{2,14},{3,15},{4,8},{5,9},{6,10},{7,11},{8,4},{9,5},... | collective-permute-start | bytes 196616 | tf_op jit(solution)/shard_map/ppermute | solution.py:53
  56.2 1.3 %collective-permute-start.17 = (bf16[16,2048]{1,0:T(8,128)(2,1)S(1)}, bf16[16,2048]{1,0:T(8,128)(2,1)S(1)}, u32[]{:S(2)}, u32[]{:S(2)}) collective-permute-start(bf16[16,2048]{1,0:T(8,128)(2,1)S(1)} %get-tuple-element.62), channel_id=1, source_target_pairs={{0,8},{1,9},{2,10},{3,11},{4,12},{5,13},{6,14},{7,15},{8,0},{9,1},... | collective-permute-start | bytes 196616 | tf_op jit(solution)/shard_map/ppermute | solution.py:53
  57.6 1.1 %collective-permute-start.15 = (bf16[64,2048]{1,0:T(8,128)(2,1)S(1)}, bf16[64,2048]{1,0:T(8,128)(2,1)S(1)}, u32[]{:S(2)}, u32[]{:S(2)}) collective-permute-start(bf16[64,2048]{1,0:T(8,128)(2,1)S(1)} %get-tuple-element.44.refs_6_), channel_id=1, source_target_pairs={{0,2},{1,3},{2,0},{3,1},{4,6},{5,7},{6,4},{7,5},{8,10},{9,11},{10,... | collective-permute-start | bytes 786440 | tf_op jit(solution)/shard_map/ppermute | solution.py:53
  58.6 1.9 %collective-permute-done.14 = bf16[64,2048]{1,0:T(8,128)(2,1)S(1)} collective-permute-done((bf16[64,2048]{1,0:T(8,128)(2,1)S(1)}, bf16[64,2048]{1,0:T(8,128)(2,1)S(1)}, u32[]{:S(2)}, u32[]{:S(2)}) %collective-permute-start.14) | collective-permute-done | bytes 262176 | tf_op jit(solution)/shard_map/ppermute | solution.py:53
  60.5 0.1 add_convert_fusion.1
  60.6 2.2 %collective-permute-done.15 = bf16[64,2048]{1,0:T(8,128)(2,1)S(1)} collective-permute-done((bf16[64,2048]{1,0:T(8,128)(2,1)S(1)}, bf16[64,2048]{1,0:T(8,128)(2,1)S(1)}, u32[]{:S(2)}, u32[]{:S(2)}) %collective-permute-start.15) | collective-permute-done | bytes 262176 | tf_op jit(solution)/shard_map/ppermute | solution.py:53
  62.8 0.1 add_convert_fusion
  62.9 1.3 %collective-permute-start.21 = (bf16[16,2048]{1,0:T(8,128)(2,1)S(1)}, bf16[16,2048]{1,0:T(8,128)(2,1)S(1)}, u32[]{:S(2)}, u32[]{:S(2)}) collective-permute-start(bf16[16,2048]{1,0:T(8,128)(2,1)S(1)} %multiply_convert_fusion), channel_id=1, source_target_pairs={{0,12},{1,13},{2,14},{3,15},{4,8},{5,9},{6,10},{7,11},{8,4},{9,5},... | collective-permute-start | bytes 196616 | tf_op jit(solution)/shard_map/ppermute | solution.py:53
  64.2 1.4 %collective-permute-start.20 = (bf16[16,2048]{1,0:T(8,128)(2,1)S(1)}, bf16[16,2048]{1,0:T(8,128)(2,1)S(1)}, u32[]{:S(2)}, u32[]{:S(2)}) collective-permute-start(bf16[16,2048]{1,0:T(8,128)(2,1)S(1)} %multiply_convert_fusion), channel_id=1, source_target_pairs={{0,8},{1,9},{2,10},{3,11},{4,12},{5,13},{6,14},{7,15},{8,0},{9,1},... | collective-permute-start | bytes 196616 | tf_op jit(solution)/shard_map/ppermute | solution.py:53
  65.6 1.0 %collective-permute-start.19 = (bf16[16,2048]{1,0:T(8,128)(2,1)S(1)}, bf16[16,2048]{1,0:T(8,128)(2,1)S(1)}, u32[]{:S(2)}, u32[]{:S(2)}) collective-permute-start(bf16[16,2048]{1,0:T(8,128)(2,1)S(1)} %multiply_convert_fusion), channel_id=1, source_target_pairs={{0,4},{1,5},{2,6},{3,7},{4,0},{5,1},{6,2},{7,3},{8,12},{9,13},{10,... | collective-permute-start | bytes 196616 | tf_op jit(solution)/shard_map/ppermute | solution.py:53
  66.6 1.5 %collective-permute-start.25 = (bf16[32,2048]{1,0:T(8,128)(2,1)S(1)}, bf16[32,2048]{1,0:T(8,128)(2,1)S(1)}, u32[]{:S(2)}, u32[]{:S(2)}) collective-permute-start(bf16[32,2048]{1,0:T(8,128)(2,1)S(1)} %get-tuple-element.56), channel_id=1, source_target_pairs={{0,2},{1,3},{2,0},{3,1},{4,6},{5,7},{6,4},{7,5},{8,10},{9,11},{10,... | collective-permute-start | bytes 393224 | tf_op jit(solution)/shard_map/ppermute | solution.py:53
  68.1 1.2 %collective-permute-done.20 = bf16[16,2048]{1,0:T(8,128)(2,1)S(1)} collective-permute-done((bf16[16,2048]{1,0:T(8,128)(2,1)S(1)}, bf16[16,2048]{1,0:T(8,128)(2,1)S(1)}, u32[]{:S(2)}, u32[]{:S(2)}) %collective-permute-start.20) | collective-permute-done | bytes 65568 | tf_op jit(solution)/shard_map/ppermute | solution.py:53
  69.4 1.2 %collective-permute-start.24 = (bf16[64,2048]{1,0:T(8,128)(2,1)S(1)}, bf16[64,2048]{1,0:T(8,128)(2,1)S(1)}, u32[]{:S(2)}, u32[]{:S(2)}) collective-permute-start(bf16[64,2048]{1,0:T(8,128)(2,1)S(1)} %pad_maximum_fusion.1), channel_id=1, source_target_pairs={{0,3},{1,2},{2,1},{3,0},{4,7},{5,6},{6,5},{7,4},{8,11},{9,10},{10,... | collective-permute-start | bytes 786440 | tf_op jit(solution)/shard_map/ppermute | solution.py:53
  70.6 1.0 %collective-permute-start.23 = (bf16[64,2048]{1,0:T(8,128)(2,1)S(1)}, bf16[64,2048]{1,0:T(8,128)(2,1)S(1)}, u32[]{:S(2)}, u32[]{:S(2)}) collective-permute-start(bf16[64,2048]{1,0:T(8,128)(2,1)S(1)} %pad_maximum_fusion.1), channel_id=1, source_target_pairs={{0,2},{1,3},{2,0},{3,1},{4,6},{5,7},{6,4},{7,5},{8,10},{9,11},{10,... | collective-permute-start | bytes 786440 | tf_op jit(solution)/shard_map/ppermute | solution.py:53
  71.5 0.5 collective-permute-start.22
  72.1 0.4 collective-permute-start.26
  72.6 1.7 %collective-permute-start.28 = (bf16[16,2048]{1,0:T(8,128)(2,1)S(1)}, bf16[16,2048]{1,0:T(8,128)(2,1)S(1)}, u32[]{:S(2)}, u32[]{:S(2)}) collective-permute-start(bf16[16,2048]{1,0:T(8,128)(2,1)S(1)} %get-tuple-element.66), channel_id=1, source_target_pairs={{0,8},{1,9},{2,10},{3,11},{4,12},{5,13},{6,14},{7,15},{8,0},{9,1},... | collective-permute-start | bytes 196616 | tf_op jit(solution)/shard_map/ppermute | solution.py:53
  74.3 1.5 %collective-permute-done.24 = bf16[64,2048]{1,0:T(8,128)(2,1)S(1)} collective-permute-done((bf16[64,2048]{1,0:T(8,128)(2,1)S(1)}, bf16[64,2048]{1,0:T(8,128)(2,1)S(1)}, u32[]{:S(2)}, u32[]{:S(2)}) %collective-permute-start.24) | collective-permute-done | bytes 262176 | tf_op jit(solution)/shard_map/ppermute | solution.py:53
  75.7 1.8 %collective-permute-start.29 = (bf16[16,2048]{1,0:T(8,128)(2,1)S(1)}, bf16[16,2048]{1,0:T(8,128)(2,1)S(1)}, u32[]{:S(2)}, u32[]{:S(2)}) collective-permute-start(bf16[16,2048]{1,0:T(8,128)(2,1)S(1)} %get-tuple-element.67), channel_id=1, source_target_pairs={{0,12},{1,13},{2,14},{3,15},{4,8},{5,9},{6,10},{7,11},{8,4},{9,5},... | collective-permute-start | bytes 196616 | tf_op jit(solution)/shard_map/ppermute | solution.py:53
  77.6 6.6 %collective-permute-done.23 = bf16[64,2048]{1,0:T(8,128)(2,1)S(1)} collective-permute-done((bf16[64,2048]{1,0:T(8,128)(2,1)S(1)}, bf16[64,2048]{1,0:T(8,128)(2,1)S(1)}, u32[]{:S(2)}, u32[]{:S(2)}) %collective-permute-start.23) | collective-permute-done | bytes 262176 | tf_op jit(solution)/shard_map/ppermute | solution.py:53
  84.2 0.1 pad_maximum_fusion.delta_ref
  84.3 1.5 %hidden_grad.1.refs_2_ = bf16[256,768]{1,0:T(8,128)(2,1)S(1)} custom-call(bf16[256,2048]{1,0:T(8,128)(2,1)S(1)} %pad_maximum_fusion.delta_ref, bf16[768,2048]{1,0:T(8,128)(2,1)S(1)} %copy-done), custom_call_target="tpu_custom_call" | custom-call | flops 805306368 | bytes 4194304 | tf_op jit(solution)/shard_map/hidden_grad/pallas_call | solution.py:284
  85.8 2.2 %collective-permute-start.30 = (bf16[256,768]{1,0:T(8,128)(2,1)S(1)}, bf16[256,768]{1,0:T(8,128)(2,1)S(1)}, u32[]{:S(2)}, u32[]{:S(2)}) collective-permute-start(bf16[256,768]{1,0:T(8,128)(2,1)S(1)} %hidden_grad.1.refs_2_), channel_id=1, source_target_pairs={{0,16},{16,0},{1,17},{17,1},{2,18},{18,2},{3,19},{19,3},{4,20},{20... | collective-permute-start | bytes 1179656 | tf_op jit(solution)/shard_map/ppermute | solution.py:78
  88.1 2.4 %grad_down.1 = bf16[768,2048]{1,0:T(8,128)(2,1)} custom-call(bf16[256,768]{1,0:T(8,128)(2,1)S(1)} %get-tuple-element.55.hidden_ref, bf16[256,2048]{1,0:T(8,128)(2,1)S(1)} %pad_maximum_fusion.delta_ref), custom_call_target="tpu_custom_call" | custom-call | flops 805306368 | bytes 4194304 | tf_op jit(solution)/shard_map/grad_down/pallas_call | solution.py:306
  90.5 0.7 add_convert_fusion.5
  91.2 4.0 %grad_gate_up.1 = (bf16[768,2048]{1,0:T(8,128)(2,1)}, bf16[768,2048]{1,0:T(8,128)(2,1)}) custom-call(f32[256,1536]{1,0:T(8,128)S(1)} %student_pre.1.refs_0_, f32[256,1536]{1,0:T(8,128)S(1)} %collective-permute-done.9.refs_1_, bf16[256,768]{1,0:T(8,128)(2,1)S(1)} %hidden_grad.1.refs_2_, bf16[256,768]{1,0:T(8,128)(2,1)S(1)} %collective-permute-done.30.refs_3_, ...), custom_call_target="tpu_custom_call" | custom-call | flops 1610612736 | bytes 7340032 | tf_op jit(solution)/shard_map/grad_gate_up/pallas_call | solution.py:338
  (50 shorter events, 0.4 us)
Async XLA Ops:
  0.6 26.4 %slice-start = ((s8[6291456]{0:T(1024)(128)(4,1)}), s8[2097152]{0:T(1024)(128)(4,1)S(1)}, s32[]{:S(2)}) async-start(s8[6291456]{0:T(1024)(128)(4,1)} %bitcast.16), calls=%async_computation | async-start | bytes 4194304
  0.6 26.4 %slice-start.2 = ((s8[6291456]{0:T(1024)(128)(4,1)}), s8[4194304]{0:T(1024)(128)(4,1)S(1)}, s32[]{:S(2)}) async-start(s8[6291456]{0:T(1024)(128)(4,1)} %bitcast.19), calls=%async_computation.2 | async-start | bytes 8388608
  2.3 4.6 %copy-start.4 = (bf16[16,2176]{1,0:T(8,128)(2,1)S(1)}, bf16[16,2176]{1,0:T(8,128)(2,1)}, u32[]{:S(2)}) copy-start(bf16[16,2176]{1,0:T(8,128)(2,1)} %payload.1) | copy-start | bytes 208900
  2.4 24.7 %slice-start.1 = ((s8[6291456]{0:T(1024)(128)(4,1)}), s8[4194304]{0:T(1024)(128)(4,1)S(1)}, s32[]{:S(2)}) async-start(s8[6291456]{0:T(1024)(128)(4,1)} %bitcast.16), calls=%async_computation.1 | async-start | bytes 8388608
  2.4 24.7 %slice-start.3 = ((s8[6291456]{0:T(1024)(128)(4,1)}), s8[2097152]{0:T(1024)(128)(4,1)S(1)}, s32[]{:S(2)}) async-start(s8[6291456]{0:T(1024)(128)(4,1)} %bitcast.19), calls=%async_computation.3 | async-start | bytes 4194304
  2.4 4.5 %collective-permute-start = (bf16[16,2176]{1,0:T(8,128)(2,1)}, bf16[16,2176]{1,0:T(8,128)(2,1)S(1)}, u32[]{:S(2)}, u32[]{:S(2)}) collective-permute-start(bf16[16,2176]{1,0:T(8,128)(2,1)} %payload.1), channel_id=1, source_target_pairs={{0,4},{1,5},{2,6},{3,7},{4,0},{5,1},{6,2},{7,3},{8,12},{9,13},{10,... | collective-permute-start | bytes 208904 | tf_op jit(solution)/shard_map/ppermute | solution.py:53
  4.6 9.8 %collective-permute-start.2 = (bf16[16,2176]{1,0:T(8,128)(2,1)}, bf16[16,2176]{1,0:T(8,128)(2,1)S(1)}, u32[]{:S(2)}, u32[]{:S(2)}) collective-permute-start(bf16[16,2176]{1,0:T(8,128)(2,1)} %payload.1), channel_id=1, source_target_pairs={{0,12},{1,13},{2,14},{3,15},{4,8},{5,9},{6,10},{7,11},{8,4},{9,5},... | collective-permute-start | bytes 208904 | tf_op jit(solution)/shard_map/ppermute | solution.py:53
  6.8 7.6 %collective-permute-start.1 = (bf16[16,2176]{1,0:T(8,128)(2,1)}, bf16[16,2176]{1,0:T(8,128)(2,1)S(1)}, u32[]{:S(2)}, u32[]{:S(2)}) collective-permute-start(bf16[16,2176]{1,0:T(8,128)(2,1)} %payload.1), channel_id=1, source_target_pairs={{0,8},{1,9},{2,10},{3,11},{4,12},{5,13},{6,14},{7,15},{8,0},{9,1},... | collective-permute-start | bytes 208904 | tf_op jit(solution)/shard_map/ppermute | solution.py:53
  6.9 20.1 %collective-permute-start.7 = (bf16[16,2176]{1,0:T(8,128)(2,1)S(1)}, bf16[16,2176]{1,0:T(8,128)(2,1)S(1)}, u32[]{:S(2)}, u32[]{:S(2)}) collective-permute-start(bf16[16,2176]{1,0:T(8,128)(2,1)S(1)} %copy-done.4), channel_id=1, source_target_pairs={{0,3},{1,2},{2,1},{3,0},{4,7},{5,6},{6,5},{7,4},{8,11},{9,10},{10,... | collective-permute-start | bytes 208904 | tf_op jit(solution)/shard_map/ppermute | solution.py:53
  9.1 17.0 %collective-permute-start.5 = (bf16[16,2176]{1,0:T(8,128)(2,1)S(1)}, bf16[16,2176]{1,0:T(8,128)(2,1)S(1)}, u32[]{:S(2)}, u32[]{:S(2)}) collective-permute-start(bf16[16,2176]{1,0:T(8,128)(2,1)S(1)} %copy-done.4), channel_id=1, source_target_pairs={{0,2},{1,3},{2,0},{3,1},{4,6},{5,7},{6,4},{7,5},{8,10},{9,11},{10,... | collective-permute-start | bytes 208904 | tf_op jit(solution)/shard_map/ppermute | solution.py:53
  9.4 7.5 %collective-permute-start.3 = (bf16[16,2176]{1,0:T(8,128)(2,1)S(1)}, bf16[16,2176]{1,0:T(8,128)(2,1)S(1)}, u32[]{:S(2)}, u32[]{:S(2)}) collective-permute-start(bf16[16,2176]{1,0:T(8,128)(2,1)S(1)} %copy-done.4), channel_id=1, source_target_pairs={{0,1},{1,0},{2,3},{3,2},{4,5},{5,4},{6,7},{7,6},{8,9},{9,8},{10,11... | collective-permute-start | bytes 208904 | tf_op jit(solution)/shard_map/ppermute | solution.py:53
  14.4 12.6 %collective-permute-start.8 = (bf16[48,2176]{1,0:T(8,128)(2,1)S(1)}, bf16[48,2176]{1,0:T(8,128)(2,1)S(1)}, u32[]{:S(2)}, u32[]{:S(2)}) collective-permute-start(bf16[48,2176]{1,0:T(8,128)(2,1)S(1)} %get-tuple-element.68), channel_id=1, source_target_pairs={{0,3},{1,2},{2,1},{3,0},{4,7},{5,6},{6,5},{7,4},{8,11},{9,10},{10,... | collective-permute-start | bytes 626696 | tf_op jit(solution)/shard_map/ppermute | solution.py:53
  16.7 10.3 %collective-permute-start.6 = (bf16[48,2176]{1,0:T(8,128)(2,1)S(1)}, bf16[48,2176]{1,0:T(8,128)(2,1)S(1)}, u32[]{:S(2)}, u32[]{:S(2)}) collective-permute-start(bf16[48,2176]{1,0:T(8,128)(2,1)S(1)} %get-tuple-element.68), channel_id=1, source_target_pairs={{0,2},{1,3},{2,0},{3,1},{4,6},{5,7},{6,4},{7,5},{8,10},{9,11},{10,... | collective-permute-start | bytes 626696 | tf_op jit(solution)/shard_map/ppermute | solution.py:53
  16.9 9.2 %collective-permute-start.4 = (bf16[48,2176]{1,0:T(8,128)(2,1)S(1)}, bf16[48,2176]{1,0:T(8,128)(2,1)S(1)}, u32[]{:S(2)}, u32[]{:S(2)}) collective-permute-start(bf16[48,2176]{1,0:T(8,128)(2,1)S(1)} %get-tuple-element.68), channel_id=1, source_target_pairs={{0,1},{1,0},{2,3},{3,2},{4,5},{5,4},{6,7},{7,6},{8,9},{9,8},{10,11... | collective-permute-start | bytes 626696 | tf_op jit(solution)/shard_map/ppermute | solution.py:53
  27.1 4.6 %copy-start.2 = (bf16[768,2048]{1,0:T(8,128)(2,1)S(1)}, bf16[768,2048]{1,0:T(8,128)(2,1)}, u32[]{:S(2)}) copy-start(bf16[768,2048]{1,0:T(8,128)(2,1)} %gate_ref.1) | copy-start | bytes 9437188
  27.1 4.6 %copy-start.3 = (bf16[768,2048]{1,0:T(8,128)(2,1)S(1)}, bf16[768,2048]{1,0:T(8,128)(2,1)}, u32[]{:S(2)}) copy-start(bf16[768,2048]{1,0:T(8,128)(2,1)} %up_ref.1) | copy-start | bytes 9437188
  31.0 3.8 %collective-permute-start.10 = (bf16[256,3072]{1,0:T(8,128)(2,1)S(1)}, bf16[256,3072]{1,0:T(8,128)(2,1)S(1)}, u32[]{:S(2)}, u32[]{:S(2)}) collective-permute-start(bf16[256,3072]{1,0:T(8,128)(2,1)S(1)} %teacher_pre.1.refs_0_), channel_id=1, source_target_pairs={{0,16},{16,0},{1,17},{17,1},{2,18},{18,2},{3,19},{19,3},{4,20},{20... | collective-permute-start | bytes 4718600 | tf_op jit(solution)/shard_map/ppermute | solution.py:78
  31.7 3.0 %copy-start.1 = (bf16[1,1536,2048]{2,1,0:T(8,128)(2,1)S(1)}, bf16[1,1536,2048]{2,1,0:T(8,128)(2,1)}, u32[]{:S(2)}) copy-start(bf16[1,1536,2048]{2,1,0:T(8,128)(2,1)} %param.14) | copy-start | bytes 18874372
  34.2 3.5 %collective-permute-start.9 = (f32[256,1536]{1,0:T(8,128)S(1)}, f32[256,1536]{1,0:T(8,128)S(1)}, u32[]{:S(2)}, u32[]{:S(2)}) collective-permute-start(f32[256,1536]{1,0:T(8,128)S(1)} %student_pre.1.refs_0_), channel_id=1, source_target_pairs={{0,16},{16,0},{1,17},{17,1},{2,18},{18,2},{3,19},{19,3},{4,20},{20... | collective-permute-start | bytes 4718600 | tf_op jit(solution)/shard_map/ppermute | solution.py:78
  34.8 2.9 %copy-start = (bf16[768,2048]{1,0:T(8,128)(2,1)S(1)}, bf16[768,2048]{1,0:T(8,128)(2,1)}, u32[]{:S(2)}) copy-start(bf16[768,2048]{1,0:T(8,128)(2,1)} %down_ref.1) | copy-start | bytes 9437188
  40.1 7.6 %collective-permute-start.11 = (bf16[64,2048]{1,0:T(8,128)(2,1)S(1)}, bf16[64,2048]{1,0:T(8,128)(2,1)S(1)}, u32[]{:S(2)}, u32[]{:S(2)}) collective-permute-start(bf16[64,2048]{1,0:T(8,128)(2,1)S(1)} %get-tuple-element.37), channel_id=1, source_target_pairs={{0,1},{1,0},{2,3},{3,2},{4,5},{5,4},{6,7},{7,6},{8,9},{9,8},{10,11... | collective-permute-start | bytes 786440 | tf_op jit(solution)/shard_map/ppermute | solution.py:53
  41.3 7.3 %collective-permute-start.12 = (bf16[64,2048]{1,0:T(8,128)(2,1)S(1)}, bf16[64,2048]{1,0:T(8,128)(2,1)S(1)}, u32[]{:S(2)}, u32[]{:S(2)}) collective-permute-start(bf16[64,2048]{1,0:T(8,128)(2,1)S(1)} %get-tuple-element.38), channel_id=1, source_target_pairs={{0,2},{1,3},{2,0},{3,1},{4,6},{5,7},{6,4},{7,5},{8,10},{9,11},{10,... | collective-permute-start | bytes 786440 | tf_op jit(solution)/shard_map/ppermute | solution.py:53
  41.7 12.4 %collective-permute-start.13 = (bf16[64,2048]{1,0:T(8,128)(2,1)S(1)}, bf16[64,2048]{1,0:T(8,128)(2,1)S(1)}, u32[]{:S(2)}, u32[]{:S(2)}) collective-permute-start(bf16[64,2048]{1,0:T(8,128)(2,1)S(1)} %get-tuple-element.39), channel_id=1, source_target_pairs={{0,3},{1,2},{2,1},{3,0},{4,7},{5,6},{6,5},{7,4},{8,11},{9,10},{10,... | collective-permute-start | bytes 786440 | tf_op jit(solution)/shard_map/ppermute | solution.py:53
  54.2 6.3 %collective-permute-start.14 = (bf16[64,2048]{1,0:T(8,128)(2,1)S(1)}, bf16[64,2048]{1,0:T(8,128)(2,1)S(1)}, u32[]{:S(2)}, u32[]{:S(2)}) collective-permute-start(bf16[64,2048]{1,0:T(8,128)(2,1)S(1)} %get-tuple-element.42.refs_4_), channel_id=1, source_target_pairs={{0,1},{1,0},{2,3},{3,2},{4,5},{5,4},{6,7},{7,6},{8,9},{9,8},{10,11... | collective-permute-start | bytes 786440 | tf_op jit(solution)/shard_map/ppermute | solution.py:53
  54.8 8.0 %collective-permute-start.16 = (bf16[16,2048]{1,0:T(8,128)(2,1)S(1)}, bf16[16,2048]{1,0:T(8,128)(2,1)S(1)}, u32[]{:S(2)}, u32[]{:S(2)}) collective-permute-start(bf16[16,2048]{1,0:T(8,128)(2,1)S(1)} %get-tuple-element.60), channel_id=1, source_target_pairs={{0,4},{1,5},{2,6},{3,7},{4,0},{5,1},{6,2},{7,3},{8,12},{9,13},{10,... | collective-permute-start | bytes 196616 | tf_op jit(solution)/shard_map/ppermute | solution.py:53
  54.9 7.9 %collective-permute-start.18 = (bf16[16,2048]{1,0:T(8,128)(2,1)S(1)}, bf16[16,2048]{1,0:T(8,128)(2,1)S(1)}, u32[]{:S(2)}, u32[]{:S(2)}) collective-permute-start(bf16[16,2048]{1,0:T(8,128)(2,1)S(1)} %get-tuple-element.61), channel_id=1, source_target_pairs={{0,12},{1,13},{2,14},{3,15},{4,8},{5,9},{6,10},{7,11},{8,4},{9,5},... | collective-permute-start | bytes 196616 | tf_op jit(solution)/shard_map/ppermute | solution.py:53
  56.2 6.7 %collective-permute-start.17 = (bf16[16,2048]{1,0:T(8,128)(2,1)S(1)}, bf16[16,2048]{1,0:T(8,128)(2,1)S(1)}, u32[]{:S(2)}, u32[]{:S(2)}) collective-permute-start(bf16[16,2048]{1,0:T(8,128)(2,1)S(1)} %get-tuple-element.62), channel_id=1, source_target_pairs={{0,8},{1,9},{2,10},{3,11},{4,12},{5,13},{6,14},{7,15},{8,0},{9,1},... | collective-permute-start | bytes 196616 | tf_op jit(solution)/shard_map/ppermute | solution.py:53
  57.6 5.2 %collective-permute-start.15 = (bf16[64,2048]{1,0:T(8,128)(2,1)S(1)}, bf16[64,2048]{1,0:T(8,128)(2,1)S(1)}, u32[]{:S(2)}, u32[]{:S(2)}) collective-permute-start(bf16[64,2048]{1,0:T(8,128)(2,1)S(1)} %get-tuple-element.44.refs_6_), channel_id=1, source_target_pairs={{0,2},{1,3},{2,0},{3,1},{4,6},{5,7},{6,4},{7,5},{8,10},{9,11},{10,... | collective-permute-start | bytes 786440 | tf_op jit(solution)/shard_map/ppermute | solution.py:53
  62.9 5.2 %collective-permute-start.21 = (bf16[16,2048]{1,0:T(8,128)(2,1)S(1)}, bf16[16,2048]{1,0:T(8,128)(2,1)S(1)}, u32[]{:S(2)}, u32[]{:S(2)}) collective-permute-start(bf16[16,2048]{1,0:T(8,128)(2,1)S(1)} %multiply_convert_fusion), channel_id=1, source_target_pairs={{0,12},{1,13},{2,14},{3,15},{4,8},{5,9},{6,10},{7,11},{8,4},{9,5},... | collective-permute-start | bytes 196616 | tf_op jit(solution)/shard_map/ppermute | solution.py:53
  64.2 5.1 %collective-permute-start.20 = (bf16[16,2048]{1,0:T(8,128)(2,1)S(1)}, bf16[16,2048]{1,0:T(8,128)(2,1)S(1)}, u32[]{:S(2)}, u32[]{:S(2)}) collective-permute-start(bf16[16,2048]{1,0:T(8,128)(2,1)S(1)} %multiply_convert_fusion), channel_id=1, source_target_pairs={{0,8},{1,9},{2,10},{3,11},{4,12},{5,13},{6,14},{7,15},{8,0},{9,1},... | collective-permute-start | bytes 196616 | tf_op jit(solution)/shard_map/ppermute | solution.py:53
  65.6 3.8 %collective-permute-start.19 = (bf16[16,2048]{1,0:T(8,128)(2,1)S(1)}, bf16[16,2048]{1,0:T(8,128)(2,1)S(1)}, u32[]{:S(2)}, u32[]{:S(2)}) collective-permute-start(bf16[16,2048]{1,0:T(8,128)(2,1)S(1)} %multiply_convert_fusion), channel_id=1, source_target_pairs={{0,4},{1,5},{2,6},{3,7},{4,0},{5,1},{6,2},{7,3},{8,12},{9,13},{10,... | collective-permute-start | bytes 196616 | tf_op jit(solution)/shard_map/ppermute | solution.py:53
  66.6 5.5 %collective-permute-start.25 = (bf16[32,2048]{1,0:T(8,128)(2,1)S(1)}, bf16[32,2048]{1,0:T(8,128)(2,1)S(1)}, u32[]{:S(2)}, u32[]{:S(2)}) collective-permute-start(bf16[32,2048]{1,0:T(8,128)(2,1)S(1)} %get-tuple-element.56), channel_id=1, source_target_pairs={{0,2},{1,3},{2,0},{3,1},{4,6},{5,7},{6,4},{7,5},{8,10},{9,11},{10,... | collective-permute-start | bytes 393224 | tf_op jit(solution)/shard_map/ppermute | solution.py:53
  68.1 4.4 %collective-permute-start.27 = (bf16[32,2048]{1,0:T(8,128)(2,1)S(1)}, bf16[32,2048]{1,0:T(8,128)(2,1)S(1)}, u32[]{:S(2)}, u32[]{:S(2)}) collective-permute-start(bf16[32,2048]{1,0:T(8,128)(2,1)S(1)} %get-tuple-element.74), channel_id=1, source_target_pairs={{0,1},{1,0},{2,3},{3,2},{4,5},{5,4},{6,7},{7,6},{8,9},{9,8},{10,11... | collective-permute-start | bytes 393224 | tf_op jit(solution)/shard_map/ppermute | solution.py:53
  69.4 6.3 %collective-permute-start.24 = (bf16[64,2048]{1,0:T(8,128)(2,1)S(1)}, bf16[64,2048]{1,0:T(8,128)(2,1)S(1)}, u32[]{:S(2)}, u32[]{:S(2)}) collective-permute-start(bf16[64,2048]{1,0:T(8,128)(2,1)S(1)} %pad_maximum_fusion.1), channel_id=1, source_target_pairs={{0,3},{1,2},{2,1},{3,0},{4,7},{5,6},{6,5},{7,4},{8,11},{9,10},{10,... | collective-permute-start | bytes 786440 | tf_op jit(solution)/shard_map/ppermute | solution.py:53
  70.6 13.6 %collective-permute-start.23 = (bf16[64,2048]{1,0:T(8,128)(2,1)S(1)}, bf16[64,2048]{1,0:T(8,128)(2,1)S(1)}, u32[]{:S(2)}, u32[]{:S(2)}) collective-permute-start(bf16[64,2048]{1,0:T(8,128)(2,1)S(1)} %pad_maximum_fusion.1), channel_id=1, source_target_pairs={{0,2},{1,3},{2,0},{3,1},{4,6},{5,7},{6,4},{7,5},{8,10},{9,11},{10,... | collective-permute-start | bytes 786440 | tf_op jit(solution)/shard_map/ppermute | solution.py:53
  71.5 12.6 %collective-permute-start.22 = (bf16[64,2048]{1,0:T(8,128)(2,1)S(1)}, bf16[64,2048]{1,0:T(8,128)(2,1)S(1)}, u32[]{:S(2)}, u32[]{:S(2)}) collective-permute-start(bf16[64,2048]{1,0:T(8,128)(2,1)S(1)} %pad_maximum_fusion.1), channel_id=1, source_target_pairs={{0,1},{1,0},{2,3},{3,2},{4,5},{5,4},{6,7},{7,6},{8,9},{9,8},{10,11... | collective-permute-start | bytes 786440 | tf_op jit(solution)/shard_map/ppermute | solution.py:53
  72.1 18.4 %collective-permute-start.26 = (bf16[16,2048]{1,0:T(8,128)(2,1)S(1)}, bf16[16,2048]{1,0:T(8,128)(2,1)S(1)}, u32[]{:S(2)}, u32[]{:S(2)}) collective-permute-start(bf16[16,2048]{1,0:T(8,128)(2,1)S(1)} %get-tuple-element.65), channel_id=1, source_target_pairs={{0,4},{1,5},{2,6},{3,7},{4,0},{5,1},{6,2},{7,3},{8,12},{9,13},{10,... | collective-permute-start | bytes 196616 | tf_op jit(solution)/shard_map/ppermute | solution.py:53
  72.6 17.9 %collective-permute-start.28 = (bf16[16,2048]{1,0:T(8,128)(2,1)S(1)}, bf16[16,2048]{1,0:T(8,128)(2,1)S(1)}, u32[]{:S(2)}, u32[]{:S(2)}) collective-permute-start(bf16[16,2048]{1,0:T(8,128)(2,1)S(1)} %get-tuple-element.66), channel_id=1, source_target_pairs={{0,8},{1,9},{2,10},{3,11},{4,12},{5,13},{6,14},{7,15},{8,0},{9,1},... | collective-permute-start | bytes 196616 | tf_op jit(solution)/shard_map/ppermute | solution.py:53
  75.7 14.8 %collective-permute-start.29 = (bf16[16,2048]{1,0:T(8,128)(2,1)S(1)}, bf16[16,2048]{1,0:T(8,128)(2,1)S(1)}, u32[]{:S(2)}, u32[]{:S(2)}) collective-permute-start(bf16[16,2048]{1,0:T(8,128)(2,1)S(1)} %get-tuple-element.67), channel_id=1, source_target_pairs={{0,12},{1,13},{2,14},{3,15},{4,8},{5,9},{6,10},{7,11},{8,4},{9,5},... | collective-permute-start | bytes 196616 | tf_op jit(solution)/shard_map/ppermute | solution.py:53
  85.8 5.3 %collective-permute-start.30 = (bf16[256,768]{1,0:T(8,128)(2,1)S(1)}, bf16[256,768]{1,0:T(8,128)(2,1)S(1)}, u32[]{:S(2)}, u32[]{:S(2)}) collective-permute-start(bf16[256,768]{1,0:T(8,128)(2,1)S(1)} %hidden_grad.1.refs_2_), channel_id=1, source_target_pairs={{0,16},{16,0},{1,17},{17,1},{2,18},{18,2},{3,19},{19,3},{4,20},{20... | collective-permute-start | bytes 1179656 | tf_op jit(solution)/shard_map/ppermute | solution.py:78

commit v3 on v2

--- a/solution.py
+++ b/solution.py
@@ -11,6 +11,8 @@
 BF16 = jnp.bfloat16
 F32 = jnp.float32
 MIB = 1024 * 1024
+IN_VMEM = pl.BlockSpec(memory_space=pltpu.VMEM)
+IN_HBM = pl.BlockSpec(memory_space=pltpu.HBM)
 LANES = 128
 TEACHER_BLOCK = 768
 STUDENT_BLOCK = 256
@@ -35,7 +37,7 @@
 
 def params(rows):
     limit = min(18 * max(1, rows // 256), 56) * MIB
-    return pltpu.CompilerParams(vmem_limit_bytes=limit, dimension_semantics=("arbitrary",))
+    return pltpu.CompilerParams(vmem_limit_bytes=limit)
 
 
 def cost(flops, nbytes):
@@ -54,6 +56,9 @@
 
     def gather_far(self, value):
         return [self.swap(value, 0, k) for k in range(1, self.outer)]
+
+    def gather_far_last(self, value):
+        return [self.swap(value, 0, k) for k in range(self.outer - 1, 0, -1)][::-1]
 
     def gather_near(self, value):
         return [self.swap(value, k, 0) for k in range(1, self.inner)]
@@ -109,7 +114,7 @@
     extra = -(-2 * owners // LANES) * LANES
     return pl.pallas_call(
         functools.partial(payload_kernel, owners),
-        in_specs=[pl.BlockSpec(memory_space=pltpu.HBM)] * 3,
+        in_specs=[IN_HBM] * 3,
         out_shape=jax.ShapeDtypeStruct((rows, columns + extra), BF16),
         scratch_shapes=[
             pltpu.VMEM(route_ids.shape[::-1], jnp.int32),
@@ -135,24 +140,22 @@
     )(value)
 
 
-def pre_kernel(x_ref, gate_ref, up_ref, out_ref):
-    block = gate_ref.shape[0]
-    out_ref[:, :block] = against(x_ref[...], gate_ref[...]).astype(out_ref.dtype)
-    out_ref[:, block:] = against(x_ref[...], up_ref[...]).astype(out_ref.dtype)
+def pre_kernel(block, x_ref, gate_ref, up_ref, out_ref):
+    columns = gate_ref.shape[1]
+    for i in range(gate_ref.shape[0] // block):
+        here = slice(i * block, (i + 1) * block)
+        for k, mat_ref in enumerate((gate_ref, up_ref)):
+            there = slice((2 * i + k) * block, (2 * i + k + 1) * block)
+            out_ref[:, there] = against(x_ref[:, :columns], mat_ref[here, :]).astype(out_ref.dtype)
 
 
 def pre_parts(x, gate, up, dtype, most, name):
     hidden, columns = gate.shape
     rows, block = x.shape[0], block_of(hidden, most)
     return pl.pallas_call(
-        pre_kernel,
-        grid=(hidden // block,),
-        in_specs=[
-            pl.BlockSpec((rows, columns), lambda i: (0, 0)),
-            pl.BlockSpec((block, columns), lambda i: (i, 0)),
-            pl.BlockSpec((block, columns), lambda i: (i, 0)),
-        ],
-        out_specs=pl.BlockSpec((rows, 2 * block), lambda i: (0, i)),
+        functools.partial(pre_kernel, block),
+        in_specs=[IN_VMEM] * 3,
+        out_specs=IN_VMEM,
         out_shape=jax.ShapeDtypeStruct((rows, 2 * hidden), dtype),
         compiler_params=params(rows),
         cost_estimate=cost(4 * rows * hidden * columns, 4 * hidden * columns + 4 * rows * hidden),
@@ -160,12 +163,17 @@
     )(x, gate, up)
 
 
-def added(refs):
-    total = refs[0][...].astype(F32)
+def added(refs, block, i):
+    here = slice(2 * i * block, 2 * (i + 1) * block)
+    total = refs[0][:, here].astype(F32)
     for ref in refs[1:]:
-        total = total + ref[...].astype(F32)
-    half = total.shape[1] // 2
-    return total[:, :half], total[:, half:]
+        total = total + ref[:, here].astype(F32)
+    return total[:, :block], total[:, block:]
+
+
+def activated(refs, block, i):
+    gate, up = added(refs, block, i)
+    return (gate * jax.nn.sigmoid(gate) * up).astype(BF16)
 
 
 def teacher_places(rows, inner):
@@ -178,46 +186,32 @@
             yield slice(here, here + length), near, part, slice(there, there + length)
 
 
-def teacher_kernel(parts, inner, owners, *refs):
+def teacher_kernel(parts, inner, owners, block, *refs):
     pre_refs, down_ref, table_ref = refs[:parts], refs[parts], refs[parts + 1]
     out_refs, total = refs[parts + 2 : parts + 6], refs[-1]
-    step = pl.program_id(0)
-    gate, up = added(pre_refs)
-    hidden = (gate * jax.nn.sigmoid(gate) * up).astype(BF16)
-    term = plain(hidden, down_ref[...])
-
-    @pl.when(step == 0)
-    def _():
-        total[...] = term
-
-    @pl.when(step > 0)
-    def _():
-        total[...] += term
-
-    @pl.when(step == pl.num_programs(0) - 1)
-    def _():
-        me = lax.axis_index("wide")
-        table = table_ref[...].astype(F32)
-        lane = lax.broadcasted_iota(jnp.int32, table.shape, 1)
-        mine = (lane == me) | (lane == me + owners)
-        weight = jnp.sum(jnp.where(mine, table, 0.0), axis=1, keepdims=True)
-        for piece, _, part, place in teacher_places(total.shape[0], inner):
-            out_refs[part][place, :] = (total[piece, :] * weight[piece, :]).astype(BF16)
+    extra = table_ref.shape[1] - down_ref.shape[1]
+    for i in range(down_ref.shape[0] // block):
+        term = plain(activated(pre_refs, block, i), down_ref[i * block : (i + 1) * block, :])
+        if i == 0:
+            total[...] = term
+        else:
+            total[...] += term
+    me = lax.axis_index("wide")
+    table = table_ref[:, down_ref.shape[1] :].astype(F32)
+    lane = lax.broadcasted_iota(jnp.int32, (table.shape[0], extra), 1)
+    mine = (lane == me) | (lane == me + owners)
+    weight = jnp.sum(jnp.where(mine, table, 0.0), axis=1, keepdims=True)
+    for piece, _, part, place in teacher_places(total.shape[0], inner):
+        out_refs[part][place, :] = (total[piece, :] * weight[piece, :]).astype(BF16)
 
 
 def teacher_parts(pres, down, payload, inner, owners):
     hidden, columns = down.shape
     rows, block = payload.shape[0], block_of(hidden, TEACHER_BLOCK)
-    extra = payload.shape[1] - columns
-    return pl.pallas_call(
-        functools.partial(teacher_kernel, len(pres), inner, owners),
-        grid=(hidden // block,),
-        in_specs=[pl.BlockSpec((rows, 2 * block), lambda i: (0, i)) for _ in pres]
-        + [
-            pl.BlockSpec((block, columns), lambda i: (i, 0)),
-            pl.BlockSpec((rows, extra), lambda i: (0, columns // extra)),
-        ],
-        out_specs=[pl.BlockSpec((rows // 4, columns), lambda i: (0, 0))] * 4,
+    return pl.pallas_call(
+        functools.partial(teacher_kernel, len(pres), inner, owners, block),
+        in_specs=[IN_VMEM] * (len(pres) + 2),
+        out_specs=[IN_VMEM] * 4,
         out_shape=[jax.ShapeDtypeStruct((rows // 4, columns), BF16)] * 4,
         scratch_shapes=[pltpu.VMEM((rows, columns), F32)],
         compiler_params=params(rows),
@@ -226,46 +220,34 @@
     )(*pres, down, payload)
 
 
-def student_kernel(parts, inner, *refs):
+def student_kernel(parts, inner, block, *refs):
     pre_refs, down_ref, teacher_refs = refs[:parts], refs[parts], refs[parts + 1 : parts + 5]
     hidden_ref, out_refs, total = refs[parts + 5], refs[parts + 6 : -1], refs[-1]
-    step = pl.program_id(0)
-    gate, up = added(pre_refs)
-    hidden = (gate * jax.nn.sigmoid(gate) * up).astype(BF16)
-    hidden_ref[...] = hidden
-    term = plain(hidden, down_ref[...])
-
-    @pl.when(step == 0)
-    def _():
-        total[...] = term
-
-    @pl.when(step > 0)
-    def _():
-        total[...] += term
-
-    @pl.when(step == pl.num_programs(0) - 1)
-    def _():
-        for piece, near, part, place in teacher_places(total.shape[0], inner):
-            length = piece.stop - piece.start
-            here = piece.start - 2 * near * length
-            taught = teacher_refs[part][place, :].astype(F32)
-            out_refs[near][here : here + length, :] = (total[piece, :] - taught).astype(BF16)
+    for i in range(down_ref.shape[0] // block):
+        here = slice(i * block, (i + 1) * block)
+        hidden = activated(pre_refs, block, i)
+        hidden_ref[:, here] = hidden
+        term = plain(hidden, down_ref[here, :])
+        if i == 0:
+            total[...] = term
+        else:
+            total[...] += term
+    for piece, near, part, place in teacher_places(total.shape[0], inner):
+        length = piece.stop - piece.start
+        here = piece.start - 2 * near * length
+        taught = teacher_refs[part][place, :].astype(F32)
+        out_refs[near][here : here + length, :] = (total[piece, :] - taught).astype(BF16)
 
 
 def student_parts(pres, down, teacher, inner):
     hidden, columns = down.shape
     rows, block = pres[0].shape[0], block_of(hidden, STUDENT_BLOCK)
-    piece = (rows // inner, columns)
     outs = pl.pallas_call(
-        functools.partial(student_kernel, len(pres), inner),
-        grid=(hidden // block,),
-        in_specs=[pl.BlockSpec((rows, 2 * block), lambda i: (0, i)) for _ in pres]
-        + [pl.BlockSpec((block, columns), lambda i: (i, 0))]
-        + [pl.BlockSpec((rows // 4, columns), lambda i: (0, 0))] * 4,
-        out_specs=[pl.BlockSpec((rows, block), lambda i: (0, i))]
-        + [pl.BlockSpec(piece, lambda i: (0, 0))] * inner,
+        functools.partial(student_kernel, len(pres), inner, block),
+        in_specs=[IN_VMEM] * (len(pres) + 5),
+        out_specs=[IN_VMEM] * (1 + inner),
         out_shape=[jax.ShapeDtypeStruct((rows, hidden), BF16)]
-        + [jax.ShapeDtypeStruct(piece, BF16)] * inner,
+        + [jax.ShapeDtypeStruct((rows // inner, columns), BF16)] * inner,
         scratch_shapes=[pltpu.VMEM((rows, columns), F32)],
         compiler_params=params(rows),
         cost_estimate=cost(2 * rows * hidden * columns, 2 * hidden * columns + 10 * rows * hidden),
@@ -274,21 +256,19 @@
     return outs[0], outs[1:]
 
 
-def hidden_grad_kernel(delta_ref, down_ref, out_ref):
-    out_ref[...] = against(delta_ref[...], down_ref[...]).astype(BF16)
+def hidden_grad_kernel(block, delta_ref, down_ref, out_ref):
+    for i in range(out_ref.shape[1] // block):
+        here = slice(i * block, (i + 1) * block)
+        out_ref[:, here] = against(delta_ref[...], down_ref[here, :]).astype(BF16)
 
 
 def hidden_grad_parts(delta, down):
     hidden, columns = down.shape
-    rows, block = delta.shape[0], block_of(hidden)
-    return pl.pallas_call(
-        hidden_grad_kernel,
-        grid=(hidden // block,),
-        in_specs=[
-            pl.BlockSpec((rows, columns), lambda i: (0, 0)),
-            pl.BlockSpec((block, columns), lambda i: (i, 0)),
-        ],
-        out_specs=pl.BlockSpec((rows, block), lambda i: (0, i)),
+    rows = delta.shape[0]
+    return pl.pallas_call(
+        functools.partial(hidden_grad_kernel, block_of(hidden)),
+        in_specs=[IN_VMEM] * 2,
+        out_specs=IN_VMEM,
         out_shape=jax.ShapeDtypeStruct((rows, hidden), BF16),
         compiler_params=params(rows),
         cost_estimate=cost(2 * rows * hidden * columns, 2 * hidden * columns + 2 * rows * columns),
@@ -296,53 +276,62 @@
     )(delta, down)
 
 
-def grad_down_kernel(hidden_ref, delta_ref, out_ref):
-    out_ref[...] = across(hidden_ref[...], delta_ref[...]).astype(BF16)
+def grad_down_kernel(block, hidden_ref, delta_ref, out_hbm, out_ref, sems):
+    copies = []
+    for i in range(out_hbm.shape[0] // block):
+        here = slice(i * block, (i + 1) * block)
+        out_ref[here, :] = across(hidden_ref[:, here], delta_ref[...]).astype(BF16)
+        copies.append(pltpu.make_async_copy(out_ref.at[here, :], out_hbm.at[here, :], sems.at[i]))
+        copies[-1].start()
+    for copy in copies:
+        copy.wait()
 
 
 def grad_down_of(hidden_rows, delta):
     rows, hidden = hidden_rows.shape
-    columns, block = delta.shape[1], block_of(hidden)
-    return pl.pallas_call(
-        grad_down_kernel,
-        grid=(hidden // block,),
-        in_specs=[
-            pl.BlockSpec((rows, block), lambda i: (0, i)),
-            pl.BlockSpec((rows, columns), lambda i: (0, 0)),
-        ],
-        out_specs=pl.BlockSpec((block, columns), lambda i: (i, 0)),
+    columns, block = delta.shape[1], block_of(hidden, 256)
+    return pl.pallas_call(
+        functools.partial(grad_down_kernel, block),
+        in_specs=[IN_VMEM] * 2,
+        out_specs=IN_HBM,
         out_shape=jax.ShapeDtypeStruct((hidden, columns), BF16),
+        scratch_shapes=[pltpu.VMEM((hidden, columns), BF16), pltpu.SemaphoreType.DMA((hidden // block,))],
         compiler_params=params(rows),
         cost_estimate=cost(2 * rows * hidden * columns, 2 * hidden * columns + 2 * rows * columns),
         name="grad_down",
     )(hidden_rows, delta)
 
 
-def grad_pre_kernel(parts, *refs):
+def grad_pre_kernel(parts, block, *refs):
     pre_refs, back_refs, x_ref = refs[:parts], refs[parts : 2 * parts], refs[2 * parts]
-    gate_ref, up_ref = refs[-2:]
-    gate, up = added(pre_refs)
-    back = back_refs[0][...].astype(F32)
-    for ref in back_refs[1:]:
-        back = back + ref[...].astype(F32)
-    sig = jax.nn.sigmoid(gate)
-    gate_grad = (back * up * sig * (1.0 + gate * (1.0 - sig))).astype(BF16)
-    up_grad = (back * gate * sig).astype(BF16)
-    gate_ref[...] = across(gate_grad, x_ref[...]).astype(BF16)
-    up_ref[...] = across(up_grad, x_ref[...]).astype(BF16)
+    outs_hbm, out_refs, sems = refs[2 * parts + 1 : 2 * parts + 3], refs[-3:-1], refs[-1]
+    columns = outs_hbm[0].shape[1]
+    copies = []
+    for i in range(outs_hbm[0].shape[0] // block):
+        here = slice(i * block, (i + 1) * block)
+        gate, up = added(pre_refs, block, i)
+        back = back_refs[0][:, here].astype(F32)
+        for ref in back_refs[1:]:
+            back = back + ref[:, here].astype(F32)
+        sig = jax.nn.sigmoid(gate)
+        grads = (back * up * sig * (1.0 + gate * (1.0 - sig))).astype(BF16), (back * gate * sig).astype(BF16)
+        for k in range(2):
+            out_refs[k][here, :] = across(grads[k], x_ref[:, :columns]).astype(BF16)
+            copies.append(pltpu.make_async_copy(out_refs[k].at[here, :], outs_hbm[k].at[here, :], sems.at[k, i]))
+            copies[-1].start()
+    for copy in copies:
+        copy.wait()
 
 
 def grad_pre_of(pres, backs, payload, columns):
     rows, hidden = backs[0].shape
     block = block_of(hidden, STUDENT_BLOCK)
     return pl.pallas_call(
-        functools.partial(grad_pre_kernel, len(pres)),
-        grid=(hidden // block,),
-        in_specs=[pl.BlockSpec((rows, 2 * block), lambda i: (0, i)) for _ in pres]
-        + [pl.BlockSpec((rows, block), lambda i: (0, i)) for _ in backs]
-        + [pl.BlockSpec((rows, columns), lambda i: (0, 0))],
-        out_specs=[pl.BlockSpec((block, columns), lambda i: (i, 0))] * 2,
+        functools.partial(grad_pre_kernel, len(pres), block),
+        in_specs=[IN_VMEM] * (2 * len(pres) + 1),
+        out_specs=[IN_HBM] * 2,
         out_shape=[jax.ShapeDtypeStruct((hidden, columns), BF16)] * 2,
+        scratch_shapes=[pltpu.VMEM((hidden, columns), BF16)] * 2 + [pltpu.SemaphoreType.DMA((2, hidden // block))],
         compiler_params=params(rows),
         cost_estimate=cost(4 * rows * hidden * columns, 4 * hidden * columns + 2 * rows * columns),
         name="grad_gate_up",
@@ -377,9 +366,9 @@
     tok_rows, columns = layer_in.shape
 
     payload = make_payload(layer_in, route_ids, route_scores, owners)
-    far = ring.gather_far(payload)
-    far[0] = passed(far[0])
-    far[0], payload = lax.optimization_barrier((far[0], payload))
+    far = ring.gather_far_last(payload)
+    far[-1] = passed(far[-1])
+    far[-1], payload = lax.optimization_barrier((far[-1], payload))
     near = ring.gather_near(payload)
     column = jnp.concatenate(far, axis=0)
     rows = ring.joined(payload, near, column, ring.gather_near(column))
@@ -402,7 +391,7 @@
     count = ring.inner // 2
     kept, sent = [even_blocks(t, count) for t in taught], [odd_blocks(t, count) for t in taught]
     column, kept = lax.optimization_barrier((column, kept))
-    taught = [added_rows(kept[k], ring.swap(sent[k], 2 - k, 0)) for k in range(2)]
+    taught = lax.optimization_barrier([added_rows(kept[k], ring.swap(sent[k], 2 - k, 0)) for k in range(2)])
     bit = 4
     while bit < ring.inner:
         count //= 2

time: 95.3 us -> 91.6 us (0.961)
  Pallas kernels: 21.1 us -> 16.5 us
  starting transfers between devices: 31.9 us -> 33.2 us
    pallas_call x7, Pallas kernels: 18.2 us -> 14.6 us  [the longest x2 5.26 us: pre_parts(): pl.pallas_call(functools.partial(pre_kernel, block), in_specs=[IN_VMEM] *...]
    ppermute x28, waiting for transfers between devices: 39.2 us -> 37.9 us  [swap(): lax.ppermute(value, 'wide', [(i, i ^ flip) for i in range(self.size)])]
    pallas_call x1, Pallas kernels: 2.91 us -> 1.92 us  [teacher_parts(): pl.pallas_call(functools.partial(teacher_kernel, len(pres), inner, owners...]
    ppermute x3, waiting for transfers between devices: 0.46 us -> 1.45 us  [from_pair(): lax.ppermute(value, 'dp', [(i, (i + s) % size) for i in range(size)])]
  transfers between devices with their start and end apart: 31 -> 31, of which waited for: 12 -> 15; matrix products, arithmetic and copies ran while one was open for 1% -> 1% of each run, Pallas kernels for 10% -> 8%
where the time goes in v3:
time: 91.6 us; the launch traced here: 91.4 us
  waiting for transfers between devices  39.3 us (43%)
  starting transfers between devices  33.2 us (36%)
  Pallas kernels  16.5 us (18%)
  other arithmetic  1.16 us (1%)
  between operations  0.98 us (1%)
    ppermute x28, waiting for transfers between devices, swap(): lax.ppermute(value, 'wide', [(i, i ^ flip) for i in range(self.size)])  37.9 us
    ppermute x28, starting transfers between devices, swap(): lax.ppermute(value, 'wide', [(i, i ^ flip) for i in range(self.size)])  29.4 us
    pallas_call x2, Pallas kernels, pre_parts(): pl.pallas_call(functools.partial(pre_kernel, block), in_specs=[IN_VMEM] *...  5.26 us
    ppermute x3, starting transfers between devices, from_pair(): lax.ppermute(value, 'dp', [(i, (i + s) % size) for i in range(size)])  3.72 us
    pallas_call x1, Pallas kernels, grad_pre_of(): pl.pallas_call(functools.partial(grad_pre_kernel, len(pres), block), in_s...  3.26 us
    pallas_call x1, Pallas kernels, grad_down_of(): pl.pallas_call(functools.partial(grad_down_kernel, block), in_specs=[IN_V...  2.14 us
    pallas_call x1, Pallas kernels, teacher_parts(): pl.pallas_call(functools.partial(teacher_kernel, len(pres), inner, owners...  1.92 us
  transfers between devices with their start and end apart: 31, of which 15 were waited for; matrix products, arithmetic and copies ran while one was open for 1% of the time, Pallas kernels for 8%

profile of v3, /device:TPU:1, one launch (start us, length us, event | category | flops | bytes accessed | tf_op | source)
XLA Modules:
  0.0 91.4 jit_solution(15609870606883224779)
XLA Ops:
  0.6 0.0 slice-start
  0.6 0.0 slice-start.2
  0.7 1.7 %payload.1 = bf16[16,2176]{1,0:T(8,128)(2,1)} custom-call(bf16[16,2048]{1,0:T(8,128)(2,1)} %layer_hbm.1, s32[8,16]{1,0:T(8,128)} %bitcast.24, f32[8,16]{1,0:T(8,128)} %bitcast.25), custom_call_target="tpu_custom_call" | custom-call | tf_op jit(solution)/shard_map/payload/pallas_call | solution.py:115
  2.3 0.0 copy-start.4
  2.4 0.0 slice-start.1
  2.4 0.0 slice-start.3
  2.4 4.2 %collective-permute-start = (bf16[16,2176]{1,0:T(8,128)(2,1)}, bf16[16,2176]{1,0:T(8,128)(2,1)S(1)}, u32[]{:S(2)}, u32[]{:S(2)}) collective-permute-start(bf16[16,2176]{1,0:T(8,128)(2,1)} %payload.1), channel_id=1, source_target_pairs={{0,12},{1,13},{2,14},{3,15},{4,8},{5,9},{6,10},{7,11},{8,4},{9,5},... | collective-permute-start | bytes 208904 | tf_op jit(solution)/shard_map/ppermute | solution.py:55
  6.6 0.4 collective-permute-start.1
  7.0 1.6 %collective-permute-done.in_ref = bf16[16,2176]{1,0:T(8,128)(2,1)S(1)} collective-permute-done((bf16[16,2176]{1,0:T(8,128)(2,1)}, bf16[16,2176]{1,0:T(8,128)(2,1)S(1)}, u32[]{:S(2)}, u32[]{:S(2)}) %collective-permute-start) | collective-permute-done | bytes 69664 | tf_op jit(solution)/shard_map/ppermute | solution.py:55
  8.6 2.2 %collective-permute-start.7 = (bf16[16,2176]{1,0:T(8,128)(2,1)S(1)}, bf16[16,2176]{1,0:T(8,128)(2,1)S(1)}, u32[]{:S(2)}, u32[]{:S(2)}) collective-permute-start(bf16[16,2176]{1,0:T(8,128)(2,1)S(1)} %copy-done.4), channel_id=1, source_target_pairs={{0,3},{1,2},{2,1},{3,0},{4,7},{5,6},{6,5},{7,4},{8,11},{9,10},{10,... | collective-permute-start | bytes 208904 | tf_op jit(solution)/shard_map/ppermute | solution.py:55
  10.8 0.2 collective-permute-start.5
  11.0 0.3 collective-permute-start.3
  11.3 1.4 %collective-permute-done.2 = bf16[16,2176]{1,0:T(8,128)(2,1)S(1)} collective-permute-done((bf16[16,2176]{1,0:T(8,128)(2,1)}, bf16[16,2176]{1,0:T(8,128)(2,1)S(1)}, u32[]{:S(2)}, u32[]{:S(2)}) %collective-permute-start.2) | collective-permute-done | bytes 69664 | tf_op jit(solution)/shard_map/ppermute | solution.py:55
  12.7 2.5 %collective-permute-start.8 = (bf16[48,2176]{1,0:T(8,128)(2,1)S(1)}, bf16[48,2176]{1,0:T(8,128)(2,1)S(1)}, u32[]{:S(2)}, u32[]{:S(2)}) collective-permute-start(bf16[48,2176]{1,0:T(8,128)(2,1)S(1)} %get-tuple-element.72), channel_id=1, source_target_pairs={{0,3},{1,2},{2,1},{3,0},{4,7},{5,6},{6,5},{7,4},{8,11},{9,10},{10,... | collective-permute-start | bytes 626696 | tf_op jit(solution)/shard_map/ppermute | solution.py:55
  15.2 0.2 collective-permute-start.6
  15.5 0.1 collective-permute-start.4
  15.6 9.6 %collective-permute-done.4 = bf16[48,2176]{1,0:T(8,128)(2,1)S(1)} collective-permute-done((bf16[48,2176]{1,0:T(8,128)(2,1)S(1)}, bf16[48,2176]{1,0:T(8,128)(2,1)S(1)}, u32[]{:S(2)}, u32[]{:S(2)}) %collective-permute-start.4) | collective-permute-done | bytes 208928 | tf_op jit(solution)/shard_map/ppermute | solution.py:55
  25.3 0.2 collective-permute-done.6
  25.7 0.0 copy-start.2
  25.7 3.4 %teacher_pre.1.refs_0_ = bf16[256,3072]{1,0:T(8,128)(2,1)S(1)} custom-call(bf16[256,2176]{1,0:T(8,128)(2,1)S(1)} %constant_dynamic-update-slice_fusion.3.x_ref.refs_3_.refs_4_, bf16[1536,2048]{1,0:T(8,128)(2,1)S(1)} %bitcast.18, bf16[1536,2048]{1,0:T(8,128)(2,1)S(1)} %bitcast.21), custom_call_target="tpu_custom_call" | custom-call | flops 3221225472 | bytes 14155776 | tf_op jit(solution)/shard_map/teacher_pre/pallas_call | solution.py:155
  29.2 1.5 %collective-permute-start.10 = (bf16[256,3072]{1,0:T(8,128)(2,1)S(1)}, bf16[256,3072]{1,0:T(8,128)(2,1)S(1)}, u32[]{:S(2)}, u32[]{:S(2)}) collective-permute-start(bf16[256,3072]{1,0:T(8,128)(2,1)S(1)} %teacher_pre.1.refs_0_), channel_id=1, source_target_pairs={{0,16},{16,0},{1,17},{17,1},{2,18},{18,2},{3,19},{19,3},{4,20},{20... | collective-permute-start | bytes 4718600 | tf_op jit(solution)/shard_map/ppermute | solution.py:83
  30.6 1.8 %student_pre.1.refs_0_ = f32[256,1536]{1,0:T(8,128)S(1)} custom-call(bf16[256,2176]{1,0:T(8,128)(2,1)S(1)} %constant_dynamic-update-slice_fusion.3.x_ref.refs_3_.refs_4_, bf16[768,2048]{1,0:T(8,128)(2,1)S(1)} %copy-done.2, bf16[768,2048]{1,0:T(8,128)(2,1)S(1)} %copy-done.3), custom_call_target="tpu_custom_call" | custom-call | flops 1610612736 | bytes 7077888 | tf_op jit(solution)/shard_map/student_pre/pallas_call | solution.py:155
  32.5 0.1 collective-permute-start.9
  32.6 1.1 %collective-permute-done.10.refs_1_ = bf16[256,3072]{1,0:T(8,128)(2,1)S(1)} collective-permute-done((bf16[256,3072]{1,0:T(8,128)(2,1)S(1)}, bf16[256,3072]{1,0:T(8,128)(2,1)S(1)}, u32[]{:S(2)}, u32[]{:S(2)}) %collective-permute-start.10) | collective-permute-done | bytes 1572896 | tf_op jit(solution)/shard_map/ppermute | solution.py:83
  33.7 1.9 %teacher_down.1 = (bf16[64,2048]{1,0:T(8,128)(2,1)S(1)}, bf16[64,2048]{1,0:T(8,128)(2,1)S(1)}, bf16[64,2048]{1,0:T(8,128)(2,1)S(1)}, bf16[64,2048]{1,0:T(8,128)(2,1)S(1)}) custom-call(bf16[256,3072]{1,0:T(8,128)(2,1)S(1)} %teacher_pre.1.refs_0_, bf16[256,3072]{1,0:T(8,128)(2,1)S(1)} %collective-permute-done.10.refs_1_, bf16[1536,2048]{1,0:T(8,128)(2,1)S(1)} %bitcast.15, ...), custom_call_target="tpu_custom_call" | custom-call | flops 1610612736 | bytes 10223616 | tf_op jit(solution)/shard_map/teacher_down/pallas_call | solution.py:211
  35.6 0.3 collective-permute-done.9.refs_1_
  35.9 1.0 %student_down.1 = (bf16[256,768]{1,0:T(8,128)(2,1)S(1)}, bf16[64,2048]{1,0:T(8,128)(2,1)S(1)}, bf16[64,2048]{1,0:T(8,128)(2,1)S(1)}, bf16[64,2048]{1,0:T(8,128)(2,1)S(1)}, bf16[64,2048]{1,0:T(8,128)(2,1)S(1)}) custom-call(f32[256,1536]{1,0:T(8,128)S(1)} %student_pre.1.refs_0_, f32[256,1536]{1,0:T(8,128)S(1)} %collective-permute-done.9.refs_1_, ...), custom_call_target="tpu_custom_call" | custom-call | flops 805306368 | bytes 5111808 | tf_op jit(solution)/shard_map/student_down/pallas_call | solution.py:245
  37.0 0.5 collective-permute-start.11
  37.5 1.0 %collective-permute-start.12 = (bf16[64,2048]{1,0:T(8,128)(2,1)S(1)}, bf16[64,2048]{1,0:T(8,128)(2,1)S(1)}, u32[]{:S(2)}, u32[]{:S(2)}) collective-permute-start(bf16[64,2048]{1,0:T(8,128)(2,1)S(1)} %get-tuple-element.40), channel_id=1, source_target_pairs={{0,2},{1,3},{2,0},{3,1},{4,6},{5,7},{6,4},{7,5},{8,10},{9,11},{10,... | collective-permute-start | bytes 786440 | tf_op jit(solution)/shard_map/ppermute | solution.py:55
  38.5 1.2 %collective-permute-start.13 = (bf16[64,2048]{1,0:T(8,128)(2,1)S(1)}, bf16[64,2048]{1,0:T(8,128)(2,1)S(1)}, u32[]{:S(2)}, u32[]{:S(2)}) collective-permute-start(bf16[64,2048]{1,0:T(8,128)(2,1)S(1)} %get-tuple-element.41), channel_id=1, source_target_pairs={{0,3},{1,2},{2,1},{3,0},{4,7},{5,6},{6,5},{7,4},{8,11},{9,10},{10,... | collective-permute-start | bytes 786440 | tf_op jit(solution)/shard_map/ppermute | solution.py:55
  39.7 4.9 %collective-permute-done.11 = bf16[64,2048]{1,0:T(8,128)(2,1)S(1)} collective-permute-done((bf16[64,2048]{1,0:T(8,128)(2,1)S(1)}, bf16[64,2048]{1,0:T(8,128)(2,1)S(1)}, u32[]{:S(2)}, u32[]{:S(2)}) %collective-permute-start.11) | collective-permute-done | bytes 262176 | tf_op jit(solution)/shard_map/ppermute | solution.py:55
  44.6 0.2 collective-permute-done.12
  44.8 5.5 %collective-permute-done.13 = bf16[64,2048]{1,0:T(8,128)(2,1)S(1)} collective-permute-done((bf16[64,2048]{1,0:T(8,128)(2,1)S(1)}, bf16[64,2048]{1,0:T(8,128)(2,1)S(1)}, u32[]{:S(2)}, u32[]{:S(2)}) %collective-permute-start.13) | collective-permute-done | bytes 262176 | tf_op jit(solution)/shard_map/ppermute | solution.py:55
  50.3 0.1 add_convert_fusion.2
  50.4 1.2 %collective-permute-start.14 = (bf16[64,2048]{1,0:T(8,128)(2,1)S(1)}, bf16[64,2048]{1,0:T(8,128)(2,1)S(1)}, u32[]{:S(2)}, u32[]{:S(2)}) collective-permute-start(bf16[64,2048]{1,0:T(8,128)(2,1)S(1)} %get-tuple-element.44.refs_4_), channel_id=1, source_target_pairs={{0,1},{1,0},{2,3},{3,2},{4,5},{5,4},{6,7},{7,6},{8,9},{9,8},{10,11... | collective-permute-start | bytes 786440 | tf_op jit(solution)/shard_map/ppermute | solution.py:55
  51.6 0.7 collective-permute-start.16
  52.3 2.1 %collective-permute-start.18 = (bf16[16,2048]{1,0:T(8,128)(2,1)S(1)}, bf16[16,2048]{1,0:T(8,128)(2,1)S(1)}, u32[]{:S(2)}, u32[]{:S(2)}) collective-permute-start(bf16[16,2048]{1,0:T(8,128)(2,1)S(1)} %get-tuple-element.65), channel_id=1, source_target_pairs={{0,12},{1,13},{2,14},{3,15},{4,8},{5,9},{6,10},{7,11},{8,4},{9,5},... | collective-permute-start | bytes 196616 | tf_op jit(solution)/shard_map/ppermute | solution.py:55
  54.4 0.2 collective-permute-start.17
  54.6 1.1 %collective-permute-start.15 = (bf16[64,2048]{1,0:T(8,128)(2,1)S(1)}, bf16[64,2048]{1,0:T(8,128)(2,1)S(1)}, u32[]{:S(2)}, u32[]{:S(2)}) collective-permute-start(bf16[64,2048]{1,0:T(8,128)(2,1)S(1)} %get-tuple-element.46.refs_6_), channel_id=1, source_target_pairs={{0,2},{1,3},{2,0},{3,1},{4,6},{5,7},{6,4},{7,5},{8,10},{9,11},{10,... | collective-permute-start | bytes 786440 | tf_op jit(solution)/shard_map/ppermute | solution.py:55
  55.7 1.0 %collective-permute-done.14 = bf16[64,2048]{1,0:T(8,128)(2,1)S(1)} collective-permute-done((bf16[64,2048]{1,0:T(8,128)(2,1)S(1)}, bf16[64,2048]{1,0:T(8,128)(2,1)S(1)}, u32[]{:S(2)}, u32[]{:S(2)}) %collective-permute-start.14) | collective-permute-done | bytes 262176 | tf_op jit(solution)/shard_map/ppermute | solution.py:55
  56.7 0.1 add_convert_fusion.1
  56.8 3.0 %collective-permute-done.15 = bf16[64,2048]{1,0:T(8,128)(2,1)S(1)} collective-permute-done((bf16[64,2048]{1,0:T(8,128)(2,1)S(1)}, bf16[64,2048]{1,0:T(8,128)(2,1)S(1)}, u32[]{:S(2)}, u32[]{:S(2)}) %collective-permute-start.15) | collective-permute-done | bytes 262176 | tf_op jit(solution)/shard_map/ppermute | solution.py:55
  59.8 0.1 add_convert_fusion
  59.9 0.5 collective-permute-done.17
  60.4 2.0 %collective-permute-start.21 = (bf16[16,2048]{1,0:T(8,128)(2,1)S(1)}, bf16[16,2048]{1,0:T(8,128)(2,1)S(1)}, u32[]{:S(2)}, u32[]{:S(2)}) collective-permute-start(bf16[16,2048]{1,0:T(8,128)(2,1)S(1)} %multiply_convert_fusion), channel_id=1, source_target_pairs={{0,12},{1,13},{2,14},{3,15},{4,8},{5,9},{6,10},{7,11},{8,4},{9,5},... | collective-permute-start | bytes 196616 | tf_op jit(solution)/shard_map/ppermute | solution.py:55
  62.4 0.4 collective-permute-start.20
  62.7 1.3 %collective-permute-start.19 = (bf16[16,2048]{1,0:T(8,128)(2,1)S(1)}, bf16[16,2048]{1,0:T(8,128)(2,1)S(1)}, u32[]{:S(2)}, u32[]{:S(2)}) collective-permute-start(bf16[16,2048]{1,0:T(8,128)(2,1)S(1)} %multiply_convert_fusion), channel_id=1, source_target_pairs={{0,4},{1,5},{2,6},{3,7},{4,0},{5,1},{6,2},{7,3},{8,12},{9,13},{10,... | collective-permute-start | bytes 196616 | tf_op jit(solution)/shard_map/ppermute | solution.py:55
  64.1 1.0 %collective-permute-start.26 = (bf16[32,2048]{1,0:T(8,128)(2,1)S(1)}, bf16[32,2048]{1,0:T(8,128)(2,1)S(1)}, u32[]{:S(2)}, u32[]{:S(2)}) collective-permute-start(bf16[32,2048]{1,0:T(8,128)(2,1)S(1)} %get-tuple-element.60), channel_id=1, source_target_pairs={{0,1},{1,0},{2,3},{3,2},{4,5},{5,4},{6,7},{7,6},{8,9},{9,8},{10,11... | collective-permute-start | bytes 393224 | tf_op jit(solution)/shard_map/ppermute | solution.py:55
  65.1 1.0 %collective-permute-start.25 = (bf16[32,2048]{1,0:T(8,128)(2,1)S(1)}, bf16[32,2048]{1,0:T(8,128)(2,1)S(1)}, u32[]{:S(2)}, u32[]{:S(2)}) collective-permute-start(bf16[32,2048]{1,0:T(8,128)(2,1)S(1)} %get-tuple-element.78), channel_id=1, source_target_pairs={{0,2},{1,3},{2,0},{3,1},{4,6},{5,7},{6,4},{7,5},{8,10},{9,11},{10,... | collective-permute-start | bytes 393224 | tf_op jit(solution)/shard_map/ppermute | solution.py:55
  66.1 1.0 %collective-permute-done.20 = bf16[16,2048]{1,0:T(8,128)(2,1)S(1)} collective-permute-done((bf16[16,2048]{1,0:T(8,128)(2,1)S(1)}, bf16[16,2048]{1,0:T(8,128)(2,1)S(1)}, u32[]{:S(2)}, u32[]{:S(2)}) %collective-permute-start.20) | collective-permute-done | bytes 65568 | tf_op jit(solution)/shard_map/ppermute | solution.py:55
  67.1 1.5 %collective-permute-start.24 = (bf16[64,2048]{1,0:T(8,128)(2,1)S(1)}, bf16[64,2048]{1,0:T(8,128)(2,1)S(1)}, u32[]{:S(2)}, u32[]{:S(2)}) collective-permute-start(bf16[64,2048]{1,0:T(8,128)(2,1)S(1)} %pad_maximum_fusion.1), channel_id=1, source_target_pairs={{0,3},{1,2},{2,1},{3,0},{4,7},{5,6},{6,5},{7,4},{8,11},{9,10},{10,... | collective-permute-start | bytes 786440 | tf_op jit(solution)/shard_map/ppermute | solution.py:55
  68.6 0.7 collective-permute-start.23
  69.3 0.5 collective-permute-start.22
  69.9 0.2 collective-permute-start.27
  70.1 1.8 %collective-permute-start.28 = (bf16[16,2048]{1,0:T(8,128)(2,1)S(1)}, bf16[16,2048]{1,0:T(8,128)(2,1)S(1)}, u32[]{:S(2)}, u32[]{:S(2)}) collective-permute-start(bf16[16,2048]{1,0:T(8,128)(2,1)S(1)} %get-tuple-element.70), channel_id=1, source_target_pairs={{0,8},{1,9},{2,10},{3,11},{4,12},{5,13},{6,14},{7,15},{8,0},{9,1},... | collective-permute-start | bytes 196616 | tf_op jit(solution)/shard_map/ppermute | solution.py:55
  72.0 2.8 %collective-permute-done.24 = bf16[64,2048]{1,0:T(8,128)(2,1)S(1)} collective-permute-done((bf16[64,2048]{1,0:T(8,128)(2,1)S(1)}, bf16[64,2048]{1,0:T(8,128)(2,1)S(1)}, u32[]{:S(2)}, u32[]{:S(2)}) %collective-permute-start.24) | collective-permute-done | bytes 262176 | tf_op jit(solution)/shard_map/ppermute | solution.py:55
  74.7 0.9 %collective-permute-start.29 = (bf16[16,2048]{1,0:T(8,128)(2,1)S(1)}, bf16[16,2048]{1,0:T(8,128)(2,1)S(1)}, u32[]{:S(2)}, u32[]{:S(2)}) collective-permute-start(bf16[16,2048]{1,0:T(8,128)(2,1)S(1)} %get-tuple-element.71), channel_id=1, source_target_pairs={{0,12},{1,13},{2,14},{3,15},{4,8},{5,9},{6,10},{7,11},{8,4},{9,5},... | collective-permute-start | bytes 196616 | tf_op jit(solution)/shard_map/ppermute | solution.py:55
  75.6 6.2 %collective-permute-done.23 = bf16[64,2048]{1,0:T(8,128)(2,1)S(1)} collective-permute-done((bf16[64,2048]{1,0:T(8,128)(2,1)S(1)}, bf16[64,2048]{1,0:T(8,128)(2,1)S(1)}, u32[]{:S(2)}, u32[]{:S(2)}) %collective-permute-start.23) | collective-permute-done | bytes 262176 | tf_op jit(solution)/shard_map/ppermute | solution.py:55
  81.8 0.1 pad_maximum_fusion.delta_ref
  81.9 1.3 %hidden_grad.1.refs_2_ = bf16[256,768]{1,0:T(8,128)(2,1)S(1)} custom-call(bf16[256,2048]{1,0:T(8,128)(2,1)S(1)} %pad_maximum_fusion.delta_ref, bf16[768,2048]{1,0:T(8,128)(2,1)S(1)} %copy-done), custom_call_target="tpu_custom_call" | custom-call | flops 805306368 | bytes 4194304 | tf_op jit(solution)/shard_map/hidden_grad/pallas_call | solution.py:268
  83.2 2.1 %collective-permute-start.30 = (bf16[256,768]{1,0:T(8,128)(2,1)S(1)}, bf16[256,768]{1,0:T(8,128)(2,1)S(1)}, u32[]{:S(2)}, u32[]{:S(2)}) collective-permute-start(bf16[256,768]{1,0:T(8,128)(2,1)S(1)} %hidden_grad.1.refs_2_), channel_id=1, source_target_pairs={{0,16},{16,0},{1,17},{17,1},{2,18},{18,2},{3,19},{19,3},{4,20},{20... | collective-permute-start | bytes 1179656 | tf_op jit(solution)/shard_map/ppermute | solution.py:83
  85.3 2.1 %grad_down.1 = bf16[768,2048]{1,0:T(8,128)(2,1)} custom-call(bf16[256,768]{1,0:T(8,128)(2,1)S(1)} %get-tuple-element.59.hidden_ref, bf16[256,2048]{1,0:T(8,128)(2,1)S(1)} %pad_maximum_fusion.delta_ref), custom_call_target="tpu_custom_call" | custom-call | flops 805306368 | bytes 4194304 | tf_op jit(solution)/shard_map/grad_down/pallas_call | solution.py:293
  87.5 0.7 add_convert_fusion.5
  88.2 3.3 %grad_gate_up.1 = (bf16[768,2048]{1,0:T(8,128)(2,1)}, bf16[768,2048]{1,0:T(8,128)(2,1)}) custom-call(f32[256,1536]{1,0:T(8,128)S(1)} %student_pre.1.refs_0_, f32[256,1536]{1,0:T(8,128)S(1)} %collective-permute-done.9.refs_1_, bf16[256,768]{1,0:T(8,128)(2,1)S(1)} %hidden_grad.1.refs_2_, bf16[256,768]{1,0:T(8,128)(2,1)S(1)} %collective-permute-done.30.refs_3_, ...), custom_call_target="tpu_custom_call" | custom-call | flops 1610612736 | bytes 7340032 | tf_op jit(solution)/shard_map/grad_gate_up/pallas_call | solution.py:329
  (50 shorter events, 0.4 us)
Async XLA Ops:
  0.6 25.0 %slice-start = ((s8[6291456]{0:T(1024)(128)(4,1)}), s8[2097152]{0:T(1024)(128)(4,1)S(1)}, s32[]{:S(2)}) async-start(s8[6291456]{0:T(1024)(128)(4,1)} %bitcast.16), calls=%async_computation | async-start | bytes 4194304
  0.6 25.0 %slice-start.2 = ((s8[6291456]{0:T(1024)(128)(4,1)}), s8[4194304]{0:T(1024)(128)(4,1)S(1)}, s32[]{:S(2)}) async-start(s8[6291456]{0:T(1024)(128)(4,1)} %bitcast.19), calls=%async_computation.2 | async-start | bytes 8388608
  2.3 6.2 %copy-start.4 = (bf16[16,2176]{1,0:T(8,128)(2,1)S(1)}, bf16[16,2176]{1,0:T(8,128)(2,1)}, u32[]{:S(2)}) copy-start(bf16[16,2176]{1,0:T(8,128)(2,1)} %payload.1) | copy-start | bytes 208900
  2.4 23.3 %slice-start.1 = ((s8[6291456]{0:T(1024)(128)(4,1)}), s8[4194304]{0:T(1024)(128)(4,1)S(1)}, s32[]{:S(2)}) async-start(s8[6291456]{0:T(1024)(128)(4,1)} %bitcast.16), calls=%async_computation.1 | async-start | bytes 8388608
  2.4 23.3 %slice-start.3 = ((s8[6291456]{0:T(1024)(128)(4,1)}), s8[2097152]{0:T(1024)(128)(4,1)S(1)}, s32[]{:S(2)}) async-start(s8[6291456]{0:T(1024)(128)(4,1)} %bitcast.19), calls=%async_computation.3 | async-start | bytes 4194304
  2.4 6.2 %collective-permute-start = (bf16[16,2176]{1,0:T(8,128)(2,1)}, bf16[16,2176]{1,0:T(8,128)(2,1)S(1)}, u32[]{:S(2)}, u32[]{:S(2)}) collective-permute-start(bf16[16,2176]{1,0:T(8,128)(2,1)} %payload.1), channel_id=1, source_target_pairs={{0,12},{1,13},{2,14},{3,15},{4,8},{5,9},{6,10},{7,11},{8,4},{9,5},... | collective-permute-start | bytes 208904 | tf_op jit(solution)/shard_map/ppermute | solution.py:55
  6.6 6.1 %collective-permute-start.2 = (bf16[16,2176]{1,0:T(8,128)(2,1)}, bf16[16,2176]{1,0:T(8,128)(2,1)S(1)}, u32[]{:S(2)}, u32[]{:S(2)}) collective-permute-start(bf16[16,2176]{1,0:T(8,128)(2,1)} %payload.1), channel_id=1, source_target_pairs={{0,8},{1,9},{2,10},{3,11},{4,12},{5,13},{6,14},{7,15},{8,0},{9,1},... | collective-permute-start | bytes 208904 | tf_op jit(solution)/shard_map/ppermute | solution.py:55
  6.6 4.7 %collective-permute-start.1 = (bf16[16,2176]{1,0:T(8,128)(2,1)}, bf16[16,2176]{1,0:T(8,128)(2,1)S(1)}, u32[]{:S(2)}, u32[]{:S(2)}) collective-permute-start(bf16[16,2176]{1,0:T(8,128)(2,1)} %payload.1), channel_id=1, source_target_pairs={{0,4},{1,5},{2,6},{3,7},{4,0},{5,1},{6,2},{7,3},{8,12},{9,13},{10,... | collective-permute-start | bytes 208904 | tf_op jit(solution)/shard_map/ppermute | solution.py:55
  8.6 17.0 %collective-permute-start.7 = (bf16[16,2176]{1,0:T(8,128)(2,1)S(1)}, bf16[16,2176]{1,0:T(8,128)(2,1)S(1)}, u32[]{:S(2)}, u32[]{:S(2)}) collective-permute-start(bf16[16,2176]{1,0:T(8,128)(2,1)S(1)} %copy-done.4), channel_id=1, source_target_pairs={{0,3},{1,2},{2,1},{3,0},{4,7},{5,6},{6,5},{7,4},{8,11},{9,10},{10,... | collective-permute-start | bytes 208904 | tf_op jit(solution)/shard_map/ppermute | solution.py:55
  10.8 14.5 %collective-permute-start.5 = (bf16[16,2176]{1,0:T(8,128)(2,1)S(1)}, bf16[16,2176]{1,0:T(8,128)(2,1)S(1)}, u32[]{:S(2)}, u32[]{:S(2)}) collective-permute-start(bf16[16,2176]{1,0:T(8,128)(2,1)S(1)} %copy-done.4), channel_id=1, source_target_pairs={{0,2},{1,3},{2,0},{3,1},{4,6},{5,7},{6,4},{7,5},{8,10},{9,11},{10,... | collective-permute-start | bytes 208904 | tf_op jit(solution)/shard_map/ppermute | solution.py:55
  11.0 4.4 %collective-permute-start.3 = (bf16[16,2176]{1,0:T(8,128)(2,1)S(1)}, bf16[16,2176]{1,0:T(8,128)(2,1)S(1)}, u32[]{:S(2)}, u32[]{:S(2)}) collective-permute-start(bf16[16,2176]{1,0:T(8,128)(2,1)S(1)} %copy-done.4), channel_id=1, source_target_pairs={{0,1},{1,0},{2,3},{3,2},{4,5},{5,4},{6,7},{7,6},{8,9},{9,8},{10,11... | collective-permute-start | bytes 208904 | tf_op jit(solution)/shard_map/ppermute | solution.py:55
  12.7 12.9 %collective-permute-start.8 = (bf16[48,2176]{1,0:T(8,128)(2,1)S(1)}, bf16[48,2176]{1,0:T(8,128)(2,1)S(1)}, u32[]{:S(2)}, u32[]{:S(2)}) collective-permute-start(bf16[48,2176]{1,0:T(8,128)(2,1)S(1)} %get-tuple-element.72), channel_id=1, source_target_pairs={{0,3},{1,2},{2,1},{3,0},{4,7},{5,6},{6,5},{7,4},{8,11},{9,10},{10,... | collective-permute-start | bytes 626696 | tf_op jit(solution)/shard_map/ppermute | solution.py:55
  15.2 10.3 %collective-permute-start.6 = (bf16[48,2176]{1,0:T(8,128)(2,1)S(1)}, bf16[48,2176]{1,0:T(8,128)(2,1)S(1)}, u32[]{:S(2)}, u32[]{:S(2)}) collective-permute-start(bf16[48,2176]{1,0:T(8,128)(2,1)S(1)} %get-tuple-element.72), channel_id=1, source_target_pairs={{0,2},{1,3},{2,0},{3,1},{4,6},{5,7},{6,4},{7,5},{8,10},{9,11},{10,... | collective-permute-start | bytes 626696 | tf_op jit(solution)/shard_map/ppermute | solution.py:55
  15.5 9.8 %collective-permute-start.4 = (bf16[48,2176]{1,0:T(8,128)(2,1)S(1)}, bf16[48,2176]{1,0:T(8,128)(2,1)S(1)}, u32[]{:S(2)}, u32[]{:S(2)}) collective-permute-start(bf16[48,2176]{1,0:T(8,128)(2,1)S(1)} %get-tuple-element.72), channel_id=1, source_target_pairs={{0,1},{1,0},{2,3},{3,2},{4,5},{5,4},{6,7},{7,6},{8,9},{9,8},{10,11... | collective-permute-start | bytes 626696 | tf_op jit(solution)/shard_map/ppermute | solution.py:55
  25.7 5.0 %copy-start.2 = (bf16[768,2048]{1,0:T(8,128)(2,1)S(1)}, bf16[768,2048]{1,0:T(8,128)(2,1)}, u32[]{:S(2)}) copy-start(bf16[768,2048]{1,0:T(8,128)(2,1)} %gate_ref.1) | copy-start | bytes 9437188
  25.7 4.9 %copy-start.3 = (bf16[768,2048]{1,0:T(8,128)(2,1)S(1)}, bf16[768,2048]{1,0:T(8,128)(2,1)}, u32[]{:S(2)}) copy-start(bf16[768,2048]{1,0:T(8,128)(2,1)} %up_ref.1) | copy-start | bytes 9437188
  29.2 4.5 %collective-permute-start.10 = (bf16[256,3072]{1,0:T(8,128)(2,1)S(1)}, bf16[256,3072]{1,0:T(8,128)(2,1)S(1)}, u32[]{:S(2)}, u32[]{:S(2)}) collective-permute-start(bf16[256,3072]{1,0:T(8,128)(2,1)S(1)} %teacher_pre.1.refs_0_), channel_id=1, source_target_pairs={{0,16},{16,0},{1,17},{17,1},{2,18},{18,2},{3,19},{19,3},{4,20},{20... | collective-permute-start | bytes 4718600 | tf_op jit(solution)/shard_map/ppermute | solution.py:83
  30.6 3.0 %copy-start.1 = (bf16[1,1536,2048]{2,1,0:T(8,128)(2,1)S(1)}, bf16[1,1536,2048]{2,1,0:T(8,128)(2,1)}, u32[]{:S(2)}) copy-start(bf16[1,1536,2048]{2,1,0:T(8,128)(2,1)} %param.14) | copy-start | bytes 18874372
  32.5 3.5 %collective-permute-start.9 = (f32[256,1536]{1,0:T(8,128)S(1)}, f32[256,1536]{1,0:T(8,128)S(1)}, u32[]{:S(2)}, u32[]{:S(2)}) collective-permute-start(f32[256,1536]{1,0:T(8,128)S(1)} %student_pre.1.refs_0_), channel_id=1, source_target_pairs={{0,16},{16,0},{1,17},{17,1},{2,18},{18,2},{3,19},{19,3},{4,20},{20... | collective-permute-start | bytes 4718600 | tf_op jit(solution)/shard_map/ppermute | solution.py:83
  33.7 2.3 %copy-start = (bf16[768,2048]{1,0:T(8,128)(2,1)S(1)}, bf16[768,2048]{1,0:T(8,128)(2,1)}, u32[]{:S(2)}) copy-start(bf16[768,2048]{1,0:T(8,128)(2,1)} %down_ref.1) | copy-start | bytes 9437188
  37.0 7.6 %collective-permute-start.11 = (bf16[64,2048]{1,0:T(8,128)(2,1)S(1)}, bf16[64,2048]{1,0:T(8,128)(2,1)S(1)}, u32[]{:S(2)}, u32[]{:S(2)}) collective-permute-start(bf16[64,2048]{1,0:T(8,128)(2,1)S(1)} %get-tuple-element.39), channel_id=1, source_target_pairs={{0,1},{1,0},{2,3},{3,2},{4,5},{5,4},{6,7},{7,6},{8,9},{9,8},{10,11... | collective-permute-start | bytes 786440 | tf_op jit(solution)/shard_map/ppermute | solution.py:55
  37.5 7.3 %collective-permute-start.12 = (bf16[64,2048]{1,0:T(8,128)(2,1)S(1)}, bf16[64,2048]{1,0:T(8,128)(2,1)S(1)}, u32[]{:S(2)}, u32[]{:S(2)}) collective-permute-start(bf16[64,2048]{1,0:T(8,128)(2,1)S(1)} %get-tuple-element.40), channel_id=1, source_target_pairs={{0,2},{1,3},{2,0},{3,1},{4,6},{5,7},{6,4},{7,5},{8,10},{9,11},{10,... | collective-permute-start | bytes 786440 | tf_op jit(solution)/shard_map/ppermute | solution.py:55
  38.5 11.8 %collective-permute-start.13 = (bf16[64,2048]{1,0:T(8,128)(2,1)S(1)}, bf16[64,2048]{1,0:T(8,128)(2,1)S(1)}, u32[]{:S(2)}, u32[]{:S(2)}) collective-permute-start(bf16[64,2048]{1,0:T(8,128)(2,1)S(1)} %get-tuple-element.41), channel_id=1, source_target_pairs={{0,3},{1,2},{2,1},{3,0},{4,7},{5,6},{6,5},{7,4},{8,11},{9,10},{10,... | collective-permute-start | bytes 786440 | tf_op jit(solution)/shard_map/ppermute | solution.py:55
  50.4 6.3 %collective-permute-start.14 = (bf16[64,2048]{1,0:T(8,128)(2,1)S(1)}, bf16[64,2048]{1,0:T(8,128)(2,1)S(1)}, u32[]{:S(2)}, u32[]{:S(2)}) collective-permute-start(bf16[64,2048]{1,0:T(8,128)(2,1)S(1)} %get-tuple-element.44.refs_4_), channel_id=1, source_target_pairs={{0,1},{1,0},{2,3},{3,2},{4,5},{5,4},{6,7},{7,6},{8,9},{9,8},{10,11... | collective-permute-start | bytes 786440 | tf_op jit(solution)/shard_map/ppermute | solution.py:55
  51.6 8.3 %collective-permute-start.16 = (bf16[16,2048]{1,0:T(8,128)(2,1)S(1)}, bf16[16,2048]{1,0:T(8,128)(2,1)S(1)}, u32[]{:S(2)}, u32[]{:S(2)}) collective-permute-start(bf16[16,2048]{1,0:T(8,128)(2,1)S(1)} %get-tuple-element.64), channel_id=1, source_target_pairs={{0,4},{1,5},{2,6},{3,7},{4,0},{5,1},{6,2},{7,3},{8,12},{9,13},{10,... | collective-permute-start | bytes 196616 | tf_op jit(solution)/shard_map/ppermute | solution.py:55
  52.3 7.6 %collective-permute-start.18 = (bf16[16,2048]{1,0:T(8,128)(2,1)S(1)}, bf16[16,2048]{1,0:T(8,128)(2,1)S(1)}, u32[]{:S(2)}, u32[]{:S(2)}) collective-permute-start(bf16[16,2048]{1,0:T(8,128)(2,1)S(1)} %get-tuple-element.65), channel_id=1, source_target_pairs={{0,12},{1,13},{2,14},{3,15},{4,8},{5,9},{6,10},{7,11},{8,4},{9,5},... | collective-permute-start | bytes 196616 | tf_op jit(solution)/shard_map/ppermute | solution.py:55
  54.4 6.0 %collective-permute-start.17 = (bf16[16,2048]{1,0:T(8,128)(2,1)S(1)}, bf16[16,2048]{1,0:T(8,128)(2,1)S(1)}, u32[]{:S(2)}, u32[]{:S(2)}) collective-permute-start(bf16[16,2048]{1,0:T(8,128)(2,1)S(1)} %get-tuple-element.66), channel_id=1, source_target_pairs={{0,8},{1,9},{2,10},{3,11},{4,12},{5,13},{6,14},{7,15},{8,0},{9,1},... | collective-permute-start | bytes 196616 | tf_op jit(solution)/shard_map/ppermute | solution.py:55
  54.6 5.2 %collective-permute-start.15 = (bf16[64,2048]{1,0:T(8,128)(2,1)S(1)}, bf16[64,2048]{1,0:T(8,128)(2,1)S(1)}, u32[]{:S(2)}, u32[]{:S(2)}) collective-permute-start(bf16[64,2048]{1,0:T(8,128)(2,1)S(1)} %get-tuple-element.46.refs_6_), channel_id=1, source_target_pairs={{0,2},{1,3},{2,0},{3,1},{4,6},{5,7},{6,4},{7,5},{8,10},{9,11},{10,... | collective-permute-start | bytes 786440 | tf_op jit(solution)/shard_map/ppermute | solution.py:55
  60.4 5.7 %collective-permute-start.21 = (bf16[16,2048]{1,0:T(8,128)(2,1)S(1)}, bf16[16,2048]{1,0:T(8,128)(2,1)S(1)}, u32[]{:S(2)}, u32[]{:S(2)}) collective-permute-start(bf16[16,2048]{1,0:T(8,128)(2,1)S(1)} %multiply_convert_fusion), channel_id=1, source_target_pairs={{0,12},{1,13},{2,14},{3,15},{4,8},{5,9},{6,10},{7,11},{8,4},{9,5},... | collective-permute-start | bytes 196616 | tf_op jit(solution)/shard_map/ppermute | solution.py:55
  62.4 4.7 %collective-permute-start.20 = (bf16[16,2048]{1,0:T(8,128)(2,1)S(1)}, bf16[16,2048]{1,0:T(8,128)(2,1)S(1)}, u32[]{:S(2)}, u32[]{:S(2)}) collective-permute-start(bf16[16,2048]{1,0:T(8,128)(2,1)S(1)} %multiply_convert_fusion), channel_id=1, source_target_pairs={{0,8},{1,9},{2,10},{3,11},{4,12},{5,13},{6,14},{7,15},{8,0},{9,1},... | collective-permute-start | bytes 196616 | tf_op jit(solution)/shard_map/ppermute | solution.py:55
  62.7 4.4 %collective-permute-start.19 = (bf16[16,2048]{1,0:T(8,128)(2,1)S(1)}, bf16[16,2048]{1,0:T(8,128)(2,1)S(1)}, u32[]{:S(2)}, u32[]{:S(2)}) collective-permute-start(bf16[16,2048]{1,0:T(8,128)(2,1)S(1)} %multiply_convert_fusion), channel_id=1, source_target_pairs={{0,4},{1,5},{2,6},{3,7},{4,0},{5,1},{6,2},{7,3},{8,12},{9,13},{10,... | collective-permute-start | bytes 196616 | tf_op jit(solution)/shard_map/ppermute | solution.py:55
  64.1 5.8 %collective-permute-start.26 = (bf16[32,2048]{1,0:T(8,128)(2,1)S(1)}, bf16[32,2048]{1,0:T(8,128)(2,1)S(1)}, u32[]{:S(2)}, u32[]{:S(2)}) collective-permute-start(bf16[32,2048]{1,0:T(8,128)(2,1)S(1)} %get-tuple-element.60), channel_id=1, source_target_pairs={{0,1},{1,0},{2,3},{3,2},{4,5},{5,4},{6,7},{7,6},{8,9},{9,8},{10,11... | collective-permute-start | bytes 393224 | tf_op jit(solution)/shard_map/ppermute | solution.py:55
  65.1 4.8 %collective-permute-start.25 = (bf16[32,2048]{1,0:T(8,128)(2,1)S(1)}, bf16[32,2048]{1,0:T(8,128)(2,1)S(1)}, u32[]{:S(2)}, u32[]{:S(2)}) collective-permute-start(bf16[32,2048]{1,0:T(8,128)(2,1)S(1)} %get-tuple-element.78), channel_id=1, source_target_pairs={{0,2},{1,3},{2,0},{3,1},{4,6},{5,7},{6,4},{7,5},{8,10},{9,11},{10,... | collective-permute-start | bytes 393224 | tf_op jit(solution)/shard_map/ppermute | solution.py:55
  67.1 7.6 %collective-permute-start.24 = (bf16[64,2048]{1,0:T(8,128)(2,1)S(1)}, bf16[64,2048]{1,0:T(8,128)(2,1)S(1)}, u32[]{:S(2)}, u32[]{:S(2)}) collective-permute-start(bf16[64,2048]{1,0:T(8,128)(2,1)S(1)} %pad_maximum_fusion.1), channel_id=1, source_target_pairs={{0,3},{1,2},{2,1},{3,0},{4,7},{5,6},{6,5},{7,4},{8,11},{9,10},{10,... | collective-permute-start | bytes 786440 | tf_op jit(solution)/shard_map/ppermute | solution.py:55
  68.6 13.2 %collective-permute-start.23 = (bf16[64,2048]{1,0:T(8,128)(2,1)S(1)}, bf16[64,2048]{1,0:T(8,128)(2,1)S(1)}, u32[]{:S(2)}, u32[]{:S(2)}) collective-permute-start(bf16[64,2048]{1,0:T(8,128)(2,1)S(1)} %pad_maximum_fusion.1), channel_id=1, source_target_pairs={{0,2},{1,3},{2,0},{3,1},{4,6},{5,7},{6,4},{7,5},{8,10},{9,11},{10,... | collective-permute-start | bytes 786440 | tf_op jit(solution)/shard_map/ppermute | solution.py:55
  69.3 12.5 %collective-permute-start.22 = (bf16[64,2048]{1,0:T(8,128)(2,1)S(1)}, bf16[64,2048]{1,0:T(8,128)(2,1)S(1)}, u32[]{:S(2)}, u32[]{:S(2)}) collective-permute-start(bf16[64,2048]{1,0:T(8,128)(2,1)S(1)} %pad_maximum_fusion.1), channel_id=1, source_target_pairs={{0,1},{1,0},{2,3},{3,2},{4,5},{5,4},{6,7},{7,6},{8,9},{9,8},{10,11... | collective-permute-start | bytes 786440 | tf_op jit(solution)/shard_map/ppermute | solution.py:55
  69.9 17.5 %collective-permute-start.27 = (bf16[16,2048]{1,0:T(8,128)(2,1)S(1)}, bf16[16,2048]{1,0:T(8,128)(2,1)S(1)}, u32[]{:S(2)}, u32[]{:S(2)}) collective-permute-start(bf16[16,2048]{1,0:T(8,128)(2,1)S(1)} %get-tuple-element.69), channel_id=1, source_target_pairs={{0,4},{1,5},{2,6},{3,7},{4,0},{5,1},{6,2},{7,3},{8,12},{9,13},{10,... | collective-permute-start | bytes 196616 | tf_op jit(solution)/shard_map/ppermute | solution.py:55
  70.1 17.3 %collective-permute-start.28 = (bf16[16,2048]{1,0:T(8,128)(2,1)S(1)}, bf16[16,2048]{1,0:T(8,128)(2,1)S(1)}, u32[]{:S(2)}, u32[]{:S(2)}) collective-permute-start(bf16[16,2048]{1,0:T(8,128)(2,1)S(1)} %get-tuple-element.70), channel_id=1, source_target_pairs={{0,8},{1,9},{2,10},{3,11},{4,12},{5,13},{6,14},{7,15},{8,0},{9,1},... | collective-permute-start | bytes 196616 | tf_op jit(solution)/shard_map/ppermute | solution.py:55
  74.7 12.8 %collective-permute-start.29 = (bf16[16,2048]{1,0:T(8,128)(2,1)S(1)}, bf16[16,2048]{1,0:T(8,128)(2,1)S(1)}, u32[]{:S(2)}, u32[]{:S(2)}) collective-permute-start(bf16[16,2048]{1,0:T(8,128)(2,1)S(1)} %get-tuple-element.71), channel_id=1, source_target_pairs={{0,12},{1,13},{2,14},{3,15},{4,8},{5,9},{6,10},{7,11},{8,4},{9,5},... | collective-permute-start | bytes 196616 | tf_op jit(solution)/shard_map/ppermute | solution.py:55
  83.2 5.0 %collective-permute-start.30 = (bf16[256,768]{1,0:T(8,128)(2,1)S(1)}, bf16[256,768]{1,0:T(8,128)(2,1)S(1)}, u32[]{:S(2)}, u32[]{:S(2)}) collective-permute-start(bf16[256,768]{1,0:T(8,128)(2,1)S(1)} %hidden_grad.1.refs_2_), channel_id=1, source_target_pairs={{0,16},{16,0},{1,17},{17,1},{2,18},{18,2},{3,19},{19,3},{4,20},{20... | collective-permute-start | bytes 1179656 | tf_op jit(solution)/shard_map/ppermute | solution.py:83

commit v4 on v3

--- a/solution.py
+++ b/solution.py
@@ -74,8 +74,7 @@
         return sum(a.astype(F32) for a in arrived).astype(BF16)
 
     def reduce_far(self, blocks):
-        arrived = [blocks[0]] + [self.swap(blocks[k], 0, k) for k in range(1, self.outer)]
-        return sum(a.astype(F32) for a in arrived)
+        return [blocks[0]] + [self.swap(blocks[k], 0, k) for k in range(1, self.outer)]
 
 
 def from_pair(value):
@@ -232,28 +231,31 @@
             total[...] = term
         else:
             total[...] += term
+    first = out_refs[0].shape[0]
     for piece, near, part, place in teacher_places(total.shape[0], inner):
-        length = piece.stop - piece.start
-        here = piece.start - 2 * near * length
-        taught = teacher_refs[part][place, :].astype(F32)
-        out_refs[near][here : here + length, :] = (total[piece, :] - taught).astype(BF16)
-
-
-def student_parts(pres, down, teacher, inner):
+        block = (total[piece, :] - teacher_refs[part][place, :].astype(F32)).astype(BF16)
+        if part < 2:
+            out_refs[2 * near][...] = block[:first]
+            out_refs[2 * near + 1][: block.shape[0] - first, :] = block[first:]
+        else:
+            out_refs[2 * near + 1][block.shape[0] - first :, :] = block
+
+
+def student_parts(pres, down, teacher, inner, first):
     hidden, columns = down.shape
     rows, block = pres[0].shape[0], block_of(hidden, STUDENT_BLOCK)
     outs = pl.pallas_call(
         functools.partial(student_kernel, len(pres), inner, block),
         in_specs=[IN_VMEM] * (len(pres) + 5),
-        out_specs=[IN_VMEM] * (1 + inner),
+        out_specs=[IN_VMEM] * (1 + 2 * inner),
         out_shape=[jax.ShapeDtypeStruct((rows, hidden), BF16)]
-        + [jax.ShapeDtypeStruct((rows // inner, columns), BF16)] * inner,
+        + [jax.ShapeDtypeStruct((height, columns), BF16) for height in (first, rows // inner - first)] * inner,
         scratch_shapes=[pltpu.VMEM((rows, columns), F32)],
         compiler_params=params(rows),
         cost_estimate=cost(2 * rows * hidden * columns, 2 * hidden * columns + 10 * rows * hidden),
         name="student_down",
     )(*pres, down, *teacher)
-    return outs[0], outs[1:]
+    return outs[0], outs[1::2], outs[2::2]
 
 
 def hidden_grad_kernel(block, delta_ref, down_ref, out_ref):
@@ -378,31 +380,36 @@
     student_pre = pre_parts(rows, student_gate, student_up, F32, STUDENT_BLOCK, "student_pre")
     student_pres = [student_pre] + from_pair(student_pre)
     teacher = teacher_parts(expert_pres, expert_down[0], rows, ring.inner, owners)
-    student_hidden, pieces = student_parts(student_pres, student_down, teacher, ring.inner)
+    student_hidden, firsts, rests = student_parts(student_pres, student_down, teacher, ring.inner, tok_rows)
 
     loss_scale = 1.0 / math.sqrt(tok_rows * owners)
-    column, teacher = lax.optimization_barrier((ring.reduce_near(pieces), teacher))
-    taught = [added_rows(teacher[2 * k], ring.swap(teacher[2 * k + 1], 1 + k, 0)) for k in range(2)]
-    blocks = list(column.reshape(ring.outer, tok_rows, columns))
-    blocks[0], taught = lax.optimization_barrier((blocks[0], taught))
-    delta = (ring.reduce_far(blocks) * loss_scale).astype(BF16)
-
-    column = jnp.concatenate([delta] + ring.gather_far(delta), axis=0)
+    column, teacher = lax.optimization_barrier((ring.reduce_near(rests), teacher))
+    arrived = [ring.swap(teacher[2 * k + 1], 1 + k, 0) for k in range(2)]
+    terms = ring.reduce_far([firsts[0]] + list(column.reshape(ring.outer - 1, tok_rows, columns)))
+    terms += [ring.swap(firsts[k], k, 0) for k in range(1, ring.inner)]
+    delta = (sum(a.astype(F32) for a in terms) * loss_scale).astype(BF16)
+    delta, arrived = lax.optimization_barrier((delta, arrived))
+    taught = [added_rows(teacher[2 * k], arrived[k]) for k in range(2)]
+
+    far = ring.gather_far(delta)
     count = ring.inner // 2
-    kept, sent = [even_blocks(t, count) for t in taught], [odd_blocks(t, count) for t in taught]
-    column, kept = lax.optimization_barrier((column, kept))
-    taught = lax.optimization_barrier([added_rows(kept[k], ring.swap(sent[k], 2 - k, 0)) for k in range(2)])
+    near = [
+        ring.swap(jnp.concatenate([delta, odd_blocks(taught[2 - k], count)], axis=0), k, 0) for k in (1, 2)
+    ]
+    column = jnp.concatenate(far, axis=0)
+    taught = [added_rows(even_blocks(taught[2 - k], count), near[k - 1][tok_rows:]) for k in (2, 1)]
+    near = [block[:tok_rows] for block in near]
     bit = 4
     while bit < ring.inner:
         count //= 2
         taught = [added_rows(even_blocks(t, count), ring.swap(odd_blocks(t, count), bit, 0)) for t in taught]
         bit *= 2
-
-    delta_all = jnp.concatenate([column] + ring.gather_near(column), axis=0)
-    taught = jnp.concatenate(taught, axis=0).reshape(ring.outer, tok_rows, columns)
-    blocks = list(taught)
-    delta_all, blocks[0] = lax.optimization_barrier((delta_all, blocks[0]))
-    teacher_out = ring.reduce_far(blocks).astype(BF16)
+    both = jnp.concatenate([delta, column], axis=0)
+    rest = [ring.swap(column if k < 3 else both, k, 0) for k in range(1, ring.inner)]
+    delta_all = jnp.concatenate([both, near[0], rest[0], near[1]] + rest[1:], axis=0)
+    terms = ring.reduce_far(list(jnp.concatenate(taught, axis=0).reshape(ring.outer, tok_rows, columns)))
+    delta_all, terms[0] = lax.optimization_barrier((delta_all, terms[0]))
+    teacher_out = sum(a.astype(F32) for a in terms).astype(BF16)
 
     back = hidden_grad_parts(delta_all, student_down)
     backs = [back] + from_pair(back)

time: 91.6 us -> 88.3 us (0.964)
  waiting for transfers between devices: 39.3 us -> 29.4 us
  starting transfers between devices: 33.2 us -> 39.4 us
    ppermute x28 -> x31, waiting for transfers between devices: 37.9 us -> 27.9 us  [swap(): lax.ppermute(value, 'wide', [(i, i ^ flip) for i in range(self.size)])]
    ppermute x3, starting transfers between devices: 3.72 us -> 7.31 us  [from_pair(): lax.ppermute(value, 'dp', [(i, (i + s) % size) for i in range(size)])]
    ppermute x28 -> x31, starting transfers between devices: 29.4 us -> 32.1 us  [swap(): lax.ppermute(value, 'wide', [(i, i ^ flip) for i in range(self.size)])]
  transfers between devices with their start and end apart: 31 -> 34, of which waited for: 15 -> 16; matrix products, arithmetic and copies ran while one was open for 1% -> 2% of each run, Pallas kernels for 8% -> 8%
where the time goes in v4:
time: 88.3 us; the launch traced here: 87.8 us
  starting transfers between devices  39.4 us (45%)
  waiting for transfers between devices  29.4 us (33%)
  Pallas kernels  16.5 us (19%)
  other arithmetic  1.08 us (1%)
  between operations  1.05 us (1%)
    ppermute x31, starting transfers between devices, swap(): lax.ppermute(value, 'wide', [(i, i ^ flip) for i in range(self.size)])  32.1 us
    ppermute x31, waiting for transfers between devices, swap(): lax.ppermute(value, 'wide', [(i, i ^ flip) for i in range(self.size)])  27.9 us
    ppermute x3, starting transfers between devices, from_pair(): lax.ppermute(value, 'dp', [(i, (i + s) % size) for i in range(size)])  7.31 us
    pallas_call x2, Pallas kernels, pre_parts(): pl.pallas_call(functools.partial(pre_kernel, block), in_specs=[IN_VMEM] *...  5.26 us
    pallas_call x1, Pallas kernels, grad_pre_of(): pl.pallas_call(functools.partial(grad_pre_kernel, len(pres), block), in_s...  3.25 us
    pallas_call x1, Pallas kernels, grad_down_of(): pl.pallas_call(functools.partial(grad_down_kernel, block), in_specs=[IN_V...  2.14 us
    pallas_call x1, Pallas kernels, teacher_parts(): pl.pallas_call(functools.partial(teacher_kernel, len(pres), inner, owners...  1.92 us
  transfers between devices with their start and end apart: 34, of which 16 were waited for; matrix products, arithmetic and copies ran while one was open for 2% of the time, Pallas kernels for 8%

profile of v4, /device:TPU:1, one launch (start us, length us, event | category | flops | bytes accessed | tf_op | source)
XLA Modules:
  0.0 87.8 jit_solution(1976182632923354269)
XLA Ops:
  0.6 0.0 slice-start
  0.6 0.0 slice-start.2
  0.7 1.7 %payload.1 = bf16[16,2176]{1,0:T(8,128)(2,1)} custom-call(bf16[16,2048]{1,0:T(8,128)(2,1)} %layer_hbm.1, s32[8,16]{1,0:T(8,128)} %bitcast.32, f32[8,16]{1,0:T(8,128)} %bitcast.33), custom_call_target="tpu_custom_call" | custom-call | tf_op jit(solution)/shard_map/payload/pallas_call | solution.py:114
  2.4 0.0 slice-start.3
  2.4 4.2 %collective-permute-start = (bf16[16,2176]{1,0:T(8,128)(2,1)}, bf16[16,2176]{1,0:T(8,128)(2,1)S(1)}, u32[]{:S(2)}, u32[]{:S(2)}) collective-permute-start(bf16[16,2176]{1,0:T(8,128)(2,1)} %payload.1), channel_id=1, source_target_pairs={{0,12},{1,13},{2,14},{3,15},{4,8},{5,9},{6,10},{7,11},{8,4},{9,5},... | collective-permute-start | bytes 208904 | tf_op jit(solution)/shard_map/ppermute | solution.py:55
  6.6 0.4 collective-permute-start.1
  7.0 1.6 %collective-permute-done.in_ref = bf16[16,2176]{1,0:T(8,128)(2,1)S(1)} collective-permute-done((bf16[16,2176]{1,0:T(8,128)(2,1)}, bf16[16,2176]{1,0:T(8,128)(2,1)S(1)}, u32[]{:S(2)}, u32[]{:S(2)}) %collective-permute-start) | collective-permute-done | bytes 69664 | tf_op jit(solution)/shard_map/ppermute | solution.py:55
  8.6 2.2 %collective-permute-start.7 = (bf16[16,2176]{1,0:T(8,128)(2,1)S(1)}, bf16[16,2176]{1,0:T(8,128)(2,1)S(1)}, u32[]{:S(2)}, u32[]{:S(2)}) collective-permute-start(bf16[16,2176]{1,0:T(8,128)(2,1)S(1)} %copy-done.4), channel_id=1, source_target_pairs={{0,3},{1,2},{2,1},{3,0},{4,7},{5,6},{6,5},{7,4},{8,11},{9,10},{10,... | collective-permute-start | bytes 208904 | tf_op jit(solution)/shard_map/ppermute | solution.py:55
  10.8 0.2 collective-permute-start.5
  11.0 0.3 collective-permute-start.3
  11.3 1.4 %collective-permute-done.2 = bf16[16,2176]{1,0:T(8,128)(2,1)S(1)} collective-permute-done((bf16[16,2176]{1,0:T(8,128)(2,1)}, bf16[16,2176]{1,0:T(8,128)(2,1)S(1)}, u32[]{:S(2)}, u32[]{:S(2)}) %collective-permute-start.2) | collective-permute-done | bytes 69664 | tf_op jit(solution)/shard_map/ppermute | solution.py:55
  12.7 2.5 %collective-permute-start.8 = (bf16[48,2176]{1,0:T(8,128)(2,1)S(1)}, bf16[48,2176]{1,0:T(8,128)(2,1)S(1)}, u32[]{:S(2)}, u32[]{:S(2)}) collective-permute-start(bf16[48,2176]{1,0:T(8,128)(2,1)S(1)} %get-tuple-element.65), channel_id=1, source_target_pairs={{0,3},{1,2},{2,1},{3,0},{4,7},{5,6},{6,5},{7,4},{8,11},{9,10},{10,... | collective-permute-start | bytes 626696 | tf_op jit(solution)/shard_map/ppermute | solution.py:55
  15.2 0.2 collective-permute-start.6
  15.5 0.1 collective-permute-start.4
  15.6 9.6 %collective-permute-done.4 = bf16[48,2176]{1,0:T(8,128)(2,1)S(1)} collective-permute-done((bf16[48,2176]{1,0:T(8,128)(2,1)S(1)}, bf16[48,2176]{1,0:T(8,128)(2,1)S(1)}, u32[]{:S(2)}, u32[]{:S(2)}) %collective-permute-start.4) | collective-permute-done | bytes 208928 | tf_op jit(solution)/shard_map/ppermute | solution.py:55
  25.3 0.2 collective-permute-done.6
  25.7 3.4 %teacher_pre.1.refs_0_ = bf16[256,3072]{1,0:T(8,128)(2,1)S(1)} custom-call(bf16[256,2176]{1,0:T(8,128)(2,1)S(1)} %constant_dynamic-update-slice_fusion.3.x_ref.refs_3_.refs_4_, bf16[1536,2048]{1,0:T(8,128)(2,1)S(1)} %bitcast.24, bf16[1536,2048]{1,0:T(8,128)(2,1)S(1)} %bitcast.27), custom_call_target="tpu_custom_call" | custom-call | flops 3221225472 | bytes 14155776 | tf_op jit(solution)/shard_map/teacher_pre/pallas_call | solution.py:154
  29.2 1.5 %collective-permute-start.10 = (bf16[256,3072]{1,0:T(8,128)(2,1)S(1)}, bf16[256,3072]{1,0:T(8,128)(2,1)S(1)}, u32[]{:S(2)}, u32[]{:S(2)}) collective-permute-start(bf16[256,3072]{1,0:T(8,128)(2,1)S(1)} %teacher_pre.1.refs_0_), channel_id=1, source_target_pairs={{0,16},{16,0},{1,17},{17,1},{2,18},{18,2},{3,19},{19,3},{4,20},{20... | collective-permute-start | bytes 4718600 | tf_op jit(solution)/shard_map/ppermute | solution.py:82
  30.6 1.8 %student_pre.1.refs_0_ = f32[256,1536]{1,0:T(8,128)S(1)} custom-call(bf16[256,2176]{1,0:T(8,128)(2,1)S(1)} %constant_dynamic-update-slice_fusion.3.x_ref.refs_3_.refs_4_, bf16[768,2048]{1,0:T(8,128)(2,1)S(1)} %copy-done.2, bf16[768,2048]{1,0:T(8,128)(2,1)S(1)} %copy-done.3), custom_call_target="tpu_custom_call" | custom-call | flops 1610612736 | bytes 7077888 | tf_op jit(solution)/shard_map/student_pre/pallas_call | solution.py:154
  32.5 0.1 collective-permute-start.9
  32.6 1.1 %collective-permute-done.10.refs_1_ = bf16[256,3072]{1,0:T(8,128)(2,1)S(1)} collective-permute-done((bf16[256,3072]{1,0:T(8,128)(2,1)S(1)}, bf16[256,3072]{1,0:T(8,128)(2,1)S(1)}, u32[]{:S(2)}, u32[]{:S(2)}) %collective-permute-start.10) | collective-permute-done | bytes 1572896 | tf_op jit(solution)/shard_map/ppermute | solution.py:82
  33.7 1.9 %teacher_down.1 = (bf16[64,2048]{1,0:T(8,128)(2,1)S(1)}, bf16[64,2048]{1,0:T(8,128)(2,1)S(1)}, bf16[64,2048]{1,0:T(8,128)(2,1)S(1)}, bf16[64,2048]{1,0:T(8,128)(2,1)S(1)}) custom-call(bf16[256,3072]{1,0:T(8,128)(2,1)S(1)} %teacher_pre.1.refs_0_, bf16[256,3072]{1,0:T(8,128)(2,1)S(1)} %collective-permute-done.10.refs_1_, bf16[1536,2048]{1,0:T(8,128)(2,1)S(1)} %bitcast.21, ...), custom_call_target="tpu_custom_call" | custom-call | flops 1610612736 | bytes 10223616 | tf_op jit(solution)/shard_map/teacher_down/pallas_call | solution.py:210
  35.6 0.3 collective-permute-done.9.refs_1_
  35.9 1.0 %student_down.1 = (bf16[256,768]{1,0:T(8,128)(2,1)S(1)}, bf16[16,2048]{1,0:T(8,128)(2,1)S(1)}, bf16[48,2048]{1,0:T(8,128)(2,1)S(1)}, bf16[16,2048]{1,0:T(8,128)(...) custom-call(f32[256,1536]{1,0:T(8,128)S(1)} %student_pre.1.refs_0_, ...), custom_call_target="tpu_custom_call" | custom-call | flops 805306368 | bytes 5111808 | tf_op jit(solution)/shard_map/student_down/pallas_call | solution.py:247
  37.0 0.5 collective-permute-start.11
  37.5 1.0 %collective-permute-start.12 = (bf16[48,2048]{1,0:T(8,128)(2,1)S(1)}, bf16[48,2048]{1,0:T(8,128)(2,1)S(1)}, u32[]{:S(2)}, u32[]{:S(2)}) collective-permute-start(bf16[48,2048]{1,0:T(8,128)(2,1)S(1)} %get-tuple-element.40), channel_id=1, source_target_pairs={{0,2},{1,3},{2,0},{3,1},{4,6},{5,7},{6,4},{7,5},{8,10},{9,11},{10,... | collective-permute-start | bytes 589832 | tf_op jit(solution)/shard_map/ppermute | solution.py:55
  38.5 1.2 %collective-permute-start.13 = (bf16[48,2048]{1,0:T(8,128)(2,1)S(1)}, bf16[48,2048]{1,0:T(8,128)(2,1)S(1)}, u32[]{:S(2)}, u32[]{:S(2)}) collective-permute-start(bf16[48,2048]{1,0:T(8,128)(2,1)S(1)} %get-tuple-element.41), channel_id=1, source_target_pairs={{0,3},{1,2},{2,1},{3,0},{4,7},{5,6},{6,5},{7,4},{8,11},{9,10},{10,... | collective-permute-start | bytes 589832 | tf_op jit(solution)/shard_map/ppermute | solution.py:55
  39.7 0.5 collective-permute-start.17
  40.1 1.0 %collective-permute-start.18 = (bf16[16,2048]{1,0:T(8,128)(2,1)S(1)}, bf16[16,2048]{1,0:T(8,128)(2,1)S(1)}, u32[]{:S(2)}, u32[]{:S(2)}) collective-permute-start(bf16[16,2048]{1,0:T(8,128)(2,1)S(1)} %get-tuple-element.44), channel_id=1, source_target_pairs={{0,2},{1,3},{2,0},{3,1},{4,6},{5,7},{6,4},{7,5},{8,10},{9,11},{10,... | collective-permute-start | bytes 196616 | tf_op jit(solution)/shard_map/ppermute | solution.py:55
  41.1 2.0 %collective-permute-done.11 = bf16[48,2048]{1,0:T(8,128)(2,1)S(1)} collective-permute-done((bf16[48,2048]{1,0:T(8,128)(2,1)S(1)}, bf16[48,2048]{1,0:T(8,128)(2,1)S(1)}, u32[]{:S(2)}, u32[]{:S(2)}) %collective-permute-start.11) | collective-permute-done | bytes 196640 | tf_op jit(solution)/shard_map/ppermute | solution.py:55
  43.2 1.2 %collective-permute-start.19 = (bf16[16,2048]{1,0:T(8,128)(2,1)S(1)}, bf16[16,2048]{1,0:T(8,128)(2,1)S(1)}, u32[]{:S(2)}, u32[]{:S(2)}) collective-permute-start(bf16[16,2048]{1,0:T(8,128)(2,1)S(1)} %get-tuple-element.45), channel_id=1, source_target_pairs={{0,3},{1,2},{2,1},{3,0},{4,7},{5,6},{6,5},{7,4},{8,11},{9,10},{10,... | collective-permute-start | bytes 196616 | tf_op jit(solution)/shard_map/ppermute | solution.py:55
  44.3 3.1 %collective-permute-done.13 = bf16[48,2048]{1,0:T(8,128)(2,1)S(1)} collective-permute-done((bf16[48,2048]{1,0:T(8,128)(2,1)S(1)}, bf16[48,2048]{1,0:T(8,128)(2,1)S(1)}, u32[]{:S(2)}, u32[]{:S(2)}) %collective-permute-start.13) | collective-permute-done | bytes 196640 | tf_op jit(solution)/shard_map/ppermute | solution.py:55
  47.5 0.1 add_convert_fusion.2
  47.6 1.3 %collective-permute-start.14 = (bf16[16,2048]{1,0:T(8,128)(2,1)S(1)}, bf16[16,2048]{1,0:T(8,128)(2,1)S(1)}, u32[]{:S(2)}, u32[]{:S(2)}) collective-permute-start(bf16[16,2048]{1,0:T(8,128)(2,1)S(1)} %get-tuple-element.58), channel_id=1, source_target_pairs={{0,4},{1,5},{2,6},{3,7},{4,0},{5,1},{6,2},{7,3},{8,12},{9,13},{10,... | collective-permute-start | bytes 196616 | tf_op jit(solution)/shard_map/ppermute | solution.py:55
  48.8 2.1 %collective-permute-start.16 = (bf16[16,2048]{1,0:T(8,128)(2,1)S(1)}, bf16[16,2048]{1,0:T(8,128)(2,1)S(1)}, u32[]{:S(2)}, u32[]{:S(2)}) collective-permute-start(bf16[16,2048]{1,0:T(8,128)(2,1)S(1)} %get-tuple-element.59), channel_id=1, source_target_pairs={{0,12},{1,13},{2,14},{3,15},{4,8},{5,9},{6,10},{7,11},{8,4},{9,5},... | collective-permute-start | bytes 196616 | tf_op jit(solution)/shard_map/ppermute | solution.py:55
  51.0 0.2 collective-permute-start.15
  51.2 0.5 collective-permute-start.20
  51.7 1.1 %collective-permute-start.21 = (bf16[64,2048]{1,0:T(8,128)(2,1)S(1)}, bf16[64,2048]{1,0:T(8,128)(2,1)S(1)}, u32[]{:S(2)}, u32[]{:S(2)}) collective-permute-start(bf16[64,2048]{1,0:T(8,128)(2,1)S(1)} %get-tuple-element.47.refs_6_), channel_id=1, source_target_pairs={{0,2},{1,3},{2,0},{3,1},{4,6},{5,7},{6,4},{7,5},{8,10},{9,11},{10,... | collective-permute-start | bytes 786440 | tf_op jit(solution)/shard_map/ppermute | solution.py:55
  52.8 1.0 %collective-permute-done.16 = bf16[16,2048]{1,0:T(8,128)(2,1)S(1)} collective-permute-done((bf16[16,2048]{1,0:T(8,128)(2,1)S(1)}, bf16[16,2048]{1,0:T(8,128)(2,1)S(1)}, u32[]{:S(2)}, u32[]{:S(2)}) %collective-permute-start.16) | collective-permute-done | bytes 65568 | tf_op jit(solution)/shard_map/ppermute | solution.py:55
  53.8 2.1 %collective-permute-done.15 = bf16[16,2048]{1,0:T(8,128)(2,1)S(1)} collective-permute-done((bf16[16,2048]{1,0:T(8,128)(2,1)S(1)}, bf16[16,2048]{1,0:T(8,128)(2,1)S(1)}, u32[]{:S(2)}, u32[]{:S(2)}) %collective-permute-start.15) | collective-permute-done | bytes 65568 | tf_op jit(solution)/shard_map/ppermute | solution.py:55
  55.9 0.1 multiply_convert_fusion
  56.0 0.7 collective-permute-done.20
  56.7 0.5 collective-permute-done.21
  57.2 2.1 %collective-permute-start.24 = (bf16[16,2048]{1,0:T(8,128)(2,1)S(1)}, bf16[16,2048]{1,0:T(8,128)(2,1)S(1)}, u32[]{:S(2)}, u32[]{:S(2)}) collective-permute-start(bf16[16,2048]{1,0:T(8,128)(2,1)S(1)} %multiply_convert_fusion), channel_id=1, source_target_pairs={{0,12},{1,13},{2,14},{3,15},{4,8},{5,9},{6,10},{7,11},{8,4},{9,5},... | collective-permute-start | bytes 196616 | tf_op jit(solution)/shard_map/ppermute | solution.py:55
  59.3 0.0 collective-permute-start.23
  59.4 1.4 %collective-permute-start.22 = (bf16[16,2048]{1,0:T(8,128)(2,1)S(1)}, bf16[16,2048]{1,0:T(8,128)(2,1)S(1)}, u32[]{:S(2)}, u32[]{:S(2)}) collective-permute-start(bf16[16,2048]{1,0:T(8,128)(2,1)S(1)} %multiply_convert_fusion), channel_id=1, source_target_pairs={{0,4},{1,5},{2,6},{3,7},{4,0},{5,1},{6,2},{7,3},{8,12},{9,13},{10,... | collective-permute-start | bytes 196616 | tf_op jit(solution)/shard_map/ppermute | solution.py:55
  60.8 0.1 add_convert_fusion
  61.0 1.2 %collective-permute-start.27 = (bf16[48,2048]{1,0:T(8,128)(2,1)S(1)}, bf16[48,2048]{1,0:T(8,128)(2,1)S(1)}, u32[]{:S(2)}, u32[]{:S(2)}) collective-permute-start(bf16[48,2048]{1,0:T(8,128)(2,1)S(1)} %get-tuple-element.77), channel_id=1, source_target_pairs={{0,2},{1,3},{2,0},{3,1},{4,6},{5,7},{6,4},{7,5},{8,10},{9,11},{10,... | collective-permute-start | bytes 589832 | tf_op jit(solution)/shard_map/ppermute | solution.py:55
  62.1 0.5 collective-permute-start.25
  62.6 0.3 collective-permute-done.22
  62.9 1.1 %collective-permute-done.23 = bf16[16,2048]{1,0:T(8,128)(2,1)S(1)} collective-permute-done((bf16[16,2048]{1,0:T(8,128)(2,1)S(1)}, bf16[16,2048]{1,0:T(8,128)(2,1)S(1)}, u32[]{:S(2)}, u32[]{:S(2)}) %collective-permute-start.23) | collective-permute-done | bytes 65568 | tf_op jit(solution)/shard_map/ppermute | solution.py:55
  64.1 1.2 %collective-permute-start.28 = (bf16[48,2048]{1,0:T(8,128)(2,1)S(1)}, bf16[48,2048]{1,0:T(8,128)(2,1)S(1)}, u32[]{:S(2)}, u32[]{:S(2)}) collective-permute-start(bf16[48,2048]{1,0:T(8,128)(2,1)S(1)} %get-tuple-element.71), channel_id=1, source_target_pairs={{0,2},{1,3},{2,0},{3,1},{4,6},{5,7},{6,4},{7,5},{8,10},{9,11},{10,... | collective-permute-start | bytes 589832 | tf_op jit(solution)/shard_map/ppermute | solution.py:55
  65.3 0.2 collective-permute-start.26
  65.5 1.4 %collective-permute-start.29 = (bf16[64,2048]{1,0:T(8,128)(2,1)S(1)}, bf16[64,2048]{1,0:T(8,128)(2,1)S(1)}, u32[]{:S(2)}, u32[]{:S(2)}) collective-permute-start(bf16[64,2048]{1,0:T(8,128)(2,1)S(1)} %pad_maximum_fusion), channel_id=1, source_target_pairs={{0,3},{1,2},{2,1},{3,0},{4,7},{5,6},{6,5},{7,4},{8,11},{9,10},{10,... | collective-permute-start | bytes 786440 | tf_op jit(solution)/shard_map/ppermute | solution.py:55
  67.0 0.1 collective-permute-start.30
  67.1 1.9 %collective-permute-start.31 = (bf16[16,2048]{1,0:T(8,128)(2,1)S(1)}, bf16[16,2048]{1,0:T(8,128)(2,1)S(1)}, u32[]{:S(2)}, u32[]{:S(2)}) collective-permute-start(bf16[16,2048]{1,0:T(8,128)(2,1)S(1)} %get-tuple-element.63), channel_id=1, source_target_pairs={{0,8},{1,9},{2,10},{3,11},{4,12},{5,13},{6,14},{7,15},{8,0},{9,1},... | collective-permute-start | bytes 196616 | tf_op jit(solution)/shard_map/ppermute | solution.py:55
  69.0 1.1 %collective-permute-done.26 = bf16[48,2048]{1,0:T(8,128)(2,1)S(1)} collective-permute-done((bf16[48,2048]{1,0:T(8,128)(2,1)S(1)}, bf16[48,2048]{1,0:T(8,128)(2,1)S(1)}, u32[]{:S(2)}, u32[]{:S(2)}) %collective-permute-start.26) | collective-permute-done | bytes 196640 | tf_op jit(solution)/shard_map/ppermute | solution.py:55
  70.1 1.5 %collective-permute-start.32 = (bf16[16,2048]{1,0:T(8,128)(2,1)S(1)}, bf16[16,2048]{1,0:T(8,128)(2,1)S(1)}, u32[]{:S(2)}, u32[]{:S(2)}) collective-permute-start(bf16[16,2048]{1,0:T(8,128)(2,1)S(1)} %get-tuple-element.64), channel_id=1, source_target_pairs={{0,12},{1,13},{2,14},{3,15},{4,8},{5,9},{6,10},{7,11},{8,4},{9,5},... | collective-permute-start | bytes 196616 | tf_op jit(solution)/shard_map/ppermute | solution.py:55
  71.7 3.0 %collective-permute-done.29 = bf16[64,2048]{1,0:T(8,128)(2,1)S(1)} collective-permute-done((bf16[64,2048]{1,0:T(8,128)(2,1)S(1)}, bf16[64,2048]{1,0:T(8,128)(2,1)S(1)}, u32[]{:S(2)}, u32[]{:S(2)}) %collective-permute-start.29) | collective-permute-done | bytes 262176 | tf_op jit(solution)/shard_map/ppermute | solution.py:55
  74.7 1.3 %hidden_grad.1.refs_2_ = bf16[256,768]{1,0:T(8,128)(2,1)S(1)} custom-call(bf16[256,2048]{1,0:T(8,128)(2,1)S(1)} %constant_dynamic-update-slice_fusion.16.delta_ref, bf16[768,2048]{1,0:T(8,128)(2,1)S(1)} %copy-done), custom_call_target="tpu_custom_call" | custom-call | flops 805306368 | bytes 4194304 | tf_op jit(solution)/shard_map/hidden_grad/pallas_call | solution.py:270
  76.0 5.7 %collective-permute-start.33 = (bf16[256,768]{1,0:T(8,128)(2,1)S(1)}, bf16[256,768]{1,0:T(8,128)(2,1)S(1)}, u32[]{:S(2)}, u32[]{:S(2)}) collective-permute-start(bf16[256,768]{1,0:T(8,128)(2,1)S(1)} %hidden_grad.1.refs_2_), channel_id=1, source_target_pairs={{0,16},{16,0},{1,17},{17,1},{2,18},{18,2},{3,19},{19,3},{4,20},{20... | collective-permute-start | bytes 1179656 | tf_op jit(solution)/shard_map/ppermute | solution.py:82
  81.7 2.1 %grad_down.1 = bf16[768,2048]{1,0:T(8,128)(2,1)} custom-call(bf16[256,768]{1,0:T(8,128)(2,1)S(1)} %get-tuple-element.57.hidden_ref, bf16[256,2048]{1,0:T(8,128)(2,1)S(1)} %constant_dynamic-update-slice_fusion.16.delta_ref), custom_call_target="tpu_custom_call" | custom-call | flops 805306368 | bytes 4194304 | tf_op jit(solution)/shard_map/grad_down/pallas_call | solution.py:295
  83.9 0.7 add_convert_fusion.3
  84.6 3.3 %grad_gate_up.1 = (bf16[768,2048]{1,0:T(8,128)(2,1)}, bf16[768,2048]{1,0:T(8,128)(2,1)}) custom-call(f32[256,1536]{1,0:T(8,128)S(1)} %student_pre.1.refs_0_, f32[256,1536]{1,0:T(8,128)S(1)} %collective-permute-done.9.refs_1_, bf16[256,768]{1,0:T(8,128)(2,1)S(1)} %hidden_grad.1.refs_2_, bf16[256,768]{1,0:T(8,128)(2,1)S(1)} %collective-permute-done.33.refs_3_, ...), custom_call_target="tpu_custom_call" | custom-call | flops 1610612736 | bytes 7340032 | tf_op jit(solution)/shard_map/grad_gate_up/pallas_call | solution.py:331
  (65 shorter events, 0.5 us)
Async XLA Ops:
  0.6 25.0 %slice-start = ((s8[6291456]{0:T(1024)(128)(4,1)}), s8[2097152]{0:T(1024)(128)(4,1)S(1)}, s32[]{:S(2)}) async-start(s8[6291456]{0:T(1024)(128)(4,1)} %bitcast.22), calls=%async_computation | async-start | bytes 4194304
  0.6 25.0 %slice-start.2 = ((s8[6291456]{0:T(1024)(128)(4,1)}), s8[4194304]{0:T(1024)(128)(4,1)S(1)}, s32[]{:S(2)}) async-start(s8[6291456]{0:T(1024)(128)(4,1)} %bitcast.25), calls=%async_computation.2 | async-start | bytes 8388608
  2.3 6.2 %copy-start.4 = (bf16[16,2176]{1,0:T(8,128)(2,1)S(1)}, bf16[16,2176]{1,0:T(8,128)(2,1)}, u32[]{:S(2)}) copy-start(bf16[16,2176]{1,0:T(8,128)(2,1)} %payload.1) | copy-start | bytes 208900
  2.4 23.3 %slice-start.1 = ((s8[6291456]{0:T(1024)(128)(4,1)}), s8[4194304]{0:T(1024)(128)(4,1)S(1)}, s32[]{:S(2)}) async-start(s8[6291456]{0:T(1024)(128)(4,1)} %bitcast.22), calls=%async_computation.1 | async-start | bytes 8388608
  2.4 23.3 %slice-start.3 = ((s8[6291456]{0:T(1024)(128)(4,1)}), s8[2097152]{0:T(1024)(128)(4,1)S(1)}, s32[]{:S(2)}) async-start(s8[6291456]{0:T(1024)(128)(4,1)} %bitcast.25), calls=%async_computation.3 | async-start | bytes 4194304
  2.4 6.2 %collective-permute-start = (bf16[16,2176]{1,0:T(8,128)(2,1)}, bf16[16,2176]{1,0:T(8,128)(2,1)S(1)}, u32[]{:S(2)}, u32[]{:S(2)}) collective-permute-start(bf16[16,2176]{1,0:T(8,128)(2,1)} %payload.1), channel_id=1, source_target_pairs={{0,12},{1,13},{2,14},{3,15},{4,8},{5,9},{6,10},{7,11},{8,4},{9,5},... | collective-permute-start | bytes 208904 | tf_op jit(solution)/shard_map/ppermute | solution.py:55
  6.6 6.1 %collective-permute-start.2 = (bf16[16,2176]{1,0:T(8,128)(2,1)}, bf16[16,2176]{1,0:T(8,128)(2,1)S(1)}, u32[]{:S(2)}, u32[]{:S(2)}) collective-permute-start(bf16[16,2176]{1,0:T(8,128)(2,1)} %payload.1), channel_id=1, source_target_pairs={{0,8},{1,9},{2,10},{3,11},{4,12},{5,13},{6,14},{7,15},{8,0},{9,1},... | collective-permute-start | bytes 208904 | tf_op jit(solution)/shard_map/ppermute | solution.py:55
  6.6 4.7 %collective-permute-start.1 = (bf16[16,2176]{1,0:T(8,128)(2,1)}, bf16[16,2176]{1,0:T(8,128)(2,1)S(1)}, u32[]{:S(2)}, u32[]{:S(2)}) collective-permute-start(bf16[16,2176]{1,0:T(8,128)(2,1)} %payload.1), channel_id=1, source_target_pairs={{0,4},{1,5},{2,6},{3,7},{4,0},{5,1},{6,2},{7,3},{8,12},{9,13},{10,... | collective-permute-start | bytes 208904 | tf_op jit(solution)/shard_map/ppermute | solution.py:55
  8.6 17.0 %collective-permute-start.7 = (bf16[16,2176]{1,0:T(8,128)(2,1)S(1)}, bf16[16,2176]{1,0:T(8,128)(2,1)S(1)}, u32[]{:S(2)}, u32[]{:S(2)}) collective-permute-start(bf16[16,2176]{1,0:T(8,128)(2,1)S(1)} %copy-done.4), channel_id=1, source_target_pairs={{0,3},{1,2},{2,1},{3,0},{4,7},{5,6},{6,5},{7,4},{8,11},{9,10},{10,... | collective-permute-start | bytes 208904 | tf_op jit(solution)/shard_map/ppermute | solution.py:55
  10.8 14.5 %collective-permute-start.5 = (bf16[16,2176]{1,0:T(8,128)(2,1)S(1)}, bf16[16,2176]{1,0:T(8,128)(2,1)S(1)}, u32[]{:S(2)}, u32[]{:S(2)}) collective-permute-start(bf16[16,2176]{1,0:T(8,128)(2,1)S(1)} %copy-done.4), channel_id=1, source_target_pairs={{0,2},{1,3},{2,0},{3,1},{4,6},{5,7},{6,4},{7,5},{8,10},{9,11},{10,... | collective-permute-start | bytes 208904 | tf_op jit(solution)/shard_map/ppermute | solution.py:55
  11.0 4.4 %collective-permute-start.3 = (bf16[16,2176]{1,0:T(8,128)(2,1)S(1)}, bf16[16,2176]{1,0:T(8,128)(2,1)S(1)}, u32[]{:S(2)}, u32[]{:S(2)}) collective-permute-start(bf16[16,2176]{1,0:T(8,128)(2,1)S(1)} %copy-done.4), channel_id=1, source_target_pairs={{0,1},{1,0},{2,3},{3,2},{4,5},{5,4},{6,7},{7,6},{8,9},{9,8},{10,11... | collective-permute-start | bytes 208904 | tf_op jit(solution)/shard_map/ppermute | solution.py:55
  12.7 12.9 %collective-permute-start.8 = (bf16[48,2176]{1,0:T(8,128)(2,1)S(1)}, bf16[48,2176]{1,0:T(8,128)(2,1)S(1)}, u32[]{:S(2)}, u32[]{:S(2)}) collective-permute-start(bf16[48,2176]{1,0:T(8,128)(2,1)S(1)} %get-tuple-element.65), channel_id=1, source_target_pairs={{0,3},{1,2},{2,1},{3,0},{4,7},{5,6},{6,5},{7,4},{8,11},{9,10},{10,... | collective-permute-start | bytes 626696 | tf_op jit(solution)/shard_map/ppermute | solution.py:55
  15.2 10.3 %collective-permute-start.6 = (bf16[48,2176]{1,0:T(8,128)(2,1)S(1)}, bf16[48,2176]{1,0:T(8,128)(2,1)S(1)}, u32[]{:S(2)}, u32[]{:S(2)}) collective-permute-start(bf16[48,2176]{1,0:T(8,128)(2,1)S(1)} %get-tuple-element.65), channel_id=1, source_target_pairs={{0,2},{1,3},{2,0},{3,1},{4,6},{5,7},{6,4},{7,5},{8,10},{9,11},{10,... | collective-permute-start | bytes 626696 | tf_op jit(solution)/shard_map/ppermute | solution.py:55
  15.5 9.8 %collective-permute-start.4 = (bf16[48,2176]{1,0:T(8,128)(2,1)S(1)}, bf16[48,2176]{1,0:T(8,128)(2,1)S(1)}, u32[]{:S(2)}, u32[]{:S(2)}) collective-permute-start(bf16[48,2176]{1,0:T(8,128)(2,1)S(1)} %get-tuple-element.65), channel_id=1, source_target_pairs={{0,1},{1,0},{2,3},{3,2},{4,5},{5,4},{6,7},{7,6},{8,9},{9,8},{10,11... | collective-permute-start | bytes 626696 | tf_op jit(solution)/shard_map/ppermute | solution.py:55
  25.7 5.0 %copy-start.2 = (bf16[768,2048]{1,0:T(8,128)(2,1)S(1)}, bf16[768,2048]{1,0:T(8,128)(2,1)}, u32[]{:S(2)}) copy-start(bf16[768,2048]{1,0:T(8,128)(2,1)} %gate_ref.1) | copy-start | bytes 9437188
  25.7 4.9 %copy-start.3 = (bf16[768,2048]{1,0:T(8,128)(2,1)S(1)}, bf16[768,2048]{1,0:T(8,128)(2,1)}, u32[]{:S(2)}) copy-start(bf16[768,2048]{1,0:T(8,128)(2,1)} %up_ref.1) | copy-start | bytes 9437188
  29.2 4.5 %collective-permute-start.10 = (bf16[256,3072]{1,0:T(8,128)(2,1)S(1)}, bf16[256,3072]{1,0:T(8,128)(2,1)S(1)}, u32[]{:S(2)}, u32[]{:S(2)}) collective-permute-start(bf16[256,3072]{1,0:T(8,128)(2,1)S(1)} %teacher_pre.1.refs_0_), channel_id=1, source_target_pairs={{0,16},{16,0},{1,17},{17,1},{2,18},{18,2},{3,19},{19,3},{4,20},{20... | collective-permute-start | bytes 4718600 | tf_op jit(solution)/shard_map/ppermute | solution.py:82
  30.6 3.0 %copy-start.1 = (bf16[1,1536,2048]{2,1,0:T(8,128)(2,1)S(1)}, bf16[1,1536,2048]{2,1,0:T(8,128)(2,1)}, u32[]{:S(2)}) copy-start(bf16[1,1536,2048]{2,1,0:T(8,128)(2,1)} %param.14) | copy-start | bytes 18874372
  32.5 3.5 %collective-permute-start.9 = (f32[256,1536]{1,0:T(8,128)S(1)}, f32[256,1536]{1,0:T(8,128)S(1)}, u32[]{:S(2)}, u32[]{:S(2)}) collective-permute-start(f32[256,1536]{1,0:T(8,128)S(1)} %student_pre.1.refs_0_), channel_id=1, source_target_pairs={{0,16},{16,0},{1,17},{17,1},{2,18},{18,2},{3,19},{19,3},{4,20},{20... | collective-permute-start | bytes 4718600 | tf_op jit(solution)/shard_map/ppermute | solution.py:82
  33.7 2.3 %copy-start = (bf16[768,2048]{1,0:T(8,128)(2,1)S(1)}, bf16[768,2048]{1,0:T(8,128)(2,1)}, u32[]{:S(2)}) copy-start(bf16[768,2048]{1,0:T(8,128)(2,1)} %down_ref.1) | copy-start | bytes 9437188
  37.0 6.2 %collective-permute-start.11 = (bf16[48,2048]{1,0:T(8,128)(2,1)S(1)}, bf16[48,2048]{1,0:T(8,128)(2,1)S(1)}, u32[]{:S(2)}, u32[]{:S(2)}) collective-permute-start(bf16[48,2048]{1,0:T(8,128)(2,1)S(1)} %get-tuple-element.39), channel_id=1, source_target_pairs={{0,1},{1,0},{2,3},{3,2},{4,5},{5,4},{6,7},{7,6},{8,9},{9,8},{10,11... | collective-permute-start | bytes 589832 | tf_op jit(solution)/shard_map/ppermute | solution.py:55
  37.5 6.8 %collective-permute-start.12 = (bf16[48,2048]{1,0:T(8,128)(2,1)S(1)}, bf16[48,2048]{1,0:T(8,128)(2,1)S(1)}, u32[]{:S(2)}, u32[]{:S(2)}) collective-permute-start(bf16[48,2048]{1,0:T(8,128)(2,1)S(1)} %get-tuple-element.40), channel_id=1, source_target_pairs={{0,2},{1,3},{2,0},{3,1},{4,6},{5,7},{6,4},{7,5},{8,10},{9,11},{10,... | collective-permute-start | bytes 589832 | tf_op jit(solution)/shard_map/ppermute | solution.py:55
  38.5 9.0 %collective-permute-start.13 = (bf16[48,2048]{1,0:T(8,128)(2,1)S(1)}, bf16[48,2048]{1,0:T(8,128)(2,1)S(1)}, u32[]{:S(2)}, u32[]{:S(2)}) collective-permute-start(bf16[48,2048]{1,0:T(8,128)(2,1)S(1)} %get-tuple-element.41), channel_id=1, source_target_pairs={{0,3},{1,2},{2,1},{3,0},{4,7},{5,6},{6,5},{7,4},{8,11},{9,10},{10,... | collective-permute-start | bytes 589832 | tf_op jit(solution)/shard_map/ppermute | solution.py:55
  39.7 11.3 %collective-permute-start.17 = (bf16[16,2048]{1,0:T(8,128)(2,1)S(1)}, bf16[16,2048]{1,0:T(8,128)(2,1)S(1)}, u32[]{:S(2)}, u32[]{:S(2)}) collective-permute-start(bf16[16,2048]{1,0:T(8,128)(2,1)S(1)} %get-tuple-element.43), channel_id=1, source_target_pairs={{0,1},{1,0},{2,3},{3,2},{4,5},{5,4},{6,7},{7,6},{8,9},{9,8},{10,11... | collective-permute-start | bytes 196616 | tf_op jit(solution)/shard_map/ppermute | solution.py:55
  40.1 11.0 %collective-permute-start.18 = (bf16[16,2048]{1,0:T(8,128)(2,1)S(1)}, bf16[16,2048]{1,0:T(8,128)(2,1)S(1)}, u32[]{:S(2)}, u32[]{:S(2)}) collective-permute-start(bf16[16,2048]{1,0:T(8,128)(2,1)S(1)} %get-tuple-element.44), channel_id=1, source_target_pairs={{0,2},{1,3},{2,0},{3,1},{4,6},{5,7},{6,4},{7,5},{8,10},{9,11},{10,... | collective-permute-start | bytes 196616 | tf_op jit(solution)/shard_map/ppermute | solution.py:55
  43.2 8.5 %collective-permute-start.19 = (bf16[16,2048]{1,0:T(8,128)(2,1)S(1)}, bf16[16,2048]{1,0:T(8,128)(2,1)S(1)}, u32[]{:S(2)}, u32[]{:S(2)}) collective-permute-start(bf16[16,2048]{1,0:T(8,128)(2,1)S(1)} %get-tuple-element.45), channel_id=1, source_target_pairs={{0,3},{1,2},{2,1},{3,0},{4,7},{5,6},{6,5},{7,4},{8,11},{9,10},{10,... | collective-permute-start | bytes 196616 | tf_op jit(solution)/shard_map/ppermute | solution.py:55
  47.6 5.2 %collective-permute-start.14 = (bf16[16,2048]{1,0:T(8,128)(2,1)S(1)}, bf16[16,2048]{1,0:T(8,128)(2,1)S(1)}, u32[]{:S(2)}, u32[]{:S(2)}) collective-permute-start(bf16[16,2048]{1,0:T(8,128)(2,1)S(1)} %get-tuple-element.58), channel_id=1, source_target_pairs={{0,4},{1,5},{2,6},{3,7},{4,0},{5,1},{6,2},{7,3},{8,12},{9,13},{10,... | collective-permute-start | bytes 196616 | tf_op jit(solution)/shard_map/ppermute | solution.py:55
  48.8 5.0 %collective-permute-start.16 = (bf16[16,2048]{1,0:T(8,128)(2,1)S(1)}, bf16[16,2048]{1,0:T(8,128)(2,1)S(1)}, u32[]{:S(2)}, u32[]{:S(2)}) collective-permute-start(bf16[16,2048]{1,0:T(8,128)(2,1)S(1)} %get-tuple-element.59), channel_id=1, source_target_pairs={{0,12},{1,13},{2,14},{3,15},{4,8},{5,9},{6,10},{7,11},{8,4},{9,5},... | collective-permute-start | bytes 196616 | tf_op jit(solution)/shard_map/ppermute | solution.py:55
  51.0 4.9 %collective-permute-start.15 = (bf16[16,2048]{1,0:T(8,128)(2,1)S(1)}, bf16[16,2048]{1,0:T(8,128)(2,1)S(1)}, u32[]{:S(2)}, u32[]{:S(2)}) collective-permute-start(bf16[16,2048]{1,0:T(8,128)(2,1)S(1)} %get-tuple-element.60), channel_id=1, source_target_pairs={{0,8},{1,9},{2,10},{3,11},{4,12},{5,13},{6,14},{7,15},{8,0},{9,1},... | collective-permute-start | bytes 196616 | tf_op jit(solution)/shard_map/ppermute | solution.py:55
  51.2 5.5 %collective-permute-start.20 = (bf16[64,2048]{1,0:T(8,128)(2,1)S(1)}, bf16[64,2048]{1,0:T(8,128)(2,1)S(1)}, u32[]{:S(2)}, u32[]{:S(2)}) collective-permute-start(bf16[64,2048]{1,0:T(8,128)(2,1)S(1)} %get-tuple-element.46.refs_4_), channel_id=1, source_target_pairs={{0,1},{1,0},{2,3},{3,2},{4,5},{5,4},{6,7},{7,6},{8,9},{9,8},{10,11... | collective-permute-start | bytes 786440 | tf_op jit(solution)/shard_map/ppermute | solution.py:55
  51.7 5.5 %collective-permute-start.21 = (bf16[64,2048]{1,0:T(8,128)(2,1)S(1)}, bf16[64,2048]{1,0:T(8,128)(2,1)S(1)}, u32[]{:S(2)}, u32[]{:S(2)}) collective-permute-start(bf16[64,2048]{1,0:T(8,128)(2,1)S(1)} %get-tuple-element.47.refs_6_), channel_id=1, source_target_pairs={{0,2},{1,3},{2,0},{3,1},{4,6},{5,7},{6,4},{7,5},{8,10},{9,11},{10,... | collective-permute-start | bytes 786440 | tf_op jit(solution)/shard_map/ppermute | solution.py:55
  57.2 6.9 %collective-permute-start.24 = (bf16[16,2048]{1,0:T(8,128)(2,1)S(1)}, bf16[16,2048]{1,0:T(8,128)(2,1)S(1)}, u32[]{:S(2)}, u32[]{:S(2)}) collective-permute-start(bf16[16,2048]{1,0:T(8,128)(2,1)S(1)} %multiply_convert_fusion), channel_id=1, source_target_pairs={{0,12},{1,13},{2,14},{3,15},{4,8},{5,9},{6,10},{7,11},{8,4},{9,5},... | collective-permute-start | bytes 196616 | tf_op jit(solution)/shard_map/ppermute | solution.py:55
  59.3 4.7 %collective-permute-start.23 = (bf16[16,2048]{1,0:T(8,128)(2,1)S(1)}, bf16[16,2048]{1,0:T(8,128)(2,1)S(1)}, u32[]{:S(2)}, u32[]{:S(2)}) collective-permute-start(bf16[16,2048]{1,0:T(8,128)(2,1)S(1)} %multiply_convert_fusion), channel_id=1, source_target_pairs={{0,8},{1,9},{2,10},{3,11},{4,12},{5,13},{6,14},{7,15},{8,0},{9,1},... | collective-permute-start | bytes 196616 | tf_op jit(solution)/shard_map/ppermute | solution.py:55
  59.4 3.6 %collective-permute-start.22 = (bf16[16,2048]{1,0:T(8,128)(2,1)S(1)}, bf16[16,2048]{1,0:T(8,128)(2,1)S(1)}, u32[]{:S(2)}, u32[]{:S(2)}) collective-permute-start(bf16[16,2048]{1,0:T(8,128)(2,1)S(1)} %multiply_convert_fusion), channel_id=1, source_target_pairs={{0,4},{1,5},{2,6},{3,7},{4,0},{5,1},{6,2},{7,3},{8,12},{9,13},{10,... | collective-permute-start | bytes 196616 | tf_op jit(solution)/shard_map/ppermute | solution.py:55
  61.0 5.9 %collective-permute-start.27 = (bf16[48,2048]{1,0:T(8,128)(2,1)S(1)}, bf16[48,2048]{1,0:T(8,128)(2,1)S(1)}, u32[]{:S(2)}, u32[]{:S(2)}) collective-permute-start(bf16[48,2048]{1,0:T(8,128)(2,1)S(1)} %get-tuple-element.77), channel_id=1, source_target_pairs={{0,2},{1,3},{2,0},{3,1},{4,6},{5,7},{6,4},{7,5},{8,10},{9,11},{10,... | collective-permute-start | bytes 589832 | tf_op jit(solution)/shard_map/ppermute | solution.py:55
  62.1 4.9 %collective-permute-start.25 = (bf16[48,2048]{1,0:T(8,128)(2,1)S(1)}, bf16[48,2048]{1,0:T(8,128)(2,1)S(1)}, u32[]{:S(2)}, u32[]{:S(2)}) collective-permute-start(bf16[48,2048]{1,0:T(8,128)(2,1)S(1)} %get-tuple-element.78), channel_id=1, source_target_pairs={{0,1},{1,0},{2,3},{3,2},{4,5},{5,4},{6,7},{7,6},{8,9},{9,8},{10,11... | collective-permute-start | bytes 589832 | tf_op jit(solution)/shard_map/ppermute | solution.py:55
  64.1 7.5 %collective-permute-start.28 = (bf16[48,2048]{1,0:T(8,128)(2,1)S(1)}, bf16[48,2048]{1,0:T(8,128)(2,1)S(1)}, u32[]{:S(2)}, u32[]{:S(2)}) collective-permute-start(bf16[48,2048]{1,0:T(8,128)(2,1)S(1)} %get-tuple-element.71), channel_id=1, source_target_pairs={{0,2},{1,3},{2,0},{3,1},{4,6},{5,7},{6,4},{7,5},{8,10},{9,11},{10,... | collective-permute-start | bytes 589832 | tf_op jit(solution)/shard_map/ppermute | solution.py:55
  65.3 4.8 %collective-permute-start.26 = (bf16[48,2048]{1,0:T(8,128)(2,1)S(1)}, bf16[48,2048]{1,0:T(8,128)(2,1)S(1)}, u32[]{:S(2)}, u32[]{:S(2)}) collective-permute-start(bf16[48,2048]{1,0:T(8,128)(2,1)S(1)} %get-tuple-element.71), channel_id=1, source_target_pairs={{0,1},{1,0},{2,3},{3,2},{4,5},{5,4},{6,7},{7,6},{8,9},{9,8},{10,11... | collective-permute-start | bytes 589832 | tf_op jit(solution)/shard_map/ppermute | solution.py:55
  65.5 9.2 %collective-permute-start.29 = (bf16[64,2048]{1,0:T(8,128)(2,1)S(1)}, bf16[64,2048]{1,0:T(8,128)(2,1)S(1)}, u32[]{:S(2)}, u32[]{:S(2)}) collective-permute-start(bf16[64,2048]{1,0:T(8,128)(2,1)S(1)} %pad_maximum_fusion), channel_id=1, source_target_pairs={{0,3},{1,2},{2,1},{3,0},{4,7},{5,6},{6,5},{7,4},{8,11},{9,10},{10,... | collective-permute-start | bytes 786440 | tf_op jit(solution)/shard_map/ppermute | solution.py:55
  67.0 16.9 %collective-permute-start.30 = (bf16[16,2048]{1,0:T(8,128)(2,1)S(1)}, bf16[16,2048]{1,0:T(8,128)(2,1)S(1)}, u32[]{:S(2)}, u32[]{:S(2)}) collective-permute-start(bf16[16,2048]{1,0:T(8,128)(2,1)S(1)} %get-tuple-element.62), channel_id=1, source_target_pairs={{0,4},{1,5},{2,6},{3,7},{4,0},{5,1},{6,2},{7,3},{8,12},{9,13},{10,... | collective-permute-start | bytes 196616 | tf_op jit(solution)/shard_map/ppermute | solution.py:55
  67.1 16.8 %collective-permute-start.31 = (bf16[16,2048]{1,0:T(8,128)(2,1)S(1)}, bf16[16,2048]{1,0:T(8,128)(2,1)S(1)}, u32[]{:S(2)}, u32[]{:S(2)}) collective-permute-start(bf16[16,2048]{1,0:T(8,128)(2,1)S(1)} %get-tuple-element.63), channel_id=1, source_target_pairs={{0,8},{1,9},{2,10},{3,11},{4,12},{5,13},{6,14},{7,15},{8,0},{9,1},... | collective-permute-start | bytes 196616 | tf_op jit(solution)/shard_map/ppermute | solution.py:55
  70.1 13.8 %collective-permute-start.32 = (bf16[16,2048]{1,0:T(8,128)(2,1)S(1)}, bf16[16,2048]{1,0:T(8,128)(2,1)S(1)}, u32[]{:S(2)}, u32[]{:S(2)}) collective-permute-start(bf16[16,2048]{1,0:T(8,128)(2,1)S(1)} %get-tuple-element.64), channel_id=1, source_target_pairs={{0,12},{1,13},{2,14},{3,15},{4,8},{5,9},{6,10},{7,11},{8,4},{9,5},... | collective-permute-start | bytes 196616 | tf_op jit(solution)/shard_map/ppermute | solution.py:55
  76.0 8.6 %collective-permute-start.33 = (bf16[256,768]{1,0:T(8,128)(2,1)S(1)}, bf16[256,768]{1,0:T(8,128)(2,1)S(1)}, u32[]{:S(2)}, u32[]{:S(2)}) collective-permute-start(bf16[256,768]{1,0:T(8,128)(2,1)S(1)} %hidden_grad.1.refs_2_), channel_id=1, source_target_pairs={{0,16},{16,0},{1,17},{17,1},{2,18},{18,2},{3,19},{19,3},{4,20},{20... | collective-permute-start | bytes 1179656 | tf_op jit(solution)/shard_map/ppermute | solution.py:82

commit v5 on v4

--- a/solution.py
+++ b/solution.py
@@ -69,9 +69,10 @@
             blocks += [first, others]
         return jnp.concatenate(blocks, axis=0)
 
-    def reduce_near(self, pieces):
-        arrived = [pieces[0]] + [self.swap(pieces[k], k, 0) for k in range(1, self.inner)]
-        return sum(a.astype(F32) for a in arrived).astype(BF16)
+    def reduce_near(self, pieces, later):
+        arrived = [self.swap(pieces[k], k, 0) for k in range(1, self.inner)]
+        arrived[0], later = lax.optimization_barrier((arrived[0], later))
+        return sum(a.astype(F32) for a in [pieces[0]] + arrived).astype(BF16), later
 
     def reduce_far(self, blocks):
         return [blocks[0]] + [self.swap(blocks[k], 0, k) for k in range(1, self.outer)]
@@ -383,7 +384,8 @@
     student_hidden, firsts, rests = student_parts(student_pres, student_down, teacher, ring.inner, tok_rows)
 
     loss_scale = 1.0 / math.sqrt(tok_rows * owners)
-    column, teacher = lax.optimization_barrier((ring.reduce_near(rests), teacher))
+    column, firsts = ring.reduce_near(rests, firsts)
+    column, teacher = lax.optimization_barrier((column, teacher))
     arrived = [ring.swap(teacher[2 * k + 1], 1 + k, 0) for k in range(2)]
     terms = ring.reduce_far([firsts[0]] + list(column.reshape(ring.outer - 1, tok_rows, columns)))
     terms += [ring.swap(firsts[k], k, 0) for k in range(1, ring.inner)]

time: 88.3 us -> 88 us (level)
  transfers between devices with their start and end apart: 34 -> 34, of which waited for: 16 -> 15; matrix products, arithmetic and copies ran while one was open for 2% -> 2% of each run, Pallas kernels for 8% -> 8%
where the time goes in v5:
time: 88 us; the launch traced here: 87.9 us
  starting transfers between devices  39.3 us (45%)
  waiting for transfers between devices  29.5 us (34%)
  Pallas kernels  16.5 us (19%)
  other arithmetic  1.08 us (1%)
  between operations  1.04 us (1%)
    ppermute x31, starting transfers between devices, swap(): lax.ppermute(value, 'wide', [(i, i ^ flip) for i in range(self.size)])  32.7 us
    ppermute x31, waiting for transfers between devices, swap(): lax.ppermute(value, 'wide', [(i, i ^ flip) for i in range(self.size)])  28.1 us
    ppermute x3, starting transfers between devices, from_pair(): lax.ppermute(value, 'dp', [(i, (i + s) % size) for i in range(size)])  6.64 us
    pallas_call x2, Pallas kernels, pre_parts(): pl.pallas_call(functools.partial(pre_kernel, block), in_specs=[IN_VMEM] *...  5.26 us
    pallas_call x1, Pallas kernels, grad_pre_of(): pl.pallas_call(functools.partial(grad_pre_kernel, len(pres), block), in_s...  3.25 us
    pallas_call x1, Pallas kernels, grad_down_of(): pl.pallas_call(functools.partial(grad_down_kernel, block), in_specs=[IN_V...  2.14 us
    pallas_call x1, Pallas kernels, teacher_parts(): pl.pallas_call(functools.partial(teacher_kernel, len(pres), inner, owners...  1.92 us
  transfers between devices with their start and end apart: 34, of which 15 were waited for; matrix products, arithmetic and copies ran while one was open for 2% of the time, Pallas kernels for 8%

profile of v5, /device:TPU:1, one launch (start us, length us, event | category | flops | bytes accessed | tf_op | source)
XLA Modules:
  0.0 87.9 jit_solution(11521592208889189112)
XLA Ops:
  0.6 0.0 slice-start
  0.6 0.0 slice-start.2
  0.7 1.7 %payload.1 = bf16[16,2176]{1,0:T(8,128)(2,1)} custom-call(bf16[16,2048]{1,0:T(8,128)(2,1)} %layer_hbm.1, s32[8,16]{1,0:T(8,128)} %bitcast.32, f32[8,16]{1,0:T(8,128)} %bitcast.33), custom_call_target="tpu_custom_call" | custom-call | tf_op jit(solution)/shard_map/payload/pallas_call | solution.py:115
  2.4 0.0 slice-start.1
  2.4 0.0 slice-start.3
  2.4 4.2 %collective-permute-start = (bf16[16,2176]{1,0:T(8,128)(2,1)}, bf16[16,2176]{1,0:T(8,128)(2,1)S(1)}, u32[]{:S(2)}, u32[]{:S(2)}) collective-permute-start(bf16[16,2176]{1,0:T(8,128)(2,1)} %payload.1), channel_id=1, source_target_pairs={{0,12},{1,13},{2,14},{3,15},{4,8},{5,9},{6,10},{7,11},{8,4},{9,5},... | collective-permute-start | bytes 208904 | tf_op jit(solution)/shard_map/ppermute | solution.py:55
  6.6 0.4 collective-permute-start.1
  7.0 1.6 %collective-permute-done.in_ref = bf16[16,2176]{1,0:T(8,128)(2,1)S(1)} collective-permute-done((bf16[16,2176]{1,0:T(8,128)(2,1)}, bf16[16,2176]{1,0:T(8,128)(2,1)S(1)}, u32[]{:S(2)}, u32[]{:S(2)}) %collective-permute-start) | collective-permute-done | bytes 69664 | tf_op jit(solution)/shard_map/ppermute | solution.py:55
  8.6 2.2 %collective-permute-start.7 = (bf16[16,2176]{1,0:T(8,128)(2,1)S(1)}, bf16[16,2176]{1,0:T(8,128)(2,1)S(1)}, u32[]{:S(2)}, u32[]{:S(2)}) collective-permute-start(bf16[16,2176]{1,0:T(8,128)(2,1)S(1)} %copy-done.4), channel_id=1, source_target_pairs={{0,3},{1,2},{2,1},{3,0},{4,7},{5,6},{6,5},{7,4},{8,11},{9,10},{10,... | collective-permute-start | bytes 208904 | tf_op jit(solution)/shard_map/ppermute | solution.py:55
  10.8 0.2 collective-permute-start.5
  11.0 0.3 collective-permute-start.3
  11.3 1.4 %collective-permute-done.2 = bf16[16,2176]{1,0:T(8,128)(2,1)S(1)} collective-permute-done((bf16[16,2176]{1,0:T(8,128)(2,1)}, bf16[16,2176]{1,0:T(8,128)(2,1)S(1)}, u32[]{:S(2)}, u32[]{:S(2)}) %collective-permute-start.2) | collective-permute-done | bytes 69664 | tf_op jit(solution)/shard_map/ppermute | solution.py:55
  12.7 2.5 %collective-permute-start.8 = (bf16[48,2176]{1,0:T(8,128)(2,1)S(1)}, bf16[48,2176]{1,0:T(8,128)(2,1)S(1)}, u32[]{:S(2)}, u32[]{:S(2)}) collective-permute-start(bf16[48,2176]{1,0:T(8,128)(2,1)S(1)} %get-tuple-element.75), channel_id=1, source_target_pairs={{0,3},{1,2},{2,1},{3,0},{4,7},{5,6},{6,5},{7,4},{8,11},{9,10},{10,... | collective-permute-start | bytes 626696 | tf_op jit(solution)/shard_map/ppermute | solution.py:55
  15.2 0.2 collective-permute-start.6
  15.5 0.1 collective-permute-start.4
  15.6 9.6 %collective-permute-done.4 = bf16[48,2176]{1,0:T(8,128)(2,1)S(1)} collective-permute-done((bf16[48,2176]{1,0:T(8,128)(2,1)S(1)}, bf16[48,2176]{1,0:T(8,128)(2,1)S(1)}, u32[]{:S(2)}, u32[]{:S(2)}) %collective-permute-start.4) | collective-permute-done | bytes 208928 | tf_op jit(solution)/shard_map/ppermute | solution.py:55
  25.3 0.2 collective-permute-done.6
  25.7 3.4 %teacher_pre.1.refs_0_ = bf16[256,3072]{1,0:T(8,128)(2,1)S(1)} custom-call(bf16[256,2176]{1,0:T(8,128)(2,1)S(1)} %constant_dynamic-update-slice_fusion.3.x_ref.refs_3_.refs_4_, bf16[1536,2048]{1,0:T(8,128)(2,1)S(1)} %bitcast.24, bf16[1536,2048]{1,0:T(8,128)(2,1)S(1)} %bitcast.27), custom_call_target="tpu_custom_call" | custom-call | flops 3221225472 | bytes 14155776 | tf_op jit(solution)/shard_map/teacher_pre/pallas_call | solution.py:155
  29.2 1.5 %collective-permute-start.10 = (bf16[256,3072]{1,0:T(8,128)(2,1)S(1)}, bf16[256,3072]{1,0:T(8,128)(2,1)S(1)}, u32[]{:S(2)}, u32[]{:S(2)}) collective-permute-start(bf16[256,3072]{1,0:T(8,128)(2,1)S(1)} %teacher_pre.1.refs_0_), channel_id=1, source_target_pairs={{0,16},{16,0},{1,17},{17,1},{2,18},{18,2},{3,19},{19,3},{4,20},{20... | collective-permute-start | bytes 4718600 | tf_op jit(solution)/shard_map/ppermute | solution.py:83
  30.6 1.8 %student_pre.1.refs_0_ = f32[256,1536]{1,0:T(8,128)S(1)} custom-call(bf16[256,2176]{1,0:T(8,128)(2,1)S(1)} %constant_dynamic-update-slice_fusion.3.x_ref.refs_3_.refs_4_, bf16[768,2048]{1,0:T(8,128)(2,1)S(1)} %copy-done.2, bf16[768,2048]{1,0:T(8,128)(2,1)S(1)} %copy-done.3), custom_call_target="tpu_custom_call" | custom-call | flops 1610612736 | bytes 7077888 | tf_op jit(solution)/shard_map/student_pre/pallas_call | solution.py:155
  32.5 0.1 collective-permute-start.9
  32.6 1.1 %collective-permute-done.10.refs_1_ = bf16[256,3072]{1,0:T(8,128)(2,1)S(1)} collective-permute-done((bf16[256,3072]{1,0:T(8,128)(2,1)S(1)}, bf16[256,3072]{1,0:T(8,128)(2,1)S(1)}, u32[]{:S(2)}, u32[]{:S(2)}) %collective-permute-start.10) | collective-permute-done | bytes 1572896 | tf_op jit(solution)/shard_map/ppermute | solution.py:83
  33.7 1.9 %teacher_down.1 = (bf16[64,2048]{1,0:T(8,128)(2,1)S(1)}, bf16[64,2048]{1,0:T(8,128)(2,1)S(1)}, bf16[64,2048]{1,0:T(8,128)(2,1)S(1)}, bf16[64,2048]{1,0:T(8,128)(2,1)S(1)}) custom-call(bf16[256,3072]{1,0:T(8,128)(2,1)S(1)} %teacher_pre.1.refs_0_, bf16[256,3072]{1,0:T(8,128)(2,1)S(1)} %collective-permute-done.10.refs_1_, bf16[1536,2048]{1,0:T(8,128)(2,1)S(1)} %bitcast.21, ...), custom_call_target="tpu_custom_call" | custom-call | flops 1610612736 | bytes 10223616 | tf_op jit(solution)/shard_map/teacher_down/pallas_call | solution.py:211
  35.6 0.3 collective-permute-done.9.refs_1_
  35.9 1.0 %student_down.1 = (bf16[256,768]{1,0:T(8,128)(2,1)S(1)}, bf16[16,2048]{1,0:T(8,128)(2,1)S(1)}, bf16[48,2048]{1,0:T(8,128)(2,1)S(1)}, bf16[16,2048]{1,0:T(8,128)(...) custom-call(f32[256,1536]{1,0:T(8,128)S(1)} %student_pre.1.refs_0_, ...), custom_call_target="tpu_custom_call" | custom-call | flops 805306368 | bytes 5111808 | tf_op jit(solution)/shard_map/student_down/pallas_call | solution.py:248
  37.0 0.5 collective-permute-start.11
  37.5 1.0 %collective-permute-start.12 = (bf16[48,2048]{1,0:T(8,128)(2,1)S(1)}, bf16[48,2048]{1,0:T(8,128)(2,1)S(1)}, u32[]{:S(2)}, u32[]{:S(2)}) collective-permute-start(bf16[48,2048]{1,0:T(8,128)(2,1)S(1)} %get-tuple-element.50), channel_id=1, source_target_pairs={{0,2},{1,3},{2,0},{3,1},{4,6},{5,7},{6,4},{7,5},{8,10},{9,11},{10,... | collective-permute-start | bytes 589832 | tf_op jit(solution)/shard_map/ppermute | solution.py:55
  38.5 1.2 %collective-permute-start.13 = (bf16[48,2048]{1,0:T(8,128)(2,1)S(1)}, bf16[48,2048]{1,0:T(8,128)(2,1)S(1)}, u32[]{:S(2)}, u32[]{:S(2)}) collective-permute-start(bf16[48,2048]{1,0:T(8,128)(2,1)S(1)} %get-tuple-element.51), channel_id=1, source_target_pairs={{0,3},{1,2},{2,1},{3,0},{4,7},{5,6},{6,5},{7,4},{8,11},{9,10},{10,... | collective-permute-start | bytes 589832 | tf_op jit(solution)/shard_map/ppermute | solution.py:55
  39.7 3.5 %collective-permute-done.11 = bf16[48,2048]{1,0:T(8,128)(2,1)S(1)} collective-permute-done((bf16[48,2048]{1,0:T(8,128)(2,1)S(1)}, bf16[48,2048]{1,0:T(8,128)(2,1)S(1)}, u32[]{:S(2)}, u32[]{:S(2)}) %collective-permute-start.11) | collective-permute-done | bytes 196640 | tf_op jit(solution)/shard_map/ppermute | solution.py:55
  43.2 0.5 collective-permute-start.17
  43.6 1.0 %collective-permute-start.18 = (bf16[16,2048]{1,0:T(8,128)(2,1)S(1)}, bf16[16,2048]{1,0:T(8,128)(2,1)S(1)}, u32[]{:S(2)}, u32[]{:S(2)}) collective-permute-start(bf16[16,2048]{1,0:T(8,128)(2,1)S(1)} %get-tuple-element.54), channel_id=1, source_target_pairs={{0,2},{1,3},{2,0},{3,1},{4,6},{5,7},{6,4},{7,5},{8,10},{9,11},{10,... | collective-permute-start | bytes 196616 | tf_op jit(solution)/shard_map/ppermute | solution.py:55
  44.6 1.2 %collective-permute-start.19 = (bf16[16,2048]{1,0:T(8,128)(2,1)S(1)}, bf16[16,2048]{1,0:T(8,128)(2,1)S(1)}, u32[]{:S(2)}, u32[]{:S(2)}) collective-permute-start(bf16[16,2048]{1,0:T(8,128)(2,1)S(1)} %get-tuple-element.55), channel_id=1, source_target_pairs={{0,3},{1,2},{2,1},{3,0},{4,7},{5,6},{6,5},{7,4},{8,11},{9,10},{10,... | collective-permute-start | bytes 196616 | tf_op jit(solution)/shard_map/ppermute | solution.py:55
  45.8 1.6 %collective-permute-done.13 = bf16[48,2048]{1,0:T(8,128)(2,1)S(1)} collective-permute-done((bf16[48,2048]{1,0:T(8,128)(2,1)S(1)}, bf16[48,2048]{1,0:T(8,128)(2,1)S(1)}, u32[]{:S(2)}, u32[]{:S(2)}) %collective-permute-start.13) | collective-permute-done | bytes 196640 | tf_op jit(solution)/shard_map/ppermute | solution.py:55
  47.5 0.1 add_convert_fusion.2
  47.6 1.3 %collective-permute-start.14 = (bf16[16,2048]{1,0:T(8,128)(2,1)S(1)}, bf16[16,2048]{1,0:T(8,128)(2,1)S(1)}, u32[]{:S(2)}, u32[]{:S(2)}) collective-permute-start(bf16[16,2048]{1,0:T(8,128)(2,1)S(1)} %get-tuple-element.68), channel_id=1, source_target_pairs={{0,4},{1,5},{2,6},{3,7},{4,0},{5,1},{6,2},{7,3},{8,12},{9,13},{10,... | collective-permute-start | bytes 196616 | tf_op jit(solution)/shard_map/ppermute | solution.py:55
  48.8 2.1 %collective-permute-start.16 = (bf16[16,2048]{1,0:T(8,128)(2,1)S(1)}, bf16[16,2048]{1,0:T(8,128)(2,1)S(1)}, u32[]{:S(2)}, u32[]{:S(2)}) collective-permute-start(bf16[16,2048]{1,0:T(8,128)(2,1)S(1)} %get-tuple-element.69), channel_id=1, source_target_pairs={{0,12},{1,13},{2,14},{3,15},{4,8},{5,9},{6,10},{7,11},{8,4},{9,5},... | collective-permute-start | bytes 196616 | tf_op jit(solution)/shard_map/ppermute | solution.py:55
  51.0 0.2 collective-permute-start.15
  51.2 0.5 collective-permute-start.20
  51.7 1.1 %collective-permute-start.21 = (bf16[64,2048]{1,0:T(8,128)(2,1)S(1)}, bf16[64,2048]{1,0:T(8,128)(2,1)S(1)}, u32[]{:S(2)}, u32[]{:S(2)}) collective-permute-start(bf16[64,2048]{1,0:T(8,128)(2,1)S(1)} %get-tuple-element.57.refs_6_), channel_id=1, source_target_pairs={{0,2},{1,3},{2,0},{3,1},{4,6},{5,7},{6,4},{7,5},{8,10},{9,11},{10,... | collective-permute-start | bytes 786440 | tf_op jit(solution)/shard_map/ppermute | solution.py:55
  52.8 1.1 %collective-permute-done.16 = bf16[16,2048]{1,0:T(8,128)(2,1)S(1)} collective-permute-done((bf16[16,2048]{1,0:T(8,128)(2,1)S(1)}, bf16[16,2048]{1,0:T(8,128)(2,1)S(1)}, u32[]{:S(2)}, u32[]{:S(2)}) %collective-permute-start.16) | collective-permute-done | bytes 65568 | tf_op jit(solution)/shard_map/ppermute | solution.py:55
  53.9 2.9 %collective-permute-done.15 = bf16[16,2048]{1,0:T(8,128)(2,1)S(1)} collective-permute-done((bf16[16,2048]{1,0:T(8,128)(2,1)S(1)}, bf16[16,2048]{1,0:T(8,128)(2,1)S(1)}, u32[]{:S(2)}, u32[]{:S(2)}) %collective-permute-start.15) | collective-permute-done | bytes 65568 | tf_op jit(solution)/shard_map/ppermute | solution.py:55
  56.8 0.1 multiply_convert_fusion
  56.9 0.3 collective-permute-done.21
  57.2 2.4 %collective-permute-start.24 = (bf16[16,2048]{1,0:T(8,128)(2,1)S(1)}, bf16[16,2048]{1,0:T(8,128)(2,1)S(1)}, u32[]{:S(2)}, u32[]{:S(2)}) collective-permute-start(bf16[16,2048]{1,0:T(8,128)(2,1)S(1)} %multiply_convert_fusion), channel_id=1, source_target_pairs={{0,12},{1,13},{2,14},{3,15},{4,8},{5,9},{6,10},{7,11},{8,4},{9,5},... | collective-permute-start | bytes 196616 | tf_op jit(solution)/shard_map/ppermute | solution.py:55
  59.6 0.1 collective-permute-start.23
  59.6 1.1 %collective-permute-start.22 = (bf16[16,2048]{1,0:T(8,128)(2,1)S(1)}, bf16[16,2048]{1,0:T(8,128)(2,1)S(1)}, u32[]{:S(2)}, u32[]{:S(2)}) collective-permute-start(bf16[16,2048]{1,0:T(8,128)(2,1)S(1)} %multiply_convert_fusion), channel_id=1, source_target_pairs={{0,4},{1,5},{2,6},{3,7},{4,0},{5,1},{6,2},{7,3},{8,12},{9,13},{10,... | collective-permute-start | bytes 196616 | tf_op jit(solution)/shard_map/ppermute | solution.py:55
  60.7 0.1 add_convert_fusion
  61.0 1.2 %collective-permute-start.27 = (bf16[48,2048]{1,0:T(8,128)(2,1)S(1)}, bf16[48,2048]{1,0:T(8,128)(2,1)S(1)}, u32[]{:S(2)}, u32[]{:S(2)}) collective-permute-start(bf16[48,2048]{1,0:T(8,128)(2,1)S(1)} %get-tuple-element.87), channel_id=1, source_target_pairs={{0,2},{1,3},{2,0},{3,1},{4,6},{5,7},{6,4},{7,5},{8,10},{9,11},{10,... | collective-permute-start | bytes 589832 | tf_op jit(solution)/shard_map/ppermute | solution.py:55
  62.1 0.5 collective-permute-start.25
  62.6 0.2 collective-permute-done.22
  62.8 1.2 %collective-permute-done.23 = bf16[16,2048]{1,0:T(8,128)(2,1)S(1)} collective-permute-done((bf16[16,2048]{1,0:T(8,128)(2,1)S(1)}, bf16[16,2048]{1,0:T(8,128)(2,1)S(1)}, u32[]{:S(2)}, u32[]{:S(2)}) %collective-permute-start.23) | collective-permute-done | bytes 65568 | tf_op jit(solution)/shard_map/ppermute | solution.py:55
  64.1 1.2 %collective-permute-start.28 = (bf16[48,2048]{1,0:T(8,128)(2,1)S(1)}, bf16[48,2048]{1,0:T(8,128)(2,1)S(1)}, u32[]{:S(2)}, u32[]{:S(2)}) collective-permute-start(bf16[48,2048]{1,0:T(8,128)(2,1)S(1)} %get-tuple-element.81), channel_id=1, source_target_pairs={{0,2},{1,3},{2,0},{3,1},{4,6},{5,7},{6,4},{7,5},{8,10},{9,11},{10,... | collective-permute-start | bytes 589832 | tf_op jit(solution)/shard_map/ppermute | solution.py:55
  65.3 0.5 collective-permute-start.26
  65.8 1.1 %collective-permute-start.29 = (bf16[64,2048]{1,0:T(8,128)(2,1)S(1)}, bf16[64,2048]{1,0:T(8,128)(2,1)S(1)}, u32[]{:S(2)}, u32[]{:S(2)}) collective-permute-start(bf16[64,2048]{1,0:T(8,128)(2,1)S(1)} %pad_maximum_fusion), channel_id=1, source_target_pairs={{0,3},{1,2},{2,1},{3,0},{4,7},{5,6},{6,5},{7,4},{8,11},{9,10},{10,... | collective-permute-start | bytes 786440 | tf_op jit(solution)/shard_map/ppermute | solution.py:55
  67.0 0.1 collective-permute-start.30
  67.1 2.1 %collective-permute-start.31 = (bf16[16,2048]{1,0:T(8,128)(2,1)S(1)}, bf16[16,2048]{1,0:T(8,128)(2,1)S(1)}, u32[]{:S(2)}, u32[]{:S(2)}) collective-permute-start(bf16[16,2048]{1,0:T(8,128)(2,1)S(1)} %get-tuple-element.73), channel_id=1, source_target_pairs={{0,8},{1,9},{2,10},{3,11},{4,12},{5,13},{6,14},{7,15},{8,0},{9,1},... | collective-permute-start | bytes 196616 | tf_op jit(solution)/shard_map/ppermute | solution.py:55
  69.3 0.8 collective-permute-done.26
  70.1 1.8 %collective-permute-start.32 = (bf16[16,2048]{1,0:T(8,128)(2,1)S(1)}, bf16[16,2048]{1,0:T(8,128)(2,1)S(1)}, u32[]{:S(2)}, u32[]{:S(2)}) collective-permute-start(bf16[16,2048]{1,0:T(8,128)(2,1)S(1)} %get-tuple-element.74), channel_id=1, source_target_pairs={{0,12},{1,13},{2,14},{3,15},{4,8},{5,9},{6,10},{7,11},{8,4},{9,5},... | collective-permute-start | bytes 196616 | tf_op jit(solution)/shard_map/ppermute | solution.py:55
  72.0 3.4 %collective-permute-done.29 = bf16[64,2048]{1,0:T(8,128)(2,1)S(1)} collective-permute-done((bf16[64,2048]{1,0:T(8,128)(2,1)S(1)}, bf16[64,2048]{1,0:T(8,128)(2,1)S(1)}, u32[]{:S(2)}, u32[]{:S(2)}) %collective-permute-start.29) | collective-permute-done | bytes 262176 | tf_op jit(solution)/shard_map/ppermute | solution.py:55
  75.4 1.2 %hidden_grad.1.refs_2_ = bf16[256,768]{1,0:T(8,128)(2,1)S(1)} custom-call(bf16[256,2048]{1,0:T(8,128)(2,1)S(1)} %constant_dynamic-update-slice_fusion.16.delta_ref, bf16[768,2048]{1,0:T(8,128)(2,1)S(1)} %copy-done), custom_call_target="tpu_custom_call" | custom-call | flops 805306368 | bytes 4194304 | tf_op jit(solution)/shard_map/hidden_grad/pallas_call | solution.py:271
  76.7 5.1 %collective-permute-start.33 = (bf16[256,768]{1,0:T(8,128)(2,1)S(1)}, bf16[256,768]{1,0:T(8,128)(2,1)S(1)}, u32[]{:S(2)}, u32[]{:S(2)}) collective-permute-start(bf16[256,768]{1,0:T(8,128)(2,1)S(1)} %hidden_grad.1.refs_2_), channel_id=1, source_target_pairs={{0,16},{16,0},{1,17},{17,1},{2,18},{18,2},{3,19},{19,3},{4,20},{20... | collective-permute-start | bytes 1179656 | tf_op jit(solution)/shard_map/ppermute | solution.py:83
  81.8 2.1 %grad_down.1 = bf16[768,2048]{1,0:T(8,128)(2,1)} custom-call(bf16[256,768]{1,0:T(8,128)(2,1)S(1)} %get-tuple-element.67.hidden_ref, bf16[256,2048]{1,0:T(8,128)(2,1)S(1)} %constant_dynamic-update-slice_fusion.16.delta_ref), custom_call_target="tpu_custom_call" | custom-call | flops 805306368 | bytes 4194304 | tf_op jit(solution)/shard_map/grad_down/pallas_call | solution.py:296
  83.9 0.7 add_convert_fusion.3
  84.6 3.3 %grad_gate_up.1 = (bf16[768,2048]{1,0:T(8,128)(2,1)}, bf16[768,2048]{1,0:T(8,128)(2,1)}) custom-call(f32[256,1536]{1,0:T(8,128)S(1)} %student_pre.1.refs_0_, f32[256,1536]{1,0:T(8,128)S(1)} %collective-permute-done.9.refs_1_, bf16[256,768]{1,0:T(8,128)(2,1)S(1)} %hidden_grad.1.refs_2_, bf16[256,768]{1,0:T(8,128)(2,1)S(1)} %collective-permute-done.33.refs_3_, ...), custom_call_target="tpu_custom_call" | custom-call | flops 1610612736 | bytes 7340032 | tf_op jit(solution)/shard_map/grad_gate_up/pallas_call | solution.py:332
  (65 shorter events, 0.5 us)
Async XLA Ops:
  0.6 25.0 %slice-start = ((s8[6291456]{0:T(1024)(128)(4,1)}), s8[2097152]{0:T(1024)(128)(4,1)S(1)}, s32[]{:S(2)}) async-start(s8[6291456]{0:T(1024)(128)(4,1)} %bitcast.22), calls=%async_computation | async-start | bytes 4194304
  0.6 25.0 %slice-start.2 = ((s8[6291456]{0:T(1024)(128)(4,1)}), s8[4194304]{0:T(1024)(128)(4,1)S(1)}, s32[]{:S(2)}) async-start(s8[6291456]{0:T(1024)(128)(4,1)} %bitcast.25), calls=%async_computation.2 | async-start | bytes 8388608
  2.3 6.2 %copy-start.4 = (bf16[16,2176]{1,0:T(8,128)(2,1)S(1)}, bf16[16,2176]{1,0:T(8,128)(2,1)}, u32[]{:S(2)}) copy-start(bf16[16,2176]{1,0:T(8,128)(2,1)} %payload.1) | copy-start | bytes 208900
  2.4 23.3 %slice-start.1 = ((s8[6291456]{0:T(1024)(128)(4,1)}), s8[4194304]{0:T(1024)(128)(4,1)S(1)}, s32[]{:S(2)}) async-start(s8[6291456]{0:T(1024)(128)(4,1)} %bitcast.22), calls=%async_computation.1 | async-start | bytes 8388608
  2.4 23.3 %slice-start.3 = ((s8[6291456]{0:T(1024)(128)(4,1)}), s8[2097152]{0:T(1024)(128)(4,1)S(1)}, s32[]{:S(2)}) async-start(s8[6291456]{0:T(1024)(128)(4,1)} %bitcast.25), calls=%async_computation.3 | async-start | bytes 4194304
  2.4 6.2 %collective-permute-start = (bf16[16,2176]{1,0:T(8,128)(2,1)}, bf16[16,2176]{1,0:T(8,128)(2,1)S(1)}, u32[]{:S(2)}, u32[]{:S(2)}) collective-permute-start(bf16[16,2176]{1,0:T(8,128)(2,1)} %payload.1), channel_id=1, source_target_pairs={{0,12},{1,13},{2,14},{3,15},{4,8},{5,9},{6,10},{7,11},{8,4},{9,5},... | collective-permute-start | bytes 208904 | tf_op jit(solution)/shard_map/ppermute | solution.py:55
  6.6 6.1 %collective-permute-start.2 = (bf16[16,2176]{1,0:T(8,128)(2,1)}, bf16[16,2176]{1,0:T(8,128)(2,1)S(1)}, u32[]{:S(2)}, u32[]{:S(2)}) collective-permute-start(bf16[16,2176]{1,0:T(8,128)(2,1)} %payload.1), channel_id=1, source_target_pairs={{0,8},{1,9},{2,10},{3,11},{4,12},{5,13},{6,14},{7,15},{8,0},{9,1},... | collective-permute-start | bytes 208904 | tf_op jit(solution)/shard_map/ppermute | solution.py:55
  6.6 4.7 %collective-permute-start.1 = (bf16[16,2176]{1,0:T(8,128)(2,1)}, bf16[16,2176]{1,0:T(8,128)(2,1)S(1)}, u32[]{:S(2)}, u32[]{:S(2)}) collective-permute-start(bf16[16,2176]{1,0:T(8,128)(2,1)} %payload.1), channel_id=1, source_target_pairs={{0,4},{1,5},{2,6},{3,7},{4,0},{5,1},{6,2},{7,3},{8,12},{9,13},{10,... | collective-permute-start | bytes 208904 | tf_op jit(solution)/shard_map/ppermute | solution.py:55
  8.6 17.0 %collective-permute-start.7 = (bf16[16,2176]{1,0:T(8,128)(2,1)S(1)}, bf16[16,2176]{1,0:T(8,128)(2,1)S(1)}, u32[]{:S(2)}, u32[]{:S(2)}) collective-permute-start(bf16[16,2176]{1,0:T(8,128)(2,1)S(1)} %copy-done.4), channel_id=1, source_target_pairs={{0,3},{1,2},{2,1},{3,0},{4,7},{5,6},{6,5},{7,4},{8,11},{9,10},{10,... | collective-permute-start | bytes 208904 | tf_op jit(solution)/shard_map/ppermute | solution.py:55
  10.8 14.5 %collective-permute-start.5 = (bf16[16,2176]{1,0:T(8,128)(2,1)S(1)}, bf16[16,2176]{1,0:T(8,128)(2,1)S(1)}, u32[]{:S(2)}, u32[]{:S(2)}) collective-permute-start(bf16[16,2176]{1,0:T(8,128)(2,1)S(1)} %copy-done.4), channel_id=1, source_target_pairs={{0,2},{1,3},{2,0},{3,1},{4,6},{5,7},{6,4},{7,5},{8,10},{9,11},{10,... | collective-permute-start | bytes 208904 | tf_op jit(solution)/shard_map/ppermute | solution.py:55
  11.0 4.4 %collective-permute-start.3 = (bf16[16,2176]{1,0:T(8,128)(2,1)S(1)}, bf16[16,2176]{1,0:T(8,128)(2,1)S(1)}, u32[]{:S(2)}, u32[]{:S(2)}) collective-permute-start(bf16[16,2176]{1,0:T(8,128)(2,1)S(1)} %copy-done.4), channel_id=1, source_target_pairs={{0,1},{1,0},{2,3},{3,2},{4,5},{5,4},{6,7},{7,6},{8,9},{9,8},{10,11... | collective-permute-start | bytes 208904 | tf_op jit(solution)/shard_map/ppermute | solution.py:55
  12.7 12.9 %collective-permute-start.8 = (bf16[48,2176]{1,0:T(8,128)(2,1)S(1)}, bf16[48,2176]{1,0:T(8,128)(2,1)S(1)}, u32[]{:S(2)}, u32[]{:S(2)}) collective-permute-start(bf16[48,2176]{1,0:T(8,128)(2,1)S(1)} %get-tuple-element.75), channel_id=1, source_target_pairs={{0,3},{1,2},{2,1},{3,0},{4,7},{5,6},{6,5},{7,4},{8,11},{9,10},{10,... | collective-permute-start | bytes 626696 | tf_op jit(solution)/shard_map/ppermute | solution.py:55
  15.2 10.3 %collective-permute-start.6 = (bf16[48,2176]{1,0:T(8,128)(2,1)S(1)}, bf16[48,2176]{1,0:T(8,128)(2,1)S(1)}, u32[]{:S(2)}, u32[]{:S(2)}) collective-permute-start(bf16[48,2176]{1,0:T(8,128)(2,1)S(1)} %get-tuple-element.75), channel_id=1, source_target_pairs={{0,2},{1,3},{2,0},{3,1},{4,6},{5,7},{6,4},{7,5},{8,10},{9,11},{10,... | collective-permute-start | bytes 626696 | tf_op jit(solution)/shard_map/ppermute | solution.py:55
  15.5 9.8 %collective-permute-start.4 = (bf16[48,2176]{1,0:T(8,128)(2,1)S(1)}, bf16[48,2176]{1,0:T(8,128)(2,1)S(1)}, u32[]{:S(2)}, u32[]{:S(2)}) collective-permute-start(bf16[48,2176]{1,0:T(8,128)(2,1)S(1)} %get-tuple-element.75), channel_id=1, source_target_pairs={{0,1},{1,0},{2,3},{3,2},{4,5},{5,4},{6,7},{7,6},{8,9},{9,8},{10,11... | collective-permute-start | bytes 626696 | tf_op jit(solution)/shard_map/ppermute | solution.py:55
  25.7 5.0 %copy-start.2 = (bf16[768,2048]{1,0:T(8,128)(2,1)S(1)}, bf16[768,2048]{1,0:T(8,128)(2,1)}, u32[]{:S(2)}) copy-start(bf16[768,2048]{1,0:T(8,128)(2,1)} %gate_ref.1) | copy-start | bytes 9437188
  25.7 4.9 %copy-start.3 = (bf16[768,2048]{1,0:T(8,128)(2,1)S(1)}, bf16[768,2048]{1,0:T(8,128)(2,1)}, u32[]{:S(2)}) copy-start(bf16[768,2048]{1,0:T(8,128)(2,1)} %up_ref.1) | copy-start | bytes 9437188
  29.2 4.5 %collective-permute-start.10 = (bf16[256,3072]{1,0:T(8,128)(2,1)S(1)}, bf16[256,3072]{1,0:T(8,128)(2,1)S(1)}, u32[]{:S(2)}, u32[]{:S(2)}) collective-permute-start(bf16[256,3072]{1,0:T(8,128)(2,1)S(1)} %teacher_pre.1.refs_0_), channel_id=1, source_target_pairs={{0,16},{16,0},{1,17},{17,1},{2,18},{18,2},{3,19},{19,3},{4,20},{20... | collective-permute-start | bytes 4718600 | tf_op jit(solution)/shard_map/ppermute | solution.py:83
  30.6 3.0 %copy-start.1 = (bf16[1,1536,2048]{2,1,0:T(8,128)(2,1)S(1)}, bf16[1,1536,2048]{2,1,0:T(8,128)(2,1)}, u32[]{:S(2)}) copy-start(bf16[1,1536,2048]{2,1,0:T(8,128)(2,1)} %param.14) | copy-start | bytes 18874372
  32.5 3.5 %collective-permute-start.9 = (f32[256,1536]{1,0:T(8,128)S(1)}, f32[256,1536]{1,0:T(8,128)S(1)}, u32[]{:S(2)}, u32[]{:S(2)}) collective-permute-start(f32[256,1536]{1,0:T(8,128)S(1)} %student_pre.1.refs_0_), channel_id=1, source_target_pairs={{0,16},{16,0},{1,17},{17,1},{2,18},{18,2},{3,19},{19,3},{4,20},{20... | collective-permute-start | bytes 4718600 | tf_op jit(solution)/shard_map/ppermute | solution.py:83
  33.7 2.3 %copy-start = (bf16[768,2048]{1,0:T(8,128)(2,1)S(1)}, bf16[768,2048]{1,0:T(8,128)(2,1)}, u32[]{:S(2)}) copy-start(bf16[768,2048]{1,0:T(8,128)(2,1)} %down_ref.1) | copy-start | bytes 9437188
  37.0 6.2 %collective-permute-start.11 = (bf16[48,2048]{1,0:T(8,128)(2,1)S(1)}, bf16[48,2048]{1,0:T(8,128)(2,1)S(1)}, u32[]{:S(2)}, u32[]{:S(2)}) collective-permute-start(bf16[48,2048]{1,0:T(8,128)(2,1)S(1)} %get-tuple-element.42), channel_id=1, source_target_pairs={{0,1},{1,0},{2,3},{3,2},{4,5},{5,4},{6,7},{7,6},{8,9},{9,8},{10,11... | collective-permute-start | bytes 589832 | tf_op jit(solution)/shard_map/ppermute | solution.py:55
  37.5 8.3 %collective-permute-start.12 = (bf16[48,2048]{1,0:T(8,128)(2,1)S(1)}, bf16[48,2048]{1,0:T(8,128)(2,1)S(1)}, u32[]{:S(2)}, u32[]{:S(2)}) collective-permute-start(bf16[48,2048]{1,0:T(8,128)(2,1)S(1)} %get-tuple-element.50), channel_id=1, source_target_pairs={{0,2},{1,3},{2,0},{3,1},{4,6},{5,7},{6,4},{7,5},{8,10},{9,11},{10,... | collective-permute-start | bytes 589832 | tf_op jit(solution)/shard_map/ppermute | solution.py:55
  38.5 9.0 %collective-permute-start.13 = (bf16[48,2048]{1,0:T(8,128)(2,1)S(1)}, bf16[48,2048]{1,0:T(8,128)(2,1)S(1)}, u32[]{:S(2)}, u32[]{:S(2)}) collective-permute-start(bf16[48,2048]{1,0:T(8,128)(2,1)S(1)} %get-tuple-element.51), channel_id=1, source_target_pairs={{0,3},{1,2},{2,1},{3,0},{4,7},{5,6},{6,5},{7,4},{8,11},{9,10},{10,... | collective-permute-start | bytes 589832 | tf_op jit(solution)/shard_map/ppermute | solution.py:55
  43.2 7.8 %collective-permute-start.17 = (bf16[16,2048]{1,0:T(8,128)(2,1)S(1)}, bf16[16,2048]{1,0:T(8,128)(2,1)S(1)}, u32[]{:S(2)}, u32[]{:S(2)}) collective-permute-start(bf16[16,2048]{1,0:T(8,128)(2,1)S(1)} %get-tuple-element.53), channel_id=1, source_target_pairs={{0,1},{1,0},{2,3},{3,2},{4,5},{5,4},{6,7},{7,6},{8,9},{9,8},{10,11... | collective-permute-start | bytes 196616 | tf_op jit(solution)/shard_map/ppermute | solution.py:55
  43.6 7.6 %collective-permute-start.18 = (bf16[16,2048]{1,0:T(8,128)(2,1)S(1)}, bf16[16,2048]{1,0:T(8,128)(2,1)S(1)}, u32[]{:S(2)}, u32[]{:S(2)}) collective-permute-start(bf16[16,2048]{1,0:T(8,128)(2,1)S(1)} %get-tuple-element.54), channel_id=1, source_target_pairs={{0,2},{1,3},{2,0},{3,1},{4,6},{5,7},{6,4},{7,5},{8,10},{9,11},{10,... | collective-permute-start | bytes 196616 | tf_op jit(solution)/shard_map/ppermute | solution.py:55
  44.6 7.1 %collective-permute-start.19 = (bf16[16,2048]{1,0:T(8,128)(2,1)S(1)}, bf16[16,2048]{1,0:T(8,128)(2,1)S(1)}, u32[]{:S(2)}, u32[]{:S(2)}) collective-permute-start(bf16[16,2048]{1,0:T(8,128)(2,1)S(1)} %get-tuple-element.55), channel_id=1, source_target_pairs={{0,3},{1,2},{2,1},{3,0},{4,7},{5,6},{6,5},{7,4},{8,11},{9,10},{10,... | collective-permute-start | bytes 196616 | tf_op jit(solution)/shard_map/ppermute | solution.py:55
  47.6 5.2 %collective-permute-start.14 = (bf16[16,2048]{1,0:T(8,128)(2,1)S(1)}, bf16[16,2048]{1,0:T(8,128)(2,1)S(1)}, u32[]{:S(2)}, u32[]{:S(2)}) collective-permute-start(bf16[16,2048]{1,0:T(8,128)(2,1)S(1)} %get-tuple-element.68), channel_id=1, source_target_pairs={{0,4},{1,5},{2,6},{3,7},{4,0},{5,1},{6,2},{7,3},{8,12},{9,13},{10,... | collective-permute-start | bytes 196616 | tf_op jit(solution)/shard_map/ppermute | solution.py:55
  48.8 5.0 %collective-permute-start.16 = (bf16[16,2048]{1,0:T(8,128)(2,1)S(1)}, bf16[16,2048]{1,0:T(8,128)(2,1)S(1)}, u32[]{:S(2)}, u32[]{:S(2)}) collective-permute-start(bf16[16,2048]{1,0:T(8,128)(2,1)S(1)} %get-tuple-element.69), channel_id=1, source_target_pairs={{0,12},{1,13},{2,14},{3,15},{4,8},{5,9},{6,10},{7,11},{8,4},{9,5},... | collective-permute-start | bytes 196616 | tf_op jit(solution)/shard_map/ppermute | solution.py:55
  51.0 5.9 %collective-permute-start.15 = (bf16[16,2048]{1,0:T(8,128)(2,1)S(1)}, bf16[16,2048]{1,0:T(8,128)(2,1)S(1)}, u32[]{:S(2)}, u32[]{:S(2)}) collective-permute-start(bf16[16,2048]{1,0:T(8,128)(2,1)S(1)} %get-tuple-element.70), channel_id=1, source_target_pairs={{0,8},{1,9},{2,10},{3,11},{4,12},{5,13},{6,14},{7,15},{8,0},{9,1},... | collective-permute-start | bytes 196616 | tf_op jit(solution)/shard_map/ppermute | solution.py:55
  51.2 5.7 %collective-permute-start.20 = (bf16[64,2048]{1,0:T(8,128)(2,1)S(1)}, bf16[64,2048]{1,0:T(8,128)(2,1)S(1)}, u32[]{:S(2)}, u32[]{:S(2)}) collective-permute-start(bf16[64,2048]{1,0:T(8,128)(2,1)S(1)} %get-tuple-element.56.refs_4_), channel_id=1, source_target_pairs={{0,1},{1,0},{2,3},{3,2},{4,5},{5,4},{6,7},{7,6},{8,9},{9,8},{10,11... | collective-permute-start | bytes 786440 | tf_op jit(solution)/shard_map/ppermute | solution.py:55
  51.7 5.5 %collective-permute-start.21 = (bf16[64,2048]{1,0:T(8,128)(2,1)S(1)}, bf16[64,2048]{1,0:T(8,128)(2,1)S(1)}, u32[]{:S(2)}, u32[]{:S(2)}) collective-permute-start(bf16[64,2048]{1,0:T(8,128)(2,1)S(1)} %get-tuple-element.57.refs_6_), channel_id=1, source_target_pairs={{0,2},{1,3},{2,0},{3,1},{4,6},{5,7},{6,4},{7,5},{8,10},{9,11},{10,... | collective-permute-start | bytes 786440 | tf_op jit(solution)/shard_map/ppermute | solution.py:55
  57.2 6.9 %collective-permute-start.24 = (bf16[16,2048]{1,0:T(8,128)(2,1)S(1)}, bf16[16,2048]{1,0:T(8,128)(2,1)S(1)}, u32[]{:S(2)}, u32[]{:S(2)}) collective-permute-start(bf16[16,2048]{1,0:T(8,128)(2,1)S(1)} %multiply_convert_fusion), channel_id=1, source_target_pairs={{0,12},{1,13},{2,14},{3,15},{4,8},{5,9},{6,10},{7,11},{8,4},{9,5},... | collective-permute-start | bytes 196616 | tf_op jit(solution)/shard_map/ppermute | solution.py:55
  59.6 4.5 %collective-permute-start.23 = (bf16[16,2048]{1,0:T(8,128)(2,1)S(1)}, bf16[16,2048]{1,0:T(8,128)(2,1)S(1)}, u32[]{:S(2)}, u32[]{:S(2)}) collective-permute-start(bf16[16,2048]{1,0:T(8,128)(2,1)S(1)} %multiply_convert_fusion), channel_id=1, source_target_pairs={{0,8},{1,9},{2,10},{3,11},{4,12},{5,13},{6,14},{7,15},{8,0},{9,1},... | collective-permute-start | bytes 196616 | tf_op jit(solution)/shard_map/ppermute | solution.py:55
  59.6 3.2 %collective-permute-start.22 = (bf16[16,2048]{1,0:T(8,128)(2,1)S(1)}, bf16[16,2048]{1,0:T(8,128)(2,1)S(1)}, u32[]{:S(2)}, u32[]{:S(2)}) collective-permute-start(bf16[16,2048]{1,0:T(8,128)(2,1)S(1)} %multiply_convert_fusion), channel_id=1, source_target_pairs={{0,4},{1,5},{2,6},{3,7},{4,0},{5,1},{6,2},{7,3},{8,12},{9,13},{10,... | collective-permute-start | bytes 196616 | tf_op jit(solution)/shard_map/ppermute | solution.py:55
  61.0 6.0 %collective-permute-start.27 = (bf16[48,2048]{1,0:T(8,128)(2,1)S(1)}, bf16[48,2048]{1,0:T(8,128)(2,1)S(1)}, u32[]{:S(2)}, u32[]{:S(2)}) collective-permute-start(bf16[48,2048]{1,0:T(8,128)(2,1)S(1)} %get-tuple-element.87), channel_id=1, source_target_pairs={{0,2},{1,3},{2,0},{3,1},{4,6},{5,7},{6,4},{7,5},{8,10},{9,11},{10,... | collective-permute-start | bytes 589832 | tf_op jit(solution)/shard_map/ppermute | solution.py:55
  62.1 5.0 %collective-permute-start.25 = (bf16[48,2048]{1,0:T(8,128)(2,1)S(1)}, bf16[48,2048]{1,0:T(8,128)(2,1)S(1)}, u32[]{:S(2)}, u32[]{:S(2)}) collective-permute-start(bf16[48,2048]{1,0:T(8,128)(2,1)S(1)} %get-tuple-element.88), channel_id=1, source_target_pairs={{0,1},{1,0},{2,3},{3,2},{4,5},{5,4},{6,7},{7,6},{8,9},{9,8},{10,11... | collective-permute-start | bytes 589832 | tf_op jit(solution)/shard_map/ppermute | solution.py:55
  64.1 7.8 %collective-permute-start.28 = (bf16[48,2048]{1,0:T(8,128)(2,1)S(1)}, bf16[48,2048]{1,0:T(8,128)(2,1)S(1)}, u32[]{:S(2)}, u32[]{:S(2)}) collective-permute-start(bf16[48,2048]{1,0:T(8,128)(2,1)S(1)} %get-tuple-element.81), channel_id=1, source_target_pairs={{0,2},{1,3},{2,0},{3,1},{4,6},{5,7},{6,4},{7,5},{8,10},{9,11},{10,... | collective-permute-start | bytes 589832 | tf_op jit(solution)/shard_map/ppermute | solution.py:55
  65.3 4.8 %collective-permute-start.26 = (bf16[48,2048]{1,0:T(8,128)(2,1)S(1)}, bf16[48,2048]{1,0:T(8,128)(2,1)S(1)}, u32[]{:S(2)}, u32[]{:S(2)}) collective-permute-start(bf16[48,2048]{1,0:T(8,128)(2,1)S(1)} %get-tuple-element.81), channel_id=1, source_target_pairs={{0,1},{1,0},{2,3},{3,2},{4,5},{5,4},{6,7},{7,6},{8,9},{9,8},{10,11... | collective-permute-start | bytes 589832 | tf_op jit(solution)/shard_map/ppermute | solution.py:55
  65.8 9.6 %collective-permute-start.29 = (bf16[64,2048]{1,0:T(8,128)(2,1)S(1)}, bf16[64,2048]{1,0:T(8,128)(2,1)S(1)}, u32[]{:S(2)}, u32[]{:S(2)}) collective-permute-start(bf16[64,2048]{1,0:T(8,128)(2,1)S(1)} %pad_maximum_fusion), channel_id=1, source_target_pairs={{0,3},{1,2},{2,1},{3,0},{4,7},{5,6},{6,5},{7,4},{8,11},{9,10},{10,... | collective-permute-start | bytes 786440 | tf_op jit(solution)/shard_map/ppermute | solution.py:55
  67.0 16.9 %collective-permute-start.30 = (bf16[16,2048]{1,0:T(8,128)(2,1)S(1)}, bf16[16,2048]{1,0:T(8,128)(2,1)S(1)}, u32[]{:S(2)}, u32[]{:S(2)}) collective-permute-start(bf16[16,2048]{1,0:T(8,128)(2,1)S(1)} %get-tuple-element.72), channel_id=1, source_target_pairs={{0,4},{1,5},{2,6},{3,7},{4,0},{5,1},{6,2},{7,3},{8,12},{9,13},{10,... | collective-permute-start | bytes 196616 | tf_op jit(solution)/shard_map/ppermute | solution.py:55
  67.1 16.8 %collective-permute-start.31 = (bf16[16,2048]{1,0:T(8,128)(2,1)S(1)}, bf16[16,2048]{1,0:T(8,128)(2,1)S(1)}, u32[]{:S(2)}, u32[]{:S(2)}) collective-permute-start(bf16[16,2048]{1,0:T(8,128)(2,1)S(1)} %get-tuple-element.73), channel_id=1, source_target_pairs={{0,8},{1,9},{2,10},{3,11},{4,12},{5,13},{6,14},{7,15},{8,0},{9,1},... | collective-permute-start | bytes 196616 | tf_op jit(solution)/shard_map/ppermute | solution.py:55
  70.1 13.8 %collective-permute-start.32 = (bf16[16,2048]{1,0:T(8,128)(2,1)S(1)}, bf16[16,2048]{1,0:T(8,128)(2,1)S(1)}, u32[]{:S(2)}, u32[]{:S(2)}) collective-permute-start(bf16[16,2048]{1,0:T(8,128)(2,1)S(1)} %get-tuple-element.74), channel_id=1, source_target_pairs={{0,12},{1,13},{2,14},{3,15},{4,8},{5,9},{6,10},{7,11},{8,4},{9,5},... | collective-permute-start | bytes 196616 | tf_op jit(solution)/shard_map/ppermute | solution.py:55
  76.7 7.9 %collective-permute-start.33 = (bf16[256,768]{1,0:T(8,128)(2,1)S(1)}, bf16[256,768]{1,0:T(8,128)(2,1)S(1)}, u32[]{:S(2)}, u32[]{:S(2)}) collective-permute-start(bf16[256,768]{1,0:T(8,128)(2,1)S(1)} %hidden_grad.1.refs_2_), channel_id=1, source_target_pairs={{0,16},{16,0},{1,17},{17,1},{2,18},{18,2},{3,19},{19,3},{4,20},{20... | collective-permute-start | bytes 1179656 | tf_op jit(solution)/shard_map/ppermute | solution.py:83
